TPU v7x, 256 devices: a whole 4x4x8 slice. The times are simulated.
256 devices in a mesh: rep: 32 (over z_lo, x, core), fsdp: 8 (over z_hi, y).
Axes of the slice: x: 4, y: 4, z: 8 (z_hi: 2, z_lo: 4; z = z_hi * 4 + z_lo), core: 2. Of those that a mesh axis runs over, the one named last changes fastest.
Arguments:
- local_params: float32 [32, 256, 8192], P('rep', 'fsdp'), may hold values from -6 to 6
- global_params: float32 [256, 8192], P('fsdp'), may hold values from -6 to 6
- momentum: float32 [256, 8192], P('fsdp', 'rep'), may hold values from -3 to 3
- tokens: bfloat16 [16384, 8192], P('rep', 'fsdp'), may hold values from -0.29882812 to 0.29882812
- kv_weight: bfloat16 [32, 8192, 2048], P('rep', 'fsdp'), may hold values from -0.5 to 0.5
- kv_cotangent: bfloat16 [16384, 2048], P(('rep', 'fsdp')), may hold values from -1.5 to 1.5
Outputs:
- new_global: float32 [256, 8192], P('fsdp', 'rep')
- new_momentum: float32 [256, 8192], P('fsdp', 'rep')
- mixed_local: float32 [32, 256, 8192], P('rep', 'fsdp')
- kv_out: float32 [16384, 2048], P(('rep', 'fsdp'))
- grad_weight: bfloat16 [32, 8192, 2048], P('rep', 'fsdp')
- grad_tokens: float32 [16384, 8192], P('rep', 'fsdp')
All inputs are finite; a program needn't handle non-finite values. Where the computation divides by a largest or mean magnitude, that divisor is 1e-20 or more.
Results may differ from a plain program's by a relative error of at most 0.014.
Values may be sent and summed in bfloat16 or wider, within the bound.
No kernel may reach another device: no remote copies, remote signals or barrier semaphores. Data moves between devices by JAX's collectives and lax.ppermute only.
A program may use at most 64 MiB of HBM per device.

v0:
```python
import jax
import jax.numpy as jnp
from jax import lax
from jax.sharding import PartitionSpec as P

BLOCK = 64


epsilon = 1e-06
momentum_rate = 0.9
outer_rate = 0.7
mix_rate = 0.5


def shards(local_params, global_params, momentum, tokens, kv_weight, kv_cotangent):
    replica_count = lax.axis_size("rep")
    row_count, full_width = global_params.shape
    own_width = full_width // replica_count
    pseudo = global_params[None] - local_params
    blocked = pseudo.reshape(1, row_count, full_width // BLOCK, BLOCK)
    scales = (jnp.max(jnp.abs(blocked), axis=-1) + epsilon).astype(jnp.bfloat16)
    quantized = (blocked / scales[..., None].astype(jnp.float32)).astype(jnp.bfloat16)
    restored = quantized.astype(jnp.float32) * scales[..., None].astype(jnp.float32)
    delta_sum = lax.psum_scatter(
        restored.reshape(row_count, full_width), "rep", scatter_dimension=1, tiled=True
    )
    delta = delta_sum / replica_count
    own_global = lax.dynamic_slice_in_dim(
        global_params, lax.axis_index("rep") * own_width, own_width, 1
    )
    new_momentum = momentum_rate * momentum + delta
    new_global = own_global - outer_rate * (delta + momentum_rate * new_momentum)
    local_rows = local_params[0]
    mixed_local = (
        mix_rate * local_rows
        + (1.0 - mix_rate) * lax.all_gather(new_global, "rep", axis=1, tiled=True)
    )[None]
    weight_rows = kv_weight[0]
    token_part = tokens
    kv_out = lax.psum_scatter(
        jnp.dot(token_part, weight_rows, preferred_element_type=jnp.float32).astype(jnp.bfloat16),
        "fsdp",
        scatter_dimension=0,
        tiled=True,
    ).astype(jnp.float32)
    cot_piece = lax.all_gather(kv_cotangent, "fsdp", axis=0, tiled=True)
    token_part = tokens
    grad_w = lax.dot_general(
        token_part, cot_piece, (((0,), (0,)), ((), ())), preferred_element_type=jnp.float32
    )
    input_part = lax.dot_general(
        cot_piece, weight_rows, (((1,), (1,)), ((), ())), preferred_element_type=jnp.float32
    )
    grad_x = input_part
    grad_w, grad_x = (grad_w, grad_x)
    grad_weight = grad_w.astype(jnp.bfloat16)[None]
    return (new_global, new_momentum, mixed_local, kv_out, grad_weight, grad_x)


def solution(mesh):
    placed = (
        P("rep", "fsdp", None),
        P("fsdp", None),
        P("fsdp", "rep"),
        P("rep", "fsdp"),
        P("rep", "fsdp", None),
        P(("rep", "fsdp"), None),
    )
    return jax.shard_map(
        shards,
        mesh=mesh,
        in_specs=placed,
        out_specs=(
            P("fsdp", "rep"),
            P("fsdp", "rep"),
            P("rep", "fsdp", None),
            P(("rep", "fsdp"), None),
            P("rep", "fsdp", None),
            P("rep", "fsdp"),
        ),
        check_vma=False,
    )
```

profile of v0, /device:TPU:1, one launch (start us, length us, event | category | flops | bytes accessed | tf_op | source)
XLA Modules:
  0.0 355.8 jit_solution(3354920361811865829)
XLA Ops:
  8.0 0.0 copy-start
  8.0 0.0 reduce-scatter.3.cloned.1.call-start
  8.1 2.7 fusion.10
  10.8 2.0 abs.18
  12.8 0.6 reduce_max.9
  13.4 1.9 div.19
  15.3 3.0 div.20
  18.4 0.0 copy-done.1
  18.4 0.0 copy-done.2
  18.4 2.3 convert_multiply_fusion
  20.7 0.0 reduce-scatter.3.cloned.1.call-update
  20.7 0.0 all-gather.5.cloned.1.call-start
  20.8 0.5 all-gather.5.cloned.1.call-update
  21.3 0.0 all-gather.3.cloned.1.call-start
  21.4 159.9 %reduce-scatter.3.cloned.1.call-done = f32[32,256]{1,0:T(8,128)} async-done(((f32[32,8192]{1,0:T(8,128)}), f32[32,256]{1,0:T(8,128)}) %reduce-scatter.3.cloned.1.call-update) | async-done | bytes 32784 | tf_op jit(solution)/shard_map/reduce_scatter | solution.py:24
  181.3 0.0 copy-done.3
  181.3 1.4 multiply_subtract_fusion
  182.7 0.0 all-gather.3.cloned.1.call-update
  182.7 0.0 reduce-scatter.5.cloned.1.call-start
  182.8 0.0 copy-done
  182.8 5.9 %fusion.4 = bf16[512,2048]{1,0:T(8,128)(2,1)} fusion(bf16[512,1024]{1,0:T(8,128)(2,1)S(1)} %copy-done, bf16[1,1024,2048]{2,1,0:T(8,128)(2,1)} %param.10), kind=kOutput, calls=%fused_computation.5 | convolution fusion | flops 2148532224 | bytes 7340032 | tf_op jit(solution)/shard_map/dot_general | solution.py:41
  188.6 0.0 reduce-scatter.5.cloned.1.call-update
  188.7 0.0 all-gather.5.cloned.1.call-done
  188.7 0.0 copy-start.4
  188.7 0.0 copy-start.5
  188.7 6.1 %convert_bitcast_fusion = bf16[1,1024,2048]{2,1,0:T(8,128)(2,1)} fusion(bf16[512,1024]{1,0:T(8,128)(2,1)S(1)} %copy-done, bf16[512,2048]{1,0:T(8,128)(2,1)} %all-gather.5.cloned.1.call-done), kind=kOutput, calls=%fused_computation.4 | convolution fusion | flops 2149580800 | bytes 7340032 | tf_op jit(solution)/shard_map/dot_general | solution.py:48
  194.9 0.0 copy-done.4
  194.9 3.7 %fusion = f32[512,1024]{1,0:T(8,128)} fusion(bf16[512,2048]{1,0:T(8,128)(2,1)S(1)} %copy-done.5, bf16[1,1024,2048]{2,1,0:T(8,128)(2,1)S(1)} %copy-done.4), kind=kOutput, calls=%fused_computation | convolution fusion | flops 2147483648 | bytes 8388608 | tf_op jit(solution)/shard_map/dot_general | solution.py:51
  198.6 51.9 %all-gather.3.cloned.1.call-done = f32[32,8192]{1,0:T(8,128)} async-done(((f32[32,256]{1,0:T(8,128)}), f32[32,8192]{1,0:T(8,128)}) %all-gather.3.cloned.1.call-update) | async-done | bytes 1048592 | tf_op jit(solution)/shard_map/all_gather | solution.py:36
  250.4 2.3 fusion.8
  252.7 93.7 %reduce-scatter.5.cloned.1.call-done = bf16[64,2048]{1,0:T(8,128)(2,1)} async-done(((bf16[512,2048]{1,0:T(8,128)(2,1)}), bf16[64,2048]{1,0:T(8,128)(2,1)}) %reduce-scatter.5.cloned.1.call-update) | async-done | bytes 262160 | tf_op jit(solution)/shard_map/reduce_scatter | solution.py:40
  346.4 1.8 convert_element_type.45
  (5 shorter events, 0.0 us)
Async XLA Ops:
  8.0 174.8 %copy-start = (bf16[512,1024]{1,0:T(8,128)(2,1)S(1)}, bf16[512,1024]{1,0:T(8,128)(2,1)}, u32[]{:S(2)}) copy-start(bf16[512,1024]{1,0:T(8,128)(2,1)} %param.9) | copy-start | bytes 3145732
  8.0 173.3 %reduce-scatter.3.cloned.1.call-start = ((), (), s32[]{:S(2)}) async-start(), calls=%async_computation.2 | async-start | bytes 1081344 | tf_op jit(solution)/shard_map/reduce_scatter | solution.py:24
  15.3 3.0 copy-start.1
  15.3 3.0 copy-start.2
  18.4 163.0 %copy-start.3 = (f32[32,256]{1,0:T(8,128)S(1)}, f32[32,256]{1,0:T(8,128)}, u32[]{:S(2)}) copy-start(f32[32,256]{1,0:T(8,128)} %param.8) | copy-start | bytes 98308
  20.7 168.0 %all-gather.5.cloned.1.call-start = ((), (), s32[]{:S(2)}) async-start(), calls=%async_computation.5 | async-start | bytes 2359296 | tf_op jit(solution)/shard_map/all_gather | solution.py:46
  21.3 229.1 %all-gather.3.cloned.1.call-start = ((), (), s32[]{:S(2)}) async-start(), calls=%async_computation.3 | async-start | bytes 1081344 | tf_op jit(solution)/shard_map/all_gather | solution.py:36
  182.7 163.6 %reduce-scatter.5.cloned.1.call-start = ((), (), s32[]{:S(2)}) async-start(), calls=%async_computation.4 | async-start | bytes 2359296 | tf_op jit(solution)/shard_map/reduce_scatter | solution.py:40
  188.7 6.2 %copy-start.4 = (bf16[1,1024,2048]{2,1,0:T(8,128)(2,1)S(1)}, bf16[1,1024,2048]{2,1,0:T(8,128)(2,1)}, u32[]{:S(2)}) copy-start(bf16[1,1024,2048]{2,1,0:T(8,128)(2,1)} %param.10) | copy-start | bytes 12582916
  188.7 6.2 %copy-start.5 = (bf16[512,2048]{1,0:T(8,128)(2,1)S(1)}, bf16[512,2048]{1,0:T(8,128)(2,1)}, u32[]{:S(2)}) copy-start(bf16[512,2048]{1,0:T(8,128)(2,1)} %all-gather.5.cloned.1.call-done) | copy-start | bytes 6291460
Sparse Core Ops, SparseCore 0:
  20.9 160.4 reduce-scatter.2
Sparse Core Ops, SparseCore 1:
  24.2 72.9 all-gather.4
  182.8 67.5 all-gather.2
  254.9 91.4 reduce-scatter.4
where the time goes:
time: 357 us; the launch traced here: 356 us
  waiting for transfers between devices  306 us (86%)
  matrix products  15.7 us (4%)
  between operations  15.7 us (4%)
  other arithmetic  11.1 us (3%)
  local copies, waits for them, and re-layouts  6.98 us (2%)
    reduce_scatter x1, waiting for transfers between devices, shards(): lax.psum_scatter(restored.reshape(row_count, full_width), 'rep', scatter_...  160 us
    reduce_scatter x1, waiting for transfers between devices, shards(): lax.psum_scatter(jnp.dot(token_part, weight_rows, preferred_element_type=...  93.7 us
    all_gather x1, waiting for transfers between devices, shards(): lax.all_gather(new_global, 'rep', axis=1, tiled=True)  51.9 us
  transfers between devices with their start and end apart: 4, of which 3 were waited for; matrix products, arithmetic and copies ran while one was open for 5% of the time, Pallas kernels for 0%

commit v1 on v0

v1 whole, which is shorter than its diff:
```python
import jax
import jax.numpy as jnp
from jax import lax
from jax.experimental import pallas as pl
from jax.experimental.pallas import tpu as pltpu
from jax.sharding import PartitionSpec as P

BLOCK = 64
epsilon = 1e-06
momentum_rate = 0.9
outer_rate = 0.7
mix_rate = 0.5

N_REP = 32
N_FSDP = 8
OWN = 256
ROWS = 32
MASKS = (0, 3, 1, 2)

f32 = jnp.float32
bf16 = jnp.bfloat16


def swap_rep(value, mask):
    return lax.ppermute(value, "rep", [(r, r ^ mask) for r in range(N_REP)])


def swap_z(value):
    return lax.ppermute(value, "fsdp", [(f, f ^ 4) for f in range(N_FSDP)])


def shift_y(value, step):
    return lax.ppermute(
        value, "fsdp", [(f, (f & 4) | ((f + step) & 3)) for f in range(N_FSDP)]
    )


def column_of(rep, position, z_lo, core):
    x = ((rep >> 1) & 3) ^ MASKS[position]
    return pl.multiple_of((z_lo * 8 + x * 2 + core) * OWN, OWN)


def quantize_kernel(rep_ref, local_ref, global_ref, keep_ref, send_ref):
    rep = rep_ref[0]
    low = lax.broadcasted_iota(jnp.int32, (ROWS, 128), 1) < BLOCK

    def restored(column):
        parts = []
        for half in range(2):
            at = pl.ds(column + half * 128, 128)
            pseudo = global_ref[:, at] - local_ref[0, :, at]
            size = jnp.abs(pseudo)
            first = jnp.max(jnp.where(low, size, 0.0), axis=1, keepdims=True)
            second = jnp.max(jnp.where(low, 0.0, size), axis=1, keepdims=True)
            scale = (jnp.where(low, first, second) + epsilon).astype(bf16).astype(f32)
            parts.append((pseudo / scale).astype(bf16).astype(f32) * scale)
        return jnp.concatenate(parts, axis=1)

    core = rep & 1
    for position in range(4):
        for z_lo in range(4):
            send_ref[position, z_lo] = restored(
                column_of(rep, position, z_lo, 1 - core)
            ).astype(bf16)
            keep_ref[position, z_lo] = restored(column_of(rep, position, z_lo, core))


VMEM = pl.BlockSpec(memory_space=pltpu.VMEM)
SMEM = pl.BlockSpec(memory_space=pltpu.SMEM)


def quantize(rep, local_params, global_params):
    return pl.pallas_call(
        quantize_kernel,
        out_shape=(
            jax.ShapeDtypeStruct((4, 4, ROWS, OWN), f32),
            jax.ShapeDtypeStruct((4, 4, ROWS, OWN), bf16),
        ),
        in_specs=[SMEM, VMEM, VMEM],
        out_specs=(VMEM, VMEM),
        compiler_params=pltpu.CompilerParams(vmem_limit_bytes=16 * 2**20),
        name="quantize",
    )(rep, local_params, global_params)


def mix_kernel(rep_ref, local_ref, global_ref, own_ref, other_ref, mixed_ref):
    rep = rep_ref[0]
    core = rep & 1
    for position in range(4):
        for z_lo in range(4):
            for update_ref, whose in ((own_ref, core), (other_ref, 1 - core)):
                at = pl.ds(column_of(rep, position, z_lo, whose), OWN)
                new_global = global_ref[:, at] - update_ref[position, z_lo].astype(f32)
                mixed_ref[0, :, at] = (
                    mix_rate * local_ref[0, :, at] + (1.0 - mix_rate) * new_global
                )


def mix(rep, local_params, global_params, own, other):
    return pl.pallas_call(
        mix_kernel,
        out_shape=jax.ShapeDtypeStruct(local_params.shape, f32),
        in_specs=[SMEM, VMEM, VMEM, VMEM, VMEM],
        out_specs=VMEM,
        compiler_params=pltpu.CompilerParams(vmem_limit_bytes=16 * 2**20),
        name="mix",
    )(rep, local_params, global_params, own, other)


def outer_step(rep, local_params, global_params, momentum):
    keep, send = quantize(rep.reshape(1), local_params, global_params)
    total = keep + swap_rep(send, 1).astype(f32)
    got = swap_rep(total[2:].astype(bf16), 2)
    total = total[:2] + got.astype(f32)
    got = swap_rep(total[1].astype(bf16), 6)
    total = total[0] + got.astype(f32)
    z_lo = rep >> 3
    mine = momentum.astype(bf16)[None]
    got = swap_rep(jnp.concatenate([total.astype(bf16), mine]), 8)
    total = total + got[:4].astype(f32)
    pair = jnp.concatenate([mine, got[4:]])
    got = swap_rep(jnp.concatenate([total.astype(bf16), pair]), 16)
    total = total + got[:4].astype(f32)
    momenta = jnp.concatenate([pair, got[4:]]).astype(f32)
    delta = total / N_REP
    own_delta = lax.dynamic_index_in_dim(delta, z_lo, 0, keepdims=False)
    new_momentum = momentum_rate * momentum + own_delta
    own_global = lax.dynamic_slice_in_dim(global_params, rep * OWN, OWN, 1)
    new_global = own_global - outer_rate * (own_delta + momentum_rate * new_momentum)
    momenta = jnp.stack(
        [
            lax.dynamic_index_in_dim(momenta, z_lo ^ z, 0, keepdims=False)
            for z in range(4)
        ]
    )
    update = outer_rate * (
        delta + momentum_rate * (momentum_rate * momenta + delta)
    )
    update = update.astype(bf16)[None]
    update = jnp.concatenate([update, swap_rep(update, 6)])
    update = jnp.concatenate([update, swap_rep(update, 2)])
    other = swap_rep(update, 1)
    mixed = mix(rep.reshape(1), local_params, global_params, update, other)
    return new_global, new_momentum, mixed


def rows_of(value, target_y, z_hi):
    return lax.dynamic_slice_in_dim(value, z_hi * 256 + target_y * 64, 64, 0)


def project(fsdp, tokens, weight):
    y, z_hi = fsdp & 3, fsdp >> 2
    partial = jnp.dot(tokens, weight, preferred_element_type=f32).astype(bf16)
    chunk = [
        [rows_of(partial, (y + d) & 3, z) for z in range(2)] for d in range(4)
    ]
    from_below = shift_y(chunk[2][0], 1)
    from_above = shift_y(chunk[2][1], -1)
    up = jnp.concatenate(
        [(chunk[1][0].astype(f32) + from_below.astype(f32)).astype(bf16), chunk[1][1]]
    )
    down = jnp.concatenate(
        [chunk[3][0], (chunk[3][1].astype(f32) + from_above.astype(f32)).astype(bf16)]
    )
    from_below = shift_y(up, 1).astype(f32)
    from_above = shift_y(down, -1).astype(f32)
    total = (
        jnp.concatenate([chunk[0][0], chunk[0][1]]).astype(f32) + from_below + from_above
    )
    mine = lax.dynamic_slice_in_dim(total, z_hi * 64, 64, 0)
    theirs = lax.dynamic_slice_in_dim(total, 64 - z_hi * 64, 64, 0)
    return mine + swap_z(theirs.astype(bf16)).astype(f32)


def gather_y(own):
    below = shift_y(own, 1)
    above = shift_y(own, -1)
    far = jnp.concatenate([shift_y(below[:32], 1), shift_y(above[32:], -1)])
    return [own, above, far, below]


def shards(local_params, global_params, momentum, tokens, kv_weight, kv_cotangent):
    rep = lax.axis_index("rep")
    fsdp = lax.axis_index("fsdp")
    y, z_hi = fsdp & 3, fsdp >> 2
    weight = kv_weight[0]

    near = gather_y(kv_cotangent)
    far = gather_y(swap_z(kv_cotangent))
    kv_out = project(fsdp, tokens, weight)
    cotangent = jnp.zeros((512, 2048), bf16)
    for z, pieces in ((z_hi, near), (1 - z_hi, far)):
        for d, piece in enumerate(pieces):
            cotangent = lax.dynamic_update_slice_in_dim(
                cotangent, piece, z * 256 + ((y + d) & 3) * 64, 0
            )
    grad_weight = lax.dot_general(
        tokens, cotangent, (((0,), (0,)), ((), ())), preferred_element_type=f32
    ).astype(bf16)[None]
    grad_tokens = lax.dot_general(
        cotangent, weight, (((1,), (1,)), ((), ())), preferred_element_type=f32
    )
    new_global, new_momentum, mixed = outer_step(
        rep, local_params, global_params, momentum
    )
    return new_global, new_momentum, mixed, kv_out, grad_weight, grad_tokens


def solution(mesh):
    return jax.shard_map(
        shards,
        mesh=mesh,
        in_specs=(
            P("rep", "fsdp", None),
            P("fsdp", None),
            P("fsdp", "rep"),
            P("rep", "fsdp"),
            P("rep", "fsdp", None),
            P(("rep", "fsdp"), None),
        ),
        out_specs=(
            P("fsdp", "rep"),
            P("fsdp", "rep"),
            P("rep", "fsdp", None),
            P(("rep", "fsdp"), None),
            P("rep", "fsdp", None),
            P("rep", "fsdp"),
        ),
        check_vma=False,
    )
```

time: 357 us -> 89.9 us (0.25)
  waiting for transfers between devices: 306 us -> 9.34 us
  starting transfers between devices: 0.17 us -> 42.8 us
  between operations: 15.7 us -> 1.05 us
  local copies, waits for them, and re-layouts: 6.98 us -> 15.9 us
  other arithmetic: 11.1 us -> 6 us
    reduce_scatter x2 -> x0, waiting for transfers between devices: 254 us -> none  [the longest x1 160 us: shards(): lax.psum_scatter(restored.reshape(row_count, full_width), 'rep', scatter_...]
    all_gather x2 -> x0, waiting for transfers between devices: 51.9 us -> none  [the longest x1 51.9 us: shards(): lax.all_gather(new_global, 'rep', axis=1, tiled=True)]
    ppermute x0 -> x22, starting transfers between devices: none -> 42.8 us  [the longest x8 17.8 us: swap_rep(): return lax.ppermute(value, 'rep', [(r, r ^ mask) for r in range(N_REP)])]
    ppermute x0 -> x22, waiting for transfers between devices: none -> 9.34 us  [the longest x8 5.61 us: swap_rep(): return lax.ppermute(value, 'rep', [(r, r ^ mask) for r in range(N_REP)])]
    unnamed x12 -> x25, local copies, waits for them, and re-layouts: 0.03 us -> 8.78 us
    div x2 -> x0, local copies, waits for them, and re-layouts: 4.96 us -> none  [shards(): blocked / scales[..., None].astype(jnp.float32)]
  transfers between devices with their start and end apart: 4 -> 22, of which waited for: 3 -> 4; matrix products, arithmetic and copies ran while one was open for 5% -> 36% of each run, Pallas kernels for 0% -> 1%
where the time goes in v1:
time: 89.9 us; the launch traced here: 89.5 us
  starting transfers between devices  42.8 us (48%)
  local copies, waits for them, and re-layouts  15.9 us (18%)
  matrix products  12.6 us (14%)
  waiting for transfers between devices  9.34 us (10%)
  other arithmetic  6 us (7%)
  Pallas kernels  1.83 us (2%)
  between operations  1.05 us (1%)
    ppermute x8, starting transfers between devices, swap_rep(): return lax.ppermute(value, 'rep', [(r, r ^ mask) for r in range(N_REP)])  17.8 us
    ppermute x12, starting transfers between devices, shift_y(): lax.ppermute(value, 'fsdp', [(f, f & 4 | f + step & 3) for f in range(N_F...  17.7 us
    unnamed x25, local copies, waits for them, and re-layouts  8.78 us
    ppermute x2, starting transfers between devices, swap_z(): return lax.ppermute(value, 'fsdp', [(f, f ^ 4) for f in range(N_FSDP)])  7.31 us
    ppermute x8, waiting for transfers between devices, swap_rep(): return lax.ppermute(value, 'rep', [(r, r ^ mask) for r in range(N_REP)])  5.61 us
    dot_general x1, matrix products, project(): partial = jnp.dot(tokens, weight, preferred_element_type=f32).astype(bf16)  4.52 us
    dot_general x1, matrix products, shards(): lax.dot_general(tokens, cotangent, (((0,), (0,)), ((), ())), preferred_el...  4.37 us
    ppermute x12, waiting for transfers between devices, shift_y(): lax.ppermute(value, 'fsdp', [(f, f & 4 | f + step & 3) for f in range(N_F...  3.72 us
  transfers between devices with their start and end apart: 22, of which 4 were waited for; matrix products, arithmetic and copies ran while one was open for 36% of the time, Pallas kernels for 1%

profile of v1, /device:TPU:1, one launch (start us, length us, event | category | flops | bytes accessed | tf_op | source)
XLA Modules:
  0.0 89.5 jit_solution(5383932368293795287)
XLA Ops:
  0.6 3.6 %collective-permute-start.13 = (bf16[64,2048]{1,0:T(8,128)(2,1)}, bf16[64,2048]{1,0:T(8,128)(2,1)}, u32[]{:S(2)}, u32[]{:S(2)}) collective-permute-start(bf16[64,2048]{1,0:T(8,128)(2,1)} %param.11), channel_id=1, source_target_pairs={{0,3},{1,0},{2,1},{3,2},{4,7},{5,4},{6,5},{7,6},{8,11},{9,8},{10,9... | collective-permute-start | bytes 786440 | tf_op jit(solution)/shard_map/ppermute | solution.py:33
  4.3 6.9 %collective-permute-start.17 = (bf16[64,2048]{1,0:T(8,128)(2,1)}, bf16[64,2048]{1,0:T(8,128)(2,1)}, u32[]{:S(2)}, u32[]{:S(2)}) collective-permute-start(bf16[64,2048]{1,0:T(8,128)(2,1)} %param.11), channel_id=1, source_target_pairs={{0,4},{1,5},{2,6},{3,7},{4,0},{5,1},{6,2},{7,3},{8,12},{9,13},{10,... | collective-permute-start | bytes 786440 | tf_op jit(solution)/shard_map/ppermute | solution.py:29
  11.2 4.5 %fusion.4 = bf16[512,2048]{1,0:T(8,128)(2,1)S(1)} fusion(bf16[512,1024]{1,0:T(8,128)(2,1)S(1)} %copy-done, bf16[1,1024,2048]{2,1,0:T(8,128)(2,1)} %param.10), kind=kOutput, calls=%fused_computation.5 | convolution fusion | flops 2148532224 | bytes 7340032 | tf_op jit(solution)/shard_map/dot_general | solution.py:153
  15.7 1.3 %copy-done.4 = bf16[512,2048]{1,0:T(8,128)(2,1)} copy-done((bf16[512,2048]{1,0:T(8,128)(2,1)}, bf16[512,2048]{1,0:T(8,128)(2,1)S(1)}, u32[]{:S(2)}) %copy-start.4) | copy-done | bytes 2097176
  17.1 1.1 %constant_dynamic-slice_fusion.5 = (bf16[64,2048]{1,0:T(8,128)(2,1)S(1)}, bf16[64,2048]{1,0:T(8,128)(2,1)}, bf16[64,2048]{1,0:T(8,128)(2,1)}, bf16[64,2048]{1,0:...) fusion(bf16[512,2048]{1,0:T(8,128)(2,1)S(1)} %fusion.4, s32[]{:T(128)S(6)} %select_n.76, ...), kind=kLoop, calls=%fused_computation.54 | loop fusion | bytes 3145752 | tf_op jit(solution)/shard_map/dynamic_slice | solution.py:148
  18.1 2.7 %collective-permute-start.10 = (bf16[64,2048]{1,0:T(8,128)(2,1)}, bf16[64,2048]{1,0:T(8,128)(2,1)}, u32[]{:S(2)}, u32[]{:S(2)}) collective-permute-start(bf16[64,2048]{1,0:T(8,128)(2,1)} %get-tuple-element.21), channel_id=1, source_target_pairs={{0,3},{1,0},{2,1},{3,2},{4,7},{5,4},{6,5},{7,6},{8,11},{9,8},{10,9... | collective-permute-start | bytes 786440 | tf_op jit(solution)/shard_map/ppermute | solution.py:33
  21.8 1.9 %collective-permute-start = (bf16[4,4,32,256]{3,2,1,0:T(8,128)(2,1)S(1)}, bf16[4,4,32,256]{3,2,1,0:T(8,128)(2,1)S(1)}, u32[]{:S(2)}, u32[]{:S(2)}) collective-permute-start(bf16[4,4,32,256]{3,2,1,0:T(8,128)(2,1)S(1)} %get-tuple-element.9), channel_id=1, source_target_pairs={{0,8},{8,0},{16,24},{24,16},{32,40},{40,32},{48,56},{56,48},{64,72... | collective-permute-start | bytes 786440 | tf_op jit(solution)/shard_map/ppermute | solution.py:25
  23.7 0.9 %slice.58 = bf16[32,2048]{1,0:T(8,128)(2,1)S(1)} slice(bf16[64,2048]{1,0:T(8,128)(2,1)} %collective-permute-done.14), slice={[0:32], [0:2048]} | slice | bytes 262144 | tf_op jit(solution)/shard_map/slice | solution.py:178
  24.7 0.9 %slice.59 = bf16[32,2048]{1,0:T(8,128)(2,1)S(1)} slice(bf16[64,2048]{1,0:T(8,128)(2,1)} %collective-permute-done.13), slice={[32:64], [0:2048]} | slice | bytes 262144 | tf_op jit(solution)/shard_map/slice | solution.py:178
  25.7 3.0 %collective-permute-start.16 = (bf16[32,2048]{1,0:T(8,128)(2,1)S(1)}, bf16[32,2048]{1,0:T(8,128)(2,1)S(1)}, u32[]{:S(2)}, u32[]{:S(2)}) collective-permute-start(bf16[32,2048]{1,0:T(8,128)(2,1)S(1)} %slice.59), channel_id=1, source_target_pairs={{0,3},{1,0},{2,1},{3,2},{4,7},{5,4},{6,5},{7,6},{8,11},{9,8},{10,9... | collective-permute-start | bytes 393224 | tf_op jit(solution)/shard_map/ppermute | solution.py:33
  28.7 1.3 %add_convert_fusion.1 = (bf16[64,2048]{1,0:T(8,128)(2,1)S(1)}, bf16[64,2048]{1,0:T(8,128)(2,1)S(1)}) fusion(bf16[64,2048]{1,0:T(8,128)(2,1)} %collective-permute-done.8, bf16[512,2048]{1,0:T(8,128)(2,1)} %copy-done.4, s32[]{:T(128)S(6)} %select_n.78, bf16[64,2048]{1,0:T(8,128)(2,1)} %collective-permute-done.10, s32[]{:T(128)S(6)} %select_n.82), kind=kLoop, calls=%fused_computation.12 | loop fusion | flops 1048576 | bytes 1572872 | tf_op jit(solution)/shard_map/convert_element_type | solution.py:160
  30.3 1.3 %collective-permute-start.1 = (bf16[2,4,32,256]{3,2,1,0:T(8,128)(2,1)S(1)}, bf16[2,4,32,256]{3,2,1,0:T(8,128)(2,1)S(1)}, u32[]{:S(2)}, u32[]{:S(2)}) collective-permute-start(bf16[2,4,32,256]{3,2,1,0:T(8,128)(2,1)S(1)} %slice.79), channel_id=1, source_target_pairs={{0,16},{8,24},{16,0},{24,8},{32,48},{40,56},{48,32},{56,40},{64,80... | collective-permute-start | bytes 393224 | tf_op jit(solution)/shard_map/ppermute | solution.py:25
  31.6 1.0 %constant_dynamic-update-slice_fusion.4 = bf16[512,2048]{1,0:T(8,128)(2,1)S(1)} fusion(bf16[512,2048]{1,0:T(8,128)(2,1)S(1)} %constant_dynamic-update-slice_fusion.5, bf16[64,2048]{1,0:T(8,128)(2,1)} %collective-permute-done.13, s32[]{:T(128)S(6)} %select_n.87), kind=kLoop, calls=%fused_computation.47 | loop fusion | bytes 524292 | tf_op jit(solution)/shard_map/dynamic_update_slice | solution.py:194
  32.6 2.7 %collective-permute-start.11 = (bf16[128,2048]{1,0:T(8,128)(2,1)S(1)}, bf16[128,2048]{1,0:T(8,128)(2,1)S(1)}, u32[]{:S(2)}, u32[]{:S(2)}) collective-permute-start(bf16[128,2048]{1,0:T(8,128)(2,1)S(1)} %pad_maximum_fusion.1), channel_id=1, source_target_pairs={{0,3},{1,0},{2,1},{3,2},{4,7},{5,4},{6,5},{7,6},{8,11},{9,8},{10,9... | collective-permute-start | bytes 1572872 | tf_op jit(solution)/shard_map/ppermute | solution.py:33
  35.3 1.8 %collective-permute-start.18 = (bf16[64,2048]{1,0:T(8,128)(2,1)}, bf16[64,2048]{1,0:T(8,128)(2,1)S(1)}, u32[]{:S(2)}, u32[]{:S(2)}) collective-permute-start(bf16[64,2048]{1,0:T(8,128)(2,1)} %collective-permute-done.17), channel_id=1, source_target_pairs={{0,3},{1,0},{2,1},{3,2},{4,7},{5,4},{6,5},{7,6},{8,11},{9,8},{10,9... | collective-permute-start | bytes 786440 | tf_op jit(solution)/shard_map/ppermute | solution.py:33
  37.5 2.6 %collective-permute-start.2 = (bf16[4,32,256]{2,1,0:T(8,128)(2,1)S(1)}, bf16[4,32,256]{2,1,0:T(8,128)(2,1)S(1)}, u32[]{:S(2)}, u32[]{:S(2)}) collective-permute-start(bf16[4,32,256]{2,1,0:T(8,128)(2,1)S(1)} %fusion.14), channel_id=1, source_target_pairs={{0,48},{8,56},{16,32},{24,40},{32,16},{40,24},{48,0},{56,8},{64,11... | collective-permute-start | bytes 196616 | tf_op jit(solution)/shard_map/ppermute | solution.py:25
  40.1 1.0 %constant_dynamic-update-slice_fusion.3 = bf16[512,2048]{1,0:T(8,128)(2,1)S(1)} fusion(bf16[512,2048]{1,0:T(8,128)(2,1)S(1)} %maximum_dynamic-update-slice_fusion, bf16[64,2048]{1,0:T(8,128)(2,1)} %collective-permute-done.14, s32[]{:T(128)S(6)} %select_n.89), kind=kLoop, calls=%fused_computation.46 | loop fusion | bytes 524292 | tf_op jit(solution)/shard_map/dynamic_update_slice | solution.py:194
  41.0 1.1 %collective-permute-done.2 = bf16[4,32,256]{2,1,0:T(8,128)(2,1)S(1)} collective-permute-done((bf16[4,32,256]{2,1,0:T(8,128)(2,1)S(1)}, bf16[4,32,256]{2,1,0:T(8,128)(2,1)S(1)}, u32[]{:S(2)}, u32[]{:S(2)}) %collective-permute-start.2) | collective-permute-done | bytes 65568 | tf_op jit(solution)/shard_map/ppermute | solution.py:25
  43.0 1.1 %constant_dynamic-update-slice_fusion.2 = bf16[512,2048]{1,0:T(8,128)(2,1)S(1)} fusion(bf16[512,2048]{1,0:T(8,128)(2,1)S(1)} %constant_dynamic-update-slice_fusion.3, bf16[64,2048]{1,0:T(8,128)(2,1)} %collective-permute-done.17, s32[]{:T(128)S(6)} %select_n.90), kind=kLoop, calls=%fused_computation.45 | loop fusion | bytes 524292 | tf_op jit(solution)/shard_map/dynamic_update_slice | solution.py:194
  44.1 3.1 %collective-permute-done.19 = bf16[64,2048]{1,0:T(8,128)(2,1)S(1)} collective-permute-done((bf16[64,2048]{1,0:T(8,128)(2,1)}, bf16[64,2048]{1,0:T(8,128)(2,1)S(1)}, u32[]{:S(2)}, u32[]{:S(2)}) %collective-permute-start.19) | collective-permute-done | bytes 262176 | tf_op jit(solution)/shard_map/ppermute | solution.py:33
  48.0 3.4 %collective-permute-start.21 = (bf16[32,2048]{1,0:T(8,128)(2,1)S(1)}, bf16[32,2048]{1,0:T(8,128)(2,1)S(1)}, u32[]{:S(2)}, u32[]{:S(2)}) collective-permute-start(bf16[32,2048]{1,0:T(8,128)(2,1)S(1)} %slice.61), channel_id=1, source_target_pairs={{0,3},{1,0},{2,1},{3,2},{4,7},{5,4},{6,5},{7,6},{8,11},{9,8},{10,9... | collective-permute-start | bytes 393224 | tf_op jit(solution)/shard_map/ppermute | solution.py:33
  51.4 1.3 %collective-permute-start.4 = (bf16[6,32,256]{2,1,0:T(8,128)(2,1)S(1)}, bf16[6,32,256]{2,1,0:T(8,128)(2,1)S(1)}, u32[]{:S(2)}, u32[]{:S(2)}) collective-permute-start(bf16[6,32,256]{2,1,0:T(8,128)(2,1)S(1)} %pad_maximum_fusion.4), channel_id=1, source_target_pairs={{0,128},{8,136},{16,144},{24,152},{32,160},{40,168},{48,176},{56,1... | collective-permute-start | bytes 294920 | tf_op jit(solution)/shard_map/ppermute | solution.py:25
  52.7 4.5 %collective-permute-done.4 = bf16[6,32,256]{2,1,0:T(8,128)(2,1)S(1)} collective-permute-done((bf16[6,32,256]{2,1,0:T(8,128)(2,1)S(1)}, bf16[6,32,256]{2,1,0:T(8,128)(2,1)S(1)}, u32[]{:S(2)}, u32[]{:S(2)}) %collective-permute-start.4) | collective-permute-done | bytes 98336 | tf_op jit(solution)/shard_map/ppermute | solution.py:25
  57.3 1.9 %collective-permute-start.5 = (bf16[1,4,32,256]{3,2,1,0:T(8,128)(2,1)S(1)}, bf16[1,4,32,256]{3,2,1,0:T(8,128)(2,1)S(1)}, u32[]{:S(2)}, u32[]{:S(2)}) collective-permute-start(bf16[1,4,32,256]{3,2,1,0:T(8,128)(2,1)S(1)} %get-tuple-element.16), channel_id=1, source_target_pairs={{0,48},{8,56},{16,32},{24,40},{32,16},{40,24},{48,0},{56,8},{64,11... | collective-permute-start | bytes 196616 | tf_op jit(solution)/shard_map/ppermute | solution.py:25
  60.0 3.7 %fusion = f32[512,1024]{1,0:T(8,128)} fusion(bf16[512,2048]{1,0:T(8,128)(2,1)S(1)} %constant_dynamic-update-slice_fusion, bf16[1,1024,2048]{2,1,0:T(8,128)(2,1)S(1)} %copy-done.11), kind=kOutput, calls=%fused_computation | convolution fusion | flops 2147483648 | bytes 8388608 | tf_op jit(solution)/shard_map/dot_general | solution.py:200
  64.9 1.0 %copy-done.3 = f32[128,2048]{1,0:T(8,128)} copy-done((f32[128,2048]{1,0:T(8,128)}, f32[128,2048]{1,0:T(8,128)S(1)}, u32[]{:S(2)}) %copy-start.3) | copy-done | bytes 1048600
  67.0 4.4 %convert_bitcast_fusion = bf16[1,1024,2048]{1,2,0:T(8,128)(2,1)} fusion(bf16[512,2048]{1,0:T(8,128)(2,1)S(1)} %constant_dynamic-update-slice_fusion, bf16[512,1024]{1,0:T(8,128)(2,1)S(1)} %copy-done), kind=kOutput, calls=%fused_computation.4 | convolution fusion | flops 2149580800 | bytes 7340032 | tf_op jit(solution)/shard_map/dot_general | solution.py:197
  71.3 6.4 %copy.12 = bf16[1,1024,2048]{2,1,0:T(8,128)(2,1)} copy(bf16[1,1024,2048]{1,2,0:T(8,128)(2,1)} %convert_bitcast_fusion) | data formatting | bytes 8388608
  77.8 0.9 %pad_maximum_fusion.2.own_ref = bf16[4,4,32,256]{3,2,1,0:T(8,128)(2,1)S(1)} fusion(bf16[2,4,32,256]{3,2,1,0:T(8,128)(2,1)} %collective-permute-done.6, bf16[1,4,32,256]{3,2,1,0:T(8,128)(2,1)S(1)} %collective-permute-done.5, bf16[1,4,32,256]{3,2,1,0:T(8,128)(2,1)S(1)} %get-tuple-element.16), kind=kLoop, calls=%fused_computation.16 | loop fusion | flops 262144 | bytes 524288 | tf_op jit(solution)/shard_map/concatenate | solution.py:141
  78.7 7.7 %collective-permute-start.7 = (bf16[4,4,32,256]{3,2,1,0:T(8,128)(2,1)S(1)}, bf16[4,4,32,256]{3,2,1,0:T(8,128)(2,1)S(1)}, u32[]{:S(2)}, u32[]{:S(2)}) collective-permute-start(bf16[4,4,32,256]{3,2,1,0:T(8,128)(2,1)S(1)} %pad_maximum_fusion.2.own_ref), channel_id=1, source_target_pairs={{0,8},{8,0},{16,24},{24,16},{32,40},{40,32},{48,56},{56,48},{64,72... | collective-permute-start | bytes 786440 | tf_op jit(solution)/shard_map/ppermute | solution.py:25
  86.4 1.9 %convert_add_fusion.1 = f32[64,2048]{1,0:T(8,128)} fusion(bf16[64,2048]{1,0:T(8,128)(2,1)S(1)} %collective-permute-done.12, f32[128,2048]{1,0:T(8,128)} %copy-done.3, s32[]{:T(128)S(6)} %select_n.84), kind=kLoop, calls=%fused_computation.9 | loop fusion | flops 262144 | bytes 1310724 | tf_op jit(solution)/shard_map/add | solution.py:172
  88.3 1.2 %mix.1 = f32[1,32,8192]{2,1,0:T(8,128)} custom-call(s32[1]{0:T(128)} %bitcast.rep_ref, f32[1,32,8192]{2,1,0:T(8,128)S(1)} %copy-done.2, f32[32,8192]{1,0:T(8,128)S(1)} %copy-done.1, bf16[4,4,32,256]{3,2,1,0:T(8,128)(2,1)S(1)} %pad_maximum_fusion.2.own_ref, bf16[4,4,32,256]{3,2,1,0:T(8,128)(2,1)S(1)} %collective-permute-done.7.other_ref), custom_call_target="tpu_custom_call" | custom-call | tf_op jit(solution)/shard_map/mix/pallas_call | solution.py:100
  (79 shorter events, 6.4 us)
Async XLA Ops:
  0.6 10.6 %copy-start = (bf16[512,1024]{1,0:T(8,128)(2,1)S(1)}, bf16[512,1024]{1,0:T(8,128)(2,1)}, u32[]{:S(2)}) copy-start(bf16[512,1024]{1,0:T(8,128)(2,1)} %param.9) | copy-start | bytes 3145732
  0.6 24.0 %collective-permute-start.13 = (bf16[64,2048]{1,0:T(8,128)(2,1)}, bf16[64,2048]{1,0:T(8,128)(2,1)}, u32[]{:S(2)}, u32[]{:S(2)}) collective-permute-start(bf16[64,2048]{1,0:T(8,128)(2,1)} %param.11), channel_id=1, source_target_pairs={{0,3},{1,0},{2,1},{3,2},{4,7},{5,4},{6,5},{7,6},{8,11},{9,8},{10,9... | collective-permute-start | bytes 786440 | tf_op jit(solution)/shard_map/ppermute | solution.py:33
  4.3 17.5 %collective-permute-start.14 = (bf16[64,2048]{1,0:T(8,128)(2,1)}, bf16[64,2048]{1,0:T(8,128)(2,1)}, u32[]{:S(2)}, u32[]{:S(2)}) collective-permute-start(bf16[64,2048]{1,0:T(8,128)(2,1)} %param.11), channel_id=1, source_target_pairs={{0,1},{1,2},{2,3},{3,0},{4,5},{5,6},{6,7},{7,4},{8,9},{9,10},{10,1... | collective-permute-start | bytes 786440 | tf_op jit(solution)/shard_map/ppermute | solution.py:33
  4.3 28.3 %collective-permute-start.17 = (bf16[64,2048]{1,0:T(8,128)(2,1)}, bf16[64,2048]{1,0:T(8,128)(2,1)}, u32[]{:S(2)}, u32[]{:S(2)}) collective-permute-start(bf16[64,2048]{1,0:T(8,128)(2,1)} %param.11), channel_id=1, source_target_pairs={{0,4},{1,5},{2,6},{3,7},{4,0},{5,1},{6,2},{7,3},{8,12},{9,13},{10,... | collective-permute-start | bytes 786440 | tf_op jit(solution)/shard_map/ppermute | solution.py:29
  15.7 1.3 %copy-start.4 = (bf16[512,2048]{1,0:T(8,128)(2,1)}, bf16[512,2048]{1,0:T(8,128)(2,1)S(1)}, u32[]{:S(2)}) copy-start(bf16[512,2048]{1,0:T(8,128)(2,1)S(1)} %fusion.4) | copy-start | bytes 6291460
  17.1 3.7 %copy-start.9 = (f32[32,256]{1,0:T(8,128)S(1)}, f32[32,256]{1,0:T(8,128)}, u32[]{:S(2)}) copy-start(f32[32,256]{1,0:T(8,128)} %param.8) | copy-start | bytes 98308
  17.1 3.8 %copy-start.1 = (f32[32,8192]{1,0:T(8,128)S(1)}, f32[32,8192]{1,0:T(8,128)}, u32[]{:S(2)}) copy-start(f32[32,8192]{1,0:T(8,128)} %global_ref.3) | copy-start | bytes 3145732
  17.1 3.8 %copy-start.2 = (f32[1,32,8192]{2,1,0:T(8,128)S(1)}, f32[1,32,8192]{2,1,0:T(8,128)}, u32[]{:S(2)}) copy-start(f32[1,32,8192]{2,1,0:T(8,128)} %local_ref.3) | copy-start | bytes 3145732
  18.1 7.6 %collective-permute-start.10 = (bf16[64,2048]{1,0:T(8,128)(2,1)}, bf16[64,2048]{1,0:T(8,128)(2,1)}, u32[]{:S(2)}, u32[]{:S(2)}) collective-permute-start(bf16[64,2048]{1,0:T(8,128)(2,1)} %get-tuple-element.21), channel_id=1, source_target_pairs={{0,3},{1,0},{2,1},{3,2},{4,7},{5,4},{6,5},{7,6},{8,11},{9,8},{10,9... | collective-permute-start | bytes 786440 | tf_op jit(solution)/shard_map/ppermute | solution.py:33
  20.8 7.9 %collective-permute-start.8 = (bf16[64,2048]{1,0:T(8,128)(2,1)}, bf16[64,2048]{1,0:T(8,128)(2,1)}, u32[]{:S(2)}, u32[]{:S(2)}) collective-permute-start(bf16[64,2048]{1,0:T(8,128)(2,1)} %get-tuple-element.24), channel_id=1, source_target_pairs={{0,1},{1,2},{2,3},{3,0},{4,5},{5,6},{6,7},{7,4},{8,9},{9,10},{10,1... | collective-permute-start | bytes 786440 | tf_op jit(solution)/shard_map/ppermute | solution.py:33
  21.5 8.5 %copy-start.7 = (bf16[64,2048]{1,0:T(8,128)(2,1)S(1)}, bf16[64,2048]{1,0:T(8,128)(2,1)}, u32[]{:S(2)}) copy-start(bf16[64,2048]{1,0:T(8,128)(2,1)} %get-tuple-element.23) | copy-start | bytes 786436
  21.8 8.3 %collective-permute-start = (bf16[4,4,32,256]{3,2,1,0:T(8,128)(2,1)S(1)}, bf16[4,4,32,256]{3,2,1,0:T(8,128)(2,1)S(1)}, u32[]{:S(2)}, u32[]{:S(2)}) collective-permute-start(bf16[4,4,32,256]{3,2,1,0:T(8,128)(2,1)S(1)} %get-tuple-element.9), channel_id=1, source_target_pairs={{0,8},{8,0},{16,24},{24,16},{32,40},{40,32},{48,56},{56,48},{64,72... | collective-permute-start | bytes 786440 | tf_op jit(solution)/shard_map/ppermute | solution.py:25
  24.7 12.5 %collective-permute-start.15 = (bf16[32,2048]{1,0:T(8,128)(2,1)S(1)}, bf16[32,2048]{1,0:T(8,128)(2,1)S(1)}, u32[]{:S(2)}, u32[]{:S(2)}) collective-permute-start(bf16[32,2048]{1,0:T(8,128)(2,1)S(1)} %slice.58), channel_id=1, source_target_pairs={{0,1},{1,2},{2,3},{3,0},{4,5},{5,6},{6,7},{7,4},{8,9},{9,10},{10,1... | collective-permute-start | bytes 393224 | tf_op jit(solution)/shard_map/ppermute | solution.py:33
  25.7 5.9 %copy-start.6 = (bf16[64,2048]{1,0:T(8,128)(2,1)S(1)}, bf16[64,2048]{1,0:T(8,128)(2,1)}, u32[]{:S(2)}) copy-start(bf16[64,2048]{1,0:T(8,128)(2,1)} %get-tuple-element.22) | copy-start | bytes 786436
  25.7 11.8 %collective-permute-start.16 = (bf16[32,2048]{1,0:T(8,128)(2,1)S(1)}, bf16[32,2048]{1,0:T(8,128)(2,1)S(1)}, u32[]{:S(2)}, u32[]{:S(2)}) collective-permute-start(bf16[32,2048]{1,0:T(8,128)(2,1)S(1)} %slice.59), channel_id=1, source_target_pairs={{0,3},{1,0},{2,1},{3,2},{4,7},{5,4},{6,5},{7,6},{8,11},{9,8},{10,9... | collective-permute-start | bytes 393224 | tf_op jit(solution)/shard_map/ppermute | solution.py:33
  30.1 34.6 %collective-permute-start.9 = (bf16[128,2048]{1,0:T(8,128)(2,1)S(1)}, bf16[128,2048]{1,0:T(8,128)(2,1)S(1)}, u32[]{:S(2)}, u32[]{:S(2)}) collective-permute-start(bf16[128,2048]{1,0:T(8,128)(2,1)S(1)} %pad_maximum_fusion), channel_id=1, source_target_pairs={{0,1},{1,2},{2,3},{3,0},{4,5},{5,6},{6,7},{7,4},{8,9},{9,10},{10,1... | collective-permute-start | bytes 1572872 | tf_op jit(solution)/shard_map/ppermute | solution.py:33
  30.3 5.1 %collective-permute-start.1 = (bf16[2,4,32,256]{3,2,1,0:T(8,128)(2,1)S(1)}, bf16[2,4,32,256]{3,2,1,0:T(8,128)(2,1)S(1)}, u32[]{:S(2)}, u32[]{:S(2)}) collective-permute-start(bf16[2,4,32,256]{3,2,1,0:T(8,128)(2,1)S(1)} %slice.79), channel_id=1, source_target_pairs={{0,16},{8,24},{16,0},{24,8},{32,48},{40,56},{48,32},{56,40},{64,80... | collective-permute-start | bytes 393224 | tf_op jit(solution)/shard_map/ppermute | solution.py:25
  32.6 32.0 %collective-permute-start.11 = (bf16[128,2048]{1,0:T(8,128)(2,1)S(1)}, bf16[128,2048]{1,0:T(8,128)(2,1)S(1)}, u32[]{:S(2)}, u32[]{:S(2)}) collective-permute-start(bf16[128,2048]{1,0:T(8,128)(2,1)S(1)} %pad_maximum_fusion.1), channel_id=1, source_target_pairs={{0,3},{1,0},{2,1},{3,2},{4,7},{5,4},{6,5},{7,6},{8,11},{9,8},{10,9... | collective-permute-start | bytes 1572872 | tf_op jit(solution)/shard_map/ppermute | solution.py:33
  35.3 12.6 %collective-permute-start.18 = (bf16[64,2048]{1,0:T(8,128)(2,1)}, bf16[64,2048]{1,0:T(8,128)(2,1)S(1)}, u32[]{:S(2)}, u32[]{:S(2)}) collective-permute-start(bf16[64,2048]{1,0:T(8,128)(2,1)} %collective-permute-done.17), channel_id=1, source_target_pairs={{0,3},{1,0},{2,1},{3,2},{4,7},{5,4},{6,5},{7,6},{8,11},{9,8},{10,9... | collective-permute-start | bytes 786440 | tf_op jit(solution)/shard_map/ppermute | solution.py:33
  37.2 10.1 %collective-permute-start.19 = (bf16[64,2048]{1,0:T(8,128)(2,1)}, bf16[64,2048]{1,0:T(8,128)(2,1)S(1)}, u32[]{:S(2)}, u32[]{:S(2)}) collective-permute-start(bf16[64,2048]{1,0:T(8,128)(2,1)} %collective-permute-done.17), channel_id=1, source_target_pairs={{0,1},{1,2},{2,3},{3,0},{4,5},{5,6},{6,7},{7,4},{8,9},{9,10},{10,1... | collective-permute-start | bytes 786440 | tf_op jit(solution)/shard_map/ppermute | solution.py:33
  37.5 4.7 %collective-permute-start.2 = (bf16[4,32,256]{2,1,0:T(8,128)(2,1)S(1)}, bf16[4,32,256]{2,1,0:T(8,128)(2,1)S(1)}, u32[]{:S(2)}, u32[]{:S(2)}) collective-permute-start(bf16[4,32,256]{2,1,0:T(8,128)(2,1)S(1)} %fusion.14), channel_id=1, source_target_pairs={{0,48},{8,56},{16,32},{24,40},{32,16},{40,24},{48,0},{56,8},{64,11... | collective-permute-start | bytes 196616 | tf_op jit(solution)/shard_map/ppermute | solution.py:25
  40.0 19.2 %copy-start.10 = (f32[32,256]{1,0:T(8,128)S(1)}, f32[32,256]{1,0:T(8,128)}, u32[]{:S(2)}) copy-start(f32[32,256]{1,0:T(8,128)} %param.8) | copy-start | bytes 98308
  42.2 9.1 %collective-permute-start.3 = (bf16[5,32,256]{2,1,0:T(8,128)(2,1)S(1)}, bf16[5,32,256]{2,1,0:T(8,128)(2,1)S(1)}, u32[]{:S(2)}, u32[]{:S(2)}) collective-permute-start(bf16[5,32,256]{2,1,0:T(8,128)(2,1)S(1)} %pad_maximum_fusion.5), channel_id=1, source_target_pairs={{0,64},{8,72},{16,80},{24,88},{32,96},{40,104},{48,112},{56,120},{... | collective-permute-start | bytes 245768 | tf_op jit(solution)/shard_map/ppermute | solution.py:25
  43.0 16.9 %copy-start.11 = (bf16[1,1024,2048]{2,1,0:T(8,128)(2,1)S(1)}, bf16[1,1024,2048]{2,1,0:T(8,128)(2,1)}, u32[]{:S(2)}) copy-start(bf16[1,1024,2048]{2,1,0:T(8,128)(2,1)} %param.10) | copy-start | bytes 12582916
  47.3 12.6 %collective-permute-start.20 = (bf16[32,2048]{1,0:T(8,128)(2,1)S(1)}, bf16[32,2048]{1,0:T(8,128)(2,1)S(1)}, u32[]{:S(2)}, u32[]{:S(2)}) collective-permute-start(bf16[32,2048]{1,0:T(8,128)(2,1)S(1)} %slice.60), channel_id=1, source_target_pairs={{0,1},{1,2},{2,3},{3,0},{4,5},{5,6},{6,7},{7,4},{8,9},{9,10},{10,1... | collective-permute-start | bytes 393224 | tf_op jit(solution)/shard_map/ppermute | solution.py:33
  48.0 11.9 %collective-permute-start.21 = (bf16[32,2048]{1,0:T(8,128)(2,1)S(1)}, bf16[32,2048]{1,0:T(8,128)(2,1)S(1)}, u32[]{:S(2)}, u32[]{:S(2)}) collective-permute-start(bf16[32,2048]{1,0:T(8,128)(2,1)S(1)} %slice.61), channel_id=1, source_target_pairs={{0,3},{1,0},{2,1},{3,2},{4,7},{5,4},{6,5},{7,6},{8,11},{9,8},{10,9... | collective-permute-start | bytes 393224 | tf_op jit(solution)/shard_map/ppermute | solution.py:33
  51.4 5.8 %collective-permute-start.4 = (bf16[6,32,256]{2,1,0:T(8,128)(2,1)S(1)}, bf16[6,32,256]{2,1,0:T(8,128)(2,1)S(1)}, u32[]{:S(2)}, u32[]{:S(2)}) collective-permute-start(bf16[6,32,256]{2,1,0:T(8,128)(2,1)S(1)} %pad_maximum_fusion.4), channel_id=1, source_target_pairs={{0,128},{8,136},{16,144},{24,152},{32,160},{40,168},{48,176},{56,1... | collective-permute-start | bytes 294920 | tf_op jit(solution)/shard_map/ppermute | solution.py:25
  57.3 6.3 %collective-permute-start.5 = (bf16[1,4,32,256]{3,2,1,0:T(8,128)(2,1)S(1)}, bf16[1,4,32,256]{3,2,1,0:T(8,128)(2,1)S(1)}, u32[]{:S(2)}, u32[]{:S(2)}) collective-permute-start(bf16[1,4,32,256]{3,2,1,0:T(8,128)(2,1)S(1)} %get-tuple-element.16), channel_id=1, source_target_pairs={{0,48},{8,56},{16,32},{24,40},{32,16},{40,24},{48,0},{56,8},{64,11... | collective-permute-start | bytes 196616 | tf_op jit(solution)/shard_map/ppermute | solution.py:25
  60.0 4.7 %copy-start.5 = (bf16[64,2048]{1,0:T(8,128)(2,1)S(1)}, bf16[64,2048]{1,0:T(8,128)(2,1)}, u32[]{:S(2)}) copy-start(bf16[64,2048]{1,0:T(8,128)(2,1)} %get-tuple-element.25) | copy-start | bytes 786436
  64.3 13.4 %collective-permute-start.6 = (bf16[2,4,32,256]{3,2,1,0:T(8,128)(2,1)}, bf16[2,4,32,256]{3,2,1,0:T(8,128)(2,1)}, u32[]{:S(2)}, u32[]{:S(2)}) collective-permute-start(bf16[2,4,32,256]{3,2,1,0:T(8,128)(2,1)} %pad_maximum_fusion.3), channel_id=1, source_target_pairs={{0,16},{8,24},{16,0},{24,8},{32,48},{40,56},{48,32},{56,40},{64,80... | collective-permute-start | bytes 393224 | tf_op jit(solution)/shard_map/ppermute | solution.py:25
  66.6 19.8 %collective-permute-start.12 = (bf16[64,2048]{1,0:T(8,128)(2,1)}, bf16[64,2048]{1,0:T(8,128)(2,1)S(1)}, u32[]{:S(2)}, u32[]{:S(2)}) collective-permute-start(bf16[64,2048]{1,0:T(8,128)(2,1)} %dynamic-slice_convert_fusion), channel_id=1, source_target_pairs={{0,4},{1,5},{2,6},{3,7},{4,0},{5,1},{6,2},{7,3},{8,12},{9,13},{10,... | collective-permute-start | bytes 786440 | tf_op jit(solution)/shard_map/ppermute | solution.py:29
  78.7 9.6 %collective-permute-start.7 = (bf16[4,4,32,256]{3,2,1,0:T(8,128)(2,1)S(1)}, bf16[4,4,32,256]{3,2,1,0:T(8,128)(2,1)S(1)}, u32[]{:S(2)}, u32[]{:S(2)}) collective-permute-start(bf16[4,4,32,256]{3,2,1,0:T(8,128)(2,1)S(1)} %pad_maximum_fusion.2.own_ref), channel_id=1, source_target_pairs={{0,8},{8,0},{16,24},{24,16},{32,40},{40,32},{48,56},{56,48},{64,72... | collective-permute-start | bytes 786440 | tf_op jit(solution)/shard_map/ppermute | solution.py:25
  (2 other events, 1.9 us)

commit v2 on v0

v2 whole, which is shorter than its diff:
```python
import jax
import jax.numpy as jnp
from jax import lax
from jax.experimental import pallas as pl
from jax.experimental.pallas import tpu as pltpu
from jax.sharding import PartitionSpec as P

BLOCK = 64
epsilon = 1e-06
momentum_rate = 0.9
outer_rate = 0.7
mix_rate = 0.5

N_REP = 32
N_FSDP = 8
OWN = 256
ROWS = 32
MASKS = (0, 3, 1, 2)

f32 = jnp.float32
bf16 = jnp.bfloat16
VMEM = pl.BlockSpec(memory_space=pltpu.VMEM)
SMEM = pl.BlockSpec(memory_space=pltpu.SMEM)
HBM = pl.BlockSpec(memory_space=pltpu.HBM)
NT = (((1,), (1,)), ((), ()))


def after(value, *others):
    return lax.optimization_barrier((value, *others))[0]


def swap_rep(value, mask):
    return lax.ppermute(value, "rep", [(r, r ^ mask) for r in range(N_REP)])


def swap_z(value):
    return lax.ppermute(value, "fsdp", [(f, f ^ 4) for f in range(N_FSDP)])


def shift_y(value, step):
    return lax.ppermute(
        value, "fsdp", [(f, (f & 4) | ((f + step) & 3)) for f in range(N_FSDP)]
    )


def call(kernel, outs, operands, limit=4, in_specs=None, out_specs=None, **more):
    return pl.pallas_call(
        kernel,
        out_shape=tuple(jax.ShapeDtypeStruct(*out) for out in outs),
        in_specs=in_specs or [VMEM] * len(operands),
        out_specs=out_specs or tuple(VMEM for _ in outs),
        cost_estimate=pl.CostEstimate(flops=0, bytes_accessed=0, transcendentals=0),
        compiler_params=pltpu.CompilerParams(vmem_limit_bytes=limit * 2**20),
        name=kernel.__name__,
        **more,
    )(*operands)


BEGIN_MB, GRADIENTS_MB, MIX_MB = 51, 51, 51


def column_of(rep, position, z_lo, core):
    x = ((rep >> 1) & 3) ^ MASKS[position]
    return pl.multiple_of((z_lo * 8 + x * 2 + core) * OWN, OWN)


def restored(pseudo):
    low = lax.broadcasted_iota(jnp.int32, pseudo.shape, 1) < BLOCK
    size = jnp.abs(pseudo)
    first = jnp.max(jnp.where(low, size, 0.0), axis=1, keepdims=True)
    second = jnp.max(jnp.where(low, 0.0, size), axis=1, keepdims=True)
    scale = (jnp.where(low, first, second) + epsilon).astype(bf16).astype(f32)
    return (pseudo / scale).astype(bf16).astype(f32) * scale


def begin(
    rep_ref, fsdp_ref, local_hbm, global_hbm, tokens_hbm, weight_hbm,
    keep, send, own_global, far, up, down, own,
    local, globals_, ordered, weight, fragment_sems, token_sems, weight_sem,
):
    rep, fsdp = rep_ref[0], fsdp_ref[0]
    core = rep & 1
    outs = ((2, far), (1, up), (3, down), (0, own))
    fragment = []
    for part in range(2):
        at = pl.ds(part * 16, 16)
        fragment.append(
            (
                pltpu.make_async_copy(
                    local_hbm.at[0, at], local.at[at], fragment_sems.at[0, part]
                ),
                pltpu.make_async_copy(
                    global_hbm.at[at], globals_.at[at], fragment_sems.at[1, part]
                ),
            )
        )
    token_copies = []
    for i, (d, _) in enumerate(outs):
        for z in range(2):
            token_copies.append(
                pltpu.make_async_copy(
                    tokens_hbm.at[pl.ds(chunk_rows(fsdp, d, z), 64)],
                    ordered.at[pl.ds(i * 128 + z * 64, 64)],
                    token_sems.at[i * 2 + z],
                )
            )
    weight_copy = pltpu.make_async_copy(weight_hbm.at[0], weight, weight_sem)
    for copy in token_copies:
        copy.start()
    weight_copy.start()
    for pair in fragment:
        for copy in pair:
            copy.start()

    for copy in token_copies:
        copy.wait()
    weight_copy.wait()
    for tile in range(8):
        at = slice(tile * 256, tile * 256 + 256)
        partial = jnp.dot(ordered[...], weight[:, at], preferred_element_type=f32).astype(
            bf16
        )
        for i, (_, out) in enumerate(outs):
            out[:, at] = partial[i * 128 : i * 128 + 128]

    def pseudo(rows, column):
        at = pl.ds(column, 128)
        return restored(globals_[rows, at] - local[rows, at])

    for part, pair in enumerate(fragment):
        for copy in pair:
            copy.wait()
        rows = slice(part * 16, part * 16 + 16)
        for position in range(4):
            for z in range(4):
                for half in range(2):
                    to = slice(half * 128, half * 128 + 128)
                    send[position, z, rows, to] = pseudo(
                        rows, column_of(rep, position, z, 1 - core) + half * 128
                    ).astype(bf16)
                    keep[position, z, rows, to] = pseudo(
                        rows, column_of(rep, position, z, core) + half * 128
                    )
    own_global[...] = globals_[:, pl.ds(column_of(rep, 0, rep >> 3, core), OWN)]


def sum_core(keep, got, rest, send):
    rest[...] = keep[:2] + got[:2].astype(f32)
    send[...] = (keep[2:] + got[2:].astype(f32)).astype(bf16)


def sum_x_pair(keep, got, rest, send):
    rest[...] = keep[0] + got[0].astype(f32)
    send[...] = (keep[1] + got[1].astype(f32)).astype(bf16)


def sum_x(keep, got, momentum, rest, send):
    total = keep[...] + got[...].astype(f32)
    rest[...] = total
    send[:4] = total.astype(bf16)
    send[4] = momentum[...].astype(bf16)


def sum_z_pair(keep, got, momentum, rest, send):
    total = keep[...] + got[:4].astype(f32)
    rest[...] = total
    send[:4] = total.astype(bf16)
    send[4] = momentum[...].astype(bf16)
    send[5] = got[4]


def update_step(
    rep_ref, keep, near, far, momentum, own_global, new_global, new_momentum, update
):
    z_lo = rep_ref[0] >> 3

    def stepped(delta, moment):
        moment = momentum_rate * moment + delta
        return outer_rate * (delta + momentum_rate * moment), moment

    sources = (momentum, near.at[4], far.at[4], far.at[5])
    for mask, source in enumerate(sources):
        z = z_lo ^ mask
        delta = (keep[z] + far[z].astype(f32)) / N_REP
        change, moment = stepped(delta, source[...].astype(f32))
        update[z] = change.astype(bf16)
        if mask == 0:
            new_momentum[...] = moment
            new_global[...] = own_global[...] - change


def join(first, second, both):
    both[0] = first[...]
    both[1] = second[...]


def mix(
    rep_ref, local_hbm, global_hbm, own_near, own_far, other_near, other_far, mixed_hbm,
    local, globals_, mixed, sems,
):
    rep = rep_ref[0]
    core = rep & 1
    copies, results = [], []
    for part in range(4):
        at = pl.ds(part * 8, 8)
        copies.append(
            (
                pltpu.make_async_copy(local_hbm.at[0, at], local.at[at], sems.at[0, part]),
                pltpu.make_async_copy(global_hbm.at[at], globals_.at[at], sems.at[1, part]),
            )
        )
        results.append(
            pltpu.make_async_copy(mixed.at[at], mixed_hbm.at[0, at], sems.at[2, part])
        )
    for pair in copies:
        for copy in pair:
            copy.start()
    for part in range(4):
        for copy in copies[part]:
            copy.wait()
        rows = slice(part * 8, part * 8 + 8)
        for pieces, whose in (((own_near, own_far), core), ((other_near, other_far), 1 - core)):
            for position in range(4):
                for z in range(4):
                    at = pl.ds(column_of(rep, position, z, whose), OWN)
                    update = pieces[position // 2][position % 2, z, rows].astype(f32)
                    mixed[rows, at] = mix_rate * local[rows, at] + (1.0 - mix_rate) * (
                        globals_[rows, at] - update
                    )
        results[part].start()
    for copy in results:
        copy.wait()


def chunk_rows(fsdp, d, z):
    return pl.multiple_of(z * 256 + ((fsdp + d) & 3) * 64, 64)


def pack(far, below, above, up, down):
    up[:64] = far[:64]
    up[64:] = below[:32]
    down[:64] = far[64:]
    down[64:] = above[32:]


def add(up, down, from_below, from_above, up_out, down_out):
    up_out[:64] = (up[:64].astype(f32) + from_below[:64].astype(f32)).astype(bf16)
    up_out[64:] = up[64:]
    down_out[:64] = down[:64]
    down_out[64:] = (down[64:].astype(f32) + from_above[:64].astype(f32)).astype(bf16)


def fold(fsdp_ref, own, from_below, from_above, mine, theirs):
    z_hi = fsdp_ref[0] >> 2

    def total(z):
        at = pl.ds(pl.multiple_of(z * 64, 64), 64)
        return own[at].astype(f32) + from_below[at].astype(f32) + from_above[at].astype(f32)

    mine[...] = total(z_hi)
    theirs[...] = total(1 - z_hi).astype(bf16)


def gradients(
    fsdp_ref, tokens_hbm, weight_hbm, own, above, below, far_below, far_above,
    z_own, z_above, z_far, z_below, grad_weight_hbm, grad_tokens_hbm,
    rows, tokens, turned, weight, grad_weight, grad_tokens, in_sems, gx_sems, gw_sems,
):
    fsdp = fsdp_ref[0]
    z_hi = fsdp >> 2
    token_copy = pltpu.make_async_copy(tokens_hbm, tokens, in_sems.at[0])
    weight_copy = pltpu.make_async_copy(weight_hbm.at[0], weight, in_sems.at[1])
    token_copy.start()
    weight_copy.start()

    for d, part in ((0, own), (1, above), (3, below)):
        rows[pl.ds(chunk_rows(fsdp, d, z_hi), 64)] = part[...]
    first = chunk_rows(fsdp, 2, z_hi)
    rows[pl.ds(first, 32)] = far_below[64:]
    rows[pl.ds(pl.multiple_of(first + 32, 32), 32)] = far_above[64:]
    for d, part in enumerate((z_own, z_above, z_far, z_below)):
        rows[pl.ds(chunk_rows(fsdp, d, 1 - z_hi), 64)] = part[...]

    token_copy.wait()
    turned[...] = tokens[...].T
    results = []
    for tile in range(4):
        at = slice(tile * 256, tile * 256 + 256)
        grad_weight[at] = jnp.dot(
            turned[at], rows[...], preferred_element_type=f32
        ).astype(bf16)
        results.append(
            pltpu.make_async_copy(
                grad_weight.at[at], grad_weight_hbm.at[0, at], gw_sems.at[tile]
            )
        )
        results[-1].start()
    weight_copy.wait()
    for tile in range(2):
        at = slice(tile * 256, tile * 256 + 256)
        for part in range(4):
            to = slice(part * 256, part * 256 + 256)
            grad_tokens[at, to] = lax.dot_general(
                rows[at], weight[to], NT, preferred_element_type=f32
            )
        results.append(
            pltpu.make_async_copy(
                grad_tokens.at[at], grad_tokens_hbm.at[at], gx_sems.at[tile]
            )
        )
        results[-1].start()
    for copy in results:
        copy.wait()


def shards(local_params, global_params, momentum, tokens, kv_weight, kv_cotangent):
    rep = lax.axis_index("rep").reshape(1)
    fsdp = lax.axis_index("fsdp").reshape(1)
    part = ((128, 2048), bf16)
    block = (ROWS, OWN)

    z_own = swap_z(kv_cotangent)
    below = shift_y(kv_cotangent, 1)
    above = shift_y(kv_cotangent, -1)
    keep, send, own_global, far, up, down, own = call(
        begin,
        [((4, 4, *block), f32), ((4, 4, *block), bf16), (block, f32)] + [part] * 4,
        (rep, fsdp, local_params, global_params, tokens, kv_weight),
        BEGIN_MB,
        in_specs=[SMEM] * 2 + [HBM] * 4,
        scratch_shapes=[
            pltpu.VMEM((ROWS, 8192), f32),
            pltpu.VMEM((ROWS, 8192), f32),
            pltpu.VMEM((512, 1024), bf16),
            pltpu.VMEM((1024, 2048), bf16),
            pltpu.SemaphoreType.DMA((2, 2)),
            pltpu.SemaphoreType.DMA((8,)),
            pltpu.SemaphoreType.DMA(()),
        ],
    )
    got_core = swap_rep(send, 1)
    far_up, far_down = call(pack, [((96, 2048), bf16)] * 2, (far, below, above))
    from_below = shift_y(far_up, 1)
    from_above = shift_y(far_down, -1)


    rest, send = call(
        sum_core,
        [((2, 4, *block), f32), ((2, 4, *block), bf16)],
        (after(keep, far_up, z_own), got_core),
    )
    got = swap_rep(send, 2)
    up, down = call(add, [part] * 2, (after(up, got), down, from_below, from_above))
    sum_below = shift_y(up, 1)
    sum_above = shift_y(down, -1)
    rest, send = call(
        sum_x_pair,
        [((4, *block), f32), ((4, *block), bf16)],
        (after(rest, up), got),
    )
    got = swap_rep(send, 6)
    rest, send = call(
        sum_x,
        [((4, *block), f32), ((5, *block), bf16)],
        (after(rest, z_own), got, momentum),
    )
    near = swap_rep(send, 8)
    rest, send = call(
        sum_z_pair,
        [((4, *block), f32), ((6, *block), bf16)],
        (rest, near, momentum),
    )
    z_far = swap_rep(send, 16)

    z_own = after(z_own, near)
    z_pieces = (z_own, shift_y(z_own, -1), shift_y(z_own, 2), shift_y(z_own, 1))
    new_global, new_momentum, update = call(
        update_step,
        [(block, f32), (block, f32), ((4, *block), bf16)],
        (rep, rest, near, z_far, momentum, own_global),
        in_specs=[SMEM] + [VMEM] * 5,
    )
    mine, theirs = call(
        fold,
        [((64, 2048), f32), ((64, 2048), bf16)],
        (fsdp, after(own, update), sum_below, sum_above),
        in_specs=[SMEM, VMEM, VMEM, VMEM],
    )
    kv_out = mine + swap_z(theirs).astype(f32)
    (first,) = call(join, [((2, 4, *block), bf16)], (update, swap_rep(update, 6)))
    second = swap_rep(first, 2)
    (mixed,) = call(
        mix,
        [(local_params.shape, f32)],
        (rep, local_params, global_params, first, second, swap_rep(first, 1), swap_rep(second, 1)),
        MIX_MB,
        in_specs=[SMEM, HBM, HBM] + [VMEM] * 4,
        out_specs=(HBM,),
        scratch_shapes=[pltpu.VMEM((ROWS, 8192), f32)] * 3
        + [pltpu.SemaphoreType.DMA((3, 4))],
    )
    grad_weight, grad_tokens = call(
        gradients,
        [((1, 1024, 2048), bf16), ((512, 1024), f32)],
        (fsdp, tokens, kv_weight, after(kv_cotangent, first), above, below, from_below, from_above, *z_pieces),
        GRADIENTS_MB,
        in_specs=[SMEM, HBM, HBM] + [VMEM] * 9,
        out_specs=(HBM, HBM),
        scratch_shapes=[
            pltpu.VMEM((512, 2048), bf16),
            pltpu.VMEM((512, 1024), bf16),
            pltpu.VMEM((1024, 512), bf16),
            pltpu.VMEM((1024, 2048), bf16),
            pltpu.VMEM((1024, 2048), bf16),
            pltpu.VMEM((512, 1024), f32),
            pltpu.SemaphoreType.DMA((2,)),
            pltpu.SemaphoreType.DMA((2,)),
            pltpu.SemaphoreType.DMA((4,)),
        ],
    )
    return new_global, new_momentum, mixed, kv_out, grad_weight, grad_tokens


def solution(mesh):
    return jax.shard_map(
        shards,
        mesh=mesh,
        in_specs=(
            P("rep", "fsdp", None),
            P("fsdp", None),
            P("fsdp", "rep"),
            P("rep", "fsdp"),
            P("rep", "fsdp", None),
            P(("rep", "fsdp"), None),
        ),
        out_specs=(
            P("fsdp", "rep"),
            P("fsdp", "rep"),
            P("rep", "fsdp", None),
            P(("rep", "fsdp"), None),
            P("rep", "fsdp", None),
            P("rep", "fsdp"),
        ),
        check_vma=False,
    )
```

time: 357 us -> 75.8 us (0.21)
  waiting for transfers between devices: 306 us -> 21.9 us
  starting transfers between devices: 0.17 us -> 36.3 us
  Pallas kernels: 0 us -> 15.8 us
  matrix products: 15.7 us -> 0 us
  between operations: 15.7 us -> 0.82 us
  other arithmetic: 11.1 us -> 0.84 us
  local copies, waits for them, and re-layouts: 6.98 us -> 0.02 us
    reduce_scatter x2 -> x0, waiting for transfers between devices: 254 us -> none  [the longest x1 160 us: shards(): lax.psum_scatter(restored.reshape(row_count, full_width), 'rep', scatter_...]
    all_gather x2 -> x0, waiting for transfers between devices: 51.9 us -> none  [the longest x1 51.9 us: shards(): lax.all_gather(new_global, 'rep', axis=1, tiled=True)]
    ppermute x0 -> x20, starting transfers between devices: none -> 36.3 us  [the longest x9 20.1 us: swap_rep(): return lax.ppermute(value, 'rep', [(r, r ^ mask) for r in range(N_REP)])]
    ppermute x0 -> x20, waiting for transfers between devices: none -> 21.9 us  [the longest x9 15.2 us: swap_rep(): return lax.ppermute(value, 'rep', [(r, r ^ mask) for r in range(N_REP)])]
    pallas_call x0 -> x12, Pallas kernels: none -> 15.8 us  [call(): pl.pallas_call(kernel, out_shape=tuple((jax.ShapeDtypeStruct(*out) for ou...]
    dot_general x3 -> x0, matrix products: 15.7 us -> none  [the longest x1 6.14 us: shards(): lax.dot_general(token_part, cot_piece, (((0,), (0,)), ((), ())), preferre...]
    div x2 -> x0, local copies, waits for them, and re-layouts: 4.96 us -> none  [shards(): blocked / scales[..., None].astype(jnp.float32)]
  transfers between devices with their start and end apart: 4 -> 20, of which waited for: 3 -> 7; matrix products, arithmetic and copies ran while one was open for 5% -> 0% of each run, Pallas kernels for 0% -> 21%
where the time goes in v2:
time: 75.8 us; the launch traced here: 75.7 us
  starting transfers between devices  36.3 us (48%)
  waiting for transfers between devices  21.9 us (29%)
  Pallas kernels  15.8 us (21%)
  other arithmetic  0.84 us (1%)
  between operations  0.82 us (1%)
    ppermute x9, starting transfers between devices, swap_rep(): return lax.ppermute(value, 'rep', [(r, r ^ mask) for r in range(N_REP)])  20.1 us
    pallas_call x12, Pallas kernels, call(): pl.pallas_call(kernel, out_shape=tuple((jax.ShapeDtypeStruct(*out) for ou...  15.8 us
    ppermute x9, waiting for transfers between devices, swap_rep(): return lax.ppermute(value, 'rep', [(r, r ^ mask) for r in range(N_REP)])  15.2 us
    ppermute x9, starting transfers between devices, shift_y(): lax.ppermute(value, 'fsdp', [(f, f & 4 | f + step & 3) for f in range(N_F...  9.17 us
    ppermute x2, starting transfers between devices, swap_z(): return lax.ppermute(value, 'fsdp', [(f, f ^ 4) for f in range(N_FSDP)])  7 us
    ppermute x9, waiting for transfers between devices, shift_y(): lax.ppermute(value, 'fsdp', [(f, f & 4 | f + step & 3) for f in range(N_F...  6.69 us
  transfers between devices with their start and end apart: 20, of which 7 were waited for; matrix products, arithmetic and copies ran while one was open for 0% of the time, Pallas kernels for 21%

profile of v2, /device:TPU:1, one launch (start us, length us, event | category | flops | bytes accessed | tf_op | source)
XLA Modules:
  0.0 75.7 jit_solution(10301702410974818195)
XLA Ops:
  0.6 3.6 %collective-permute-start.1 = (bf16[64,2048]{1,0:T(8,128)(2,1)}, bf16[64,2048]{1,0:T(8,128)(2,1)S(1)}, u32[]{:S(2)}, u32[]{:S(2)}) collective-permute-start(bf16[64,2048]{1,0:T(8,128)(2,1)} %own), channel_id=1, source_target_pairs={{0,3},{1,0},{2,1},{3,2},{4,7},{5,4},{6,5},{7,6},{8,11},{9,8},{10,9... | collective-permute-start | bytes 786440 | tf_op jit(solution)/shard_map/ppermute | solution.py:41
  4.3 6.9 %collective-permute-start.2 = (bf16[64,2048]{1,0:T(8,128)(2,1)}, bf16[64,2048]{1,0:T(8,128)(2,1)S(1)}, u32[]{:S(2)}, u32[]{:S(2)}) collective-permute-start(bf16[64,2048]{1,0:T(8,128)(2,1)} %own), channel_id=1, source_target_pairs={{0,4},{1,5},{2,6},{3,7},{4,0},{5,1},{6,2},{7,3},{8,12},{9,13},{10,... | collective-permute-start | bytes 786440 | tf_op jit(solution)/shard_map/ppermute | solution.py:37
  11.2 6.3 %begin.1 = (f32[4,4,32,256]{3,2,1,0:T(8,128)S(1)}, bf16[4,4,32,256]{3,2,1,0:T(8,128)(2,1)S(1)}, f32[32,256]{1,0:T(8,128)S(1)}, bf16[128,2048]{1,0:T(8,128)(2,1)S...) custom-call(s32[1]{0:T(128)} %bitcast.rep_ref, ...), custom_call_target="tpu_custom_call" | custom-call | tf_op jit(solution)/shard_map/begin/pallas_call | solution.py:47
  17.5 0.0 copy-start.3
  17.5 1.3 %collective-permute-start.3 = (bf16[4,4,32,256]{3,2,1,0:T(8,128)(2,1)S(1)}, bf16[4,4,32,256]{3,2,1,0:T(8,128)(2,1)S(1)}, u32[]{:S(2)}, u32[]{:S(2)}) collective-permute-start(bf16[4,4,32,256]{3,2,1,0:T(8,128)(2,1)S(1)} %get-tuple-element.43), channel_id=1, source_target_pairs={{0,8},{8,0},{16,24},{24,16},{32,40},{40,32},{48,56},{56,48},{64,72... | collective-permute-start | bytes 786440 | tf_op jit(solution)/shard_map/ppermute | solution.py:33
  18.8 0.1 pack.1
  18.9 3.0 %collective-permute-start.6 = (bf16[96,2048]{1,0:T(8,128)(2,1)S(1)}, bf16[96,2048]{1,0:T(8,128)(2,1)S(1)}, u32[]{:S(2)}, u32[]{:S(2)}) collective-permute-start(bf16[96,2048]{1,0:T(8,128)(2,1)S(1)} %get-tuple-element.49), channel_id=1, source_target_pairs={{0,3},{1,0},{2,1},{3,2},{4,7},{5,4},{6,5},{7,6},{8,11},{9,8},{10,9... | collective-permute-start | bytes 1179656 | tf_op jit(solution)/shard_map/ppermute | solution.py:41
  22.0 1.3 %collective-permute-start.4 = (bf16[2,4,32,256]{3,2,1,0:T(8,128)(2,1)S(1)}, bf16[2,4,32,256]{3,2,1,0:T(8,128)(2,1)S(1)}, u32[]{:S(2)}, u32[]{:S(2)}) collective-permute-start(bf16[2,4,32,256]{3,2,1,0:T(8,128)(2,1)S(1)} %get-tuple-element.46), channel_id=1, source_target_pairs={{0,16},{8,24},{16,0},{24,8},{32,48},{40,56},{48,32},{56,40},{64,80... | collective-permute-start | bytes 393224 | tf_op jit(solution)/shard_map/ppermute | solution.py:33
  23.3 3.6 %collective-permute-done.4.got = bf16[2,4,32,256]{3,2,1,0:T(8,128)(2,1)S(1)} collective-permute-done((bf16[2,4,32,256]{3,2,1,0:T(8,128)(2,1)S(1)}, bf16[2,4,32,256]{3,2,1,0:T(8,128)(2,1)S(1)}, u32[]{:S(2)}, u32[]{:S(2)}) %collective-permute-start.4) | collective-permute-done | bytes 131104 | tf_op jit(solution)/shard_map/ppermute | solution.py:33
  26.8 3.6 %collective-permute-done.6.from_above.far_above = bf16[96,2048]{1,0:T(8,128)(2,1)S(1)} collective-permute-done((bf16[96,2048]{1,0:T(8,128)(2,1)S(1)}, bf16[96,2048]{1,0:T(8,128)(2,1)S(1)}, u32[]{:S(2)}, u32[]{:S(2)}) %collective-permute-start.6) | collective-permute-done | bytes 393248 | tf_op jit(solution)/shard_map/ppermute | solution.py:41
  30.4 3.1 %collective-permute-done.5.from_below.far_below = bf16[96,2048]{1,0:T(8,128)(2,1)S(1)} collective-permute-done((bf16[96,2048]{1,0:T(8,128)(2,1)S(1)}, bf16[96,2048]{1,0:T(8,128)(2,1)S(1)}, u32[]{:S(2)}, u32[]{:S(2)}) %collective-permute-start.5) | collective-permute-done | bytes 393248 | tf_op jit(solution)/shard_map/ppermute | solution.py:41
  33.5 0.1 add.6
  33.7 0.4 collective-permute-start.15
  34.1 1.1 %collective-permute-start.14 = (bf16[128,2048]{1,0:T(8,128)(2,1)S(1)}, bf16[128,2048]{1,0:T(8,128)(2,1)S(1)}, u32[]{:S(2)}, u32[]{:S(2)}) collective-permute-start(bf16[128,2048]{1,0:T(8,128)(2,1)S(1)} %get-tuple-element.50), channel_id=1, source_target_pairs={{0,1},{1,2},{2,3},{3,0},{4,5},{5,6},{6,7},{7,4},{8,9},{9,10},{10,1... | collective-permute-start | bytes 1572872 | tf_op jit(solution)/shard_map/ppermute | solution.py:41
  35.2 2.6 %collective-permute-start.7 = (bf16[4,32,256]{2,1,0:T(8,128)(2,1)S(1)}, bf16[4,32,256]{2,1,0:T(8,128)(2,1)S(1)}, u32[]{:S(2)}, u32[]{:S(2)}) collective-permute-start(bf16[4,32,256]{2,1,0:T(8,128)(2,1)S(1)} %get-tuple-element.54), channel_id=1, source_target_pairs={{0,48},{8,56},{16,32},{24,40},{32,16},{40,24},{48,0},{56,8},{64,11... | collective-permute-start | bytes 196616 | tf_op jit(solution)/shard_map/ppermute | solution.py:33
  37.8 2.1 %collective-permute-done.7.got = bf16[4,32,256]{2,1,0:T(8,128)(2,1)S(1)} collective-permute-done((bf16[4,32,256]{2,1,0:T(8,128)(2,1)S(1)}, bf16[4,32,256]{2,1,0:T(8,128)(2,1)S(1)}, u32[]{:S(2)}, u32[]{:S(2)}) %collective-permute-start.7) | collective-permute-done | bytes 65568 | tf_op jit(solution)/shard_map/ppermute | solution.py:33
  40.0 0.8 %collective-permute-start.8 = (bf16[5,32,256]{2,1,0:T(8,128)(2,1)S(1)}, bf16[5,32,256]{2,1,0:T(8,128)(2,1)S(1)}, u32[]{:S(2)}, u32[]{:S(2)}) collective-permute-start(bf16[5,32,256]{2,1,0:T(8,128)(2,1)S(1)} %get-tuple-element.56), channel_id=1, source_target_pairs={{0,64},{8,72},{16,80},{24,88},{32,96},{40,104},{48,112},{56,120},{... | collective-permute-start | bytes 245768 | tf_op jit(solution)/shard_map/ppermute | solution.py:33
  40.8 2.8 %collective-permute-done.8.got.near = bf16[5,32,256]{2,1,0:T(8,128)(2,1)S(1)} collective-permute-done((bf16[5,32,256]{2,1,0:T(8,128)(2,1)S(1)}, bf16[5,32,256]{2,1,0:T(8,128)(2,1)S(1)}, u32[]{:S(2)}, u32[]{:S(2)}) %collective-permute-start.8) | collective-permute-done | bytes 81952 | tf_op jit(solution)/shard_map/ppermute | solution.py:33
  43.7 1.3 %collective-permute-start.9 = (bf16[6,32,256]{2,1,0:T(8,128)(2,1)S(1)}, bf16[6,32,256]{2,1,0:T(8,128)(2,1)S(1)}, u32[]{:S(2)}, u32[]{:S(2)}) collective-permute-start(bf16[6,32,256]{2,1,0:T(8,128)(2,1)S(1)} %get-tuple-element.58), channel_id=1, source_target_pairs={{0,128},{8,136},{16,144},{24,152},{32,160},{40,168},{48,176},{56,1... | collective-permute-start | bytes 294920 | tf_op jit(solution)/shard_map/ppermute | solution.py:33
  45.0 4.5 %collective-permute-done.9.far = bf16[6,32,256]{2,1,0:T(8,128)(2,1)S(1)} collective-permute-done((bf16[6,32,256]{2,1,0:T(8,128)(2,1)S(1)}, bf16[6,32,256]{2,1,0:T(8,128)(2,1)S(1)}, u32[]{:S(2)}, u32[]{:S(2)}) %collective-permute-start.9) | collective-permute-done | bytes 98336 | tf_op jit(solution)/shard_map/ppermute | solution.py:33
  49.5 0.7 update_step.1
  50.1 2.5 %collective-permute-start.10 = (bf16[4,32,256]{2,1,0:T(8,128)(2,1)S(1)}, bf16[4,32,256]{2,1,0:T(8,128)(2,1)S(1)}, u32[]{:S(2)}, u32[]{:S(2)}) collective-permute-start(bf16[4,32,256]{2,1,0:T(8,128)(2,1)S(1)} %get-tuple-element.62.first), channel_id=1, source_target_pairs={{0,48},{8,56},{16,32},{24,40},{32,16},{40,24},{48,0},{56,8},{64,11... | collective-permute-start | bytes 196616 | tf_op jit(solution)/shard_map/ppermute | solution.py:33
  52.6 2.1 %collective-permute-done.10.second = bf16[4,32,256]{2,1,0:T(8,128)(2,1)S(1)} collective-permute-done((bf16[4,32,256]{2,1,0:T(8,128)(2,1)S(1)}, bf16[4,32,256]{2,1,0:T(8,128)(2,1)S(1)}, u32[]{:S(2)}, u32[]{:S(2)}) %collective-permute-start.10) | collective-permute-done | bytes 65568 | tf_op jit(solution)/shard_map/ppermute | solution.py:33
  54.8 0.9 %collective-permute-start.17 = (bf16[64,2048]{1,0:T(8,128)(2,1)S(1)}, bf16[64,2048]{1,0:T(8,128)(2,1)S(1)}, u32[]{:S(2)}, u32[]{:S(2)}) collective-permute-start(bf16[64,2048]{1,0:T(8,128)(2,1)S(1)} %collective-permute-done.2.z_own), channel_id=1, source_target_pairs={{0,3},{1,0},{2,1},{3,2},{4,7},{5,4},{6,5},{7,6},{8,11},{9,8},{10,9... | collective-permute-start | bytes 786440 | tf_op jit(solution)/shard_map/ppermute | solution.py:41
  55.7 0.1 collective-permute-start.11
  55.8 0.2 fold.1
  56.1 0.1 collective-permute-start.16
  56.2 7.3 %collective-permute-start.12 = (bf16[2,4,32,256]{3,2,1,0:T(8,128)(2,1)S(1)}, bf16[2,4,32,256]{3,2,1,0:T(8,128)(2,1)S(1)}, u32[]{:S(2)}, u32[]{:S(2)}) collective-permute-start(bf16[2,4,32,256]{3,2,1,0:T(8,128)(2,1)S(1)} %join.1.own_near), channel_id=1, source_target_pairs={{0,8},{8,0},{16,24},{24,16},{32,40},{40,32},{48,56},{56,48},{64,72... | collective-permute-start | bytes 393224 | tf_op jit(solution)/shard_map/ppermute | solution.py:33
  63.5 2.9 %collective-permute-start.13 = (bf16[2,4,32,256]{3,2,1,0:T(8,128)(2,1)S(1)}, bf16[2,4,32,256]{3,2,1,0:T(8,128)(2,1)S(1)}, u32[]{:S(2)}, u32[]{:S(2)}) collective-permute-start(bf16[2,4,32,256]{3,2,1,0:T(8,128)(2,1)S(1)} %collective-permute-done.11.own_far), channel_id=1, source_target_pairs={{0,8},{8,0},{16,24},{24,16},{32,40},{40,32},{48,56},{56,48},{64,72... | collective-permute-start | bytes 393224 | tf_op jit(solution)/shard_map/ppermute | solution.py:33
  66.5 7.0 %gradients.1 = (bf16[1,1024,2048]{2,1,0:T(8,128)(2,1)}, f32[512,1024]{1,0:T(8,128)}) custom-call(s32[1]{0:T(128)} %bitcast.1.fsdp_ref, bf16[512,1024]{1,0:T(8,128)(2,1)} %tokens_hbm.3, bf16[1,1024,2048]{2,1,0:T(8,128)(2,1)} %weight_hbm.3, bf16[64,2048]{1,0:T(8,128)(2,1)S(1)} %copy-done.3, bf16[64,2048]{1,0:T(8,128)(2,1)S(1)} %collective-permute-done.1.above, ...), custom_call_target="tpu_custom_call" | custom-call | tf_op jit(solution)/shard_map/gradients/pallas_call | solution.py:47
  73.5 1.3 %mix.1 = f32[1,32,8192]{2,1,0:T(8,128)} custom-call(s32[1]{0:T(128)} %bitcast.rep_ref, f32[1,32,8192]{2,1,0:T(8,128)S(1)} %copy-done, f32[32,8192]{1,0:T(8,128)S(1)} %copy-done.1, bf16[2,4,32,256]{3,2,1,0:T(8,128)(2,1)S(1)} %join.1.own_near, bf16[2,4,32,256]{3,2,1,0:T(8,128)(2,1)S(1)} %collective-permute-done.11.own_far, ...), custom_call_target="tpu_custom_call" | custom-call | tf_op jit(solution)/shard_map/mix/pallas_call | solution.py:47
  74.9 0.8 %convert_add_fusion = f32[64,2048]{1,0:T(8,128)} fusion(f32[64,2048]{1,0:T(8,128)S(1)} %get-tuple-element.66, bf16[64,2048]{1,0:T(8,128)(2,1)S(1)} %collective-permute-done.16), kind=kLoop, calls=%fused_computation | loop fusion | flops 262144 | bytes 1310720 | tf_op jit(solution)/shard_map/add | solution.py:389
  (29 shorter events, 0.2 us)
Async XLA Ops:
  0.6 18.2 %collective-permute-start.1 = (bf16[64,2048]{1,0:T(8,128)(2,1)}, bf16[64,2048]{1,0:T(8,128)(2,1)S(1)}, u32[]{:S(2)}, u32[]{:S(2)}) collective-permute-start(bf16[64,2048]{1,0:T(8,128)(2,1)} %own), channel_id=1, source_target_pairs={{0,3},{1,0},{2,1},{3,2},{4,7},{5,4},{6,5},{7,6},{8,11},{9,8},{10,9... | collective-permute-start | bytes 786440 | tf_op jit(solution)/shard_map/ppermute | solution.py:41
  4.3 14.6 %collective-permute-start = (bf16[64,2048]{1,0:T(8,128)(2,1)}, bf16[64,2048]{1,0:T(8,128)(2,1)S(1)}, u32[]{:S(2)}, u32[]{:S(2)}) collective-permute-start(bf16[64,2048]{1,0:T(8,128)(2,1)} %own), channel_id=1, source_target_pairs={{0,1},{1,2},{2,3},{3,0},{4,5},{5,6},{6,7},{7,4},{8,9},{9,10},{10,1... | collective-permute-start | bytes 786440 | tf_op jit(solution)/shard_map/ppermute | solution.py:41
  4.3 17.6 %collective-permute-start.2 = (bf16[64,2048]{1,0:T(8,128)(2,1)}, bf16[64,2048]{1,0:T(8,128)(2,1)S(1)}, u32[]{:S(2)}, u32[]{:S(2)}) collective-permute-start(bf16[64,2048]{1,0:T(8,128)(2,1)} %own), channel_id=1, source_target_pairs={{0,4},{1,5},{2,6},{3,7},{4,0},{5,1},{6,2},{7,3},{8,12},{9,13},{10,... | collective-permute-start | bytes 786440 | tf_op jit(solution)/shard_map/ppermute | solution.py:37
  11.2 28.8 %copy-start.2 = (f32[32,256]{1,0:T(8,128)S(1)}, f32[32,256]{1,0:T(8,128)}, u32[]{:S(2)}) copy-start(f32[32,256]{1,0:T(8,128)} %momentum.5) | copy-start | bytes 98308
  17.5 49.0 %copy-start.3 = (bf16[64,2048]{1,0:T(8,128)(2,1)S(1)}, bf16[64,2048]{1,0:T(8,128)(2,1)}, u32[]{:S(2)}) copy-start(bf16[64,2048]{1,0:T(8,128)(2,1)} %own) | copy-start | bytes 786436
  17.5 4.4 %collective-permute-start.3 = (bf16[4,4,32,256]{3,2,1,0:T(8,128)(2,1)S(1)}, bf16[4,4,32,256]{3,2,1,0:T(8,128)(2,1)S(1)}, u32[]{:S(2)}, u32[]{:S(2)}) collective-permute-start(bf16[4,4,32,256]{3,2,1,0:T(8,128)(2,1)S(1)} %get-tuple-element.43), channel_id=1, source_target_pairs={{0,8},{8,0},{16,24},{24,16},{32,40},{40,32},{48,56},{56,48},{64,72... | collective-permute-start | bytes 786440 | tf_op jit(solution)/shard_map/ppermute | solution.py:33
  18.9 11.5 %collective-permute-start.6 = (bf16[96,2048]{1,0:T(8,128)(2,1)S(1)}, bf16[96,2048]{1,0:T(8,128)(2,1)S(1)}, u32[]{:S(2)}, u32[]{:S(2)}) collective-permute-start(bf16[96,2048]{1,0:T(8,128)(2,1)S(1)} %get-tuple-element.49), channel_id=1, source_target_pairs={{0,3},{1,0},{2,1},{3,2},{4,7},{5,4},{6,5},{7,6},{8,11},{9,8},{10,9... | collective-permute-start | bytes 1179656 | tf_op jit(solution)/shard_map/ppermute | solution.py:41
  21.9 11.6 %collective-permute-start.5 = (bf16[96,2048]{1,0:T(8,128)(2,1)S(1)}, bf16[96,2048]{1,0:T(8,128)(2,1)S(1)}, u32[]{:S(2)}, u32[]{:S(2)}) collective-permute-start(bf16[96,2048]{1,0:T(8,128)(2,1)S(1)} %get-tuple-element.41), channel_id=1, source_target_pairs={{0,1},{1,2},{2,3},{3,0},{4,5},{5,6},{6,7},{7,4},{8,9},{9,10},{10,1... | collective-permute-start | bytes 1179656 | tf_op jit(solution)/shard_map/ppermute | solution.py:41
  22.0 4.9 %collective-permute-start.4 = (bf16[2,4,32,256]{3,2,1,0:T(8,128)(2,1)S(1)}, bf16[2,4,32,256]{3,2,1,0:T(8,128)(2,1)S(1)}, u32[]{:S(2)}, u32[]{:S(2)}) collective-permute-start(bf16[2,4,32,256]{3,2,1,0:T(8,128)(2,1)S(1)} %get-tuple-element.46), channel_id=1, source_target_pairs={{0,16},{8,24},{16,0},{24,8},{32,48},{40,56},{48,32},{56,40},{64,80... | collective-permute-start | bytes 393224 | tf_op jit(solution)/shard_map/ppermute | solution.py:33
  33.7 22.1 %collective-permute-start.15 = (bf16[128,2048]{1,0:T(8,128)(2,1)S(1)}, bf16[128,2048]{1,0:T(8,128)(2,1)S(1)}, u32[]{:S(2)}, u32[]{:S(2)}) collective-permute-start(bf16[128,2048]{1,0:T(8,128)(2,1)S(1)} %get-tuple-element.65), channel_id=1, source_target_pairs={{0,3},{1,0},{2,1},{3,2},{4,7},{5,4},{6,5},{7,6},{8,11},{9,8},{10,9... | collective-permute-start | bytes 1572872 | tf_op jit(solution)/shard_map/ppermute | solution.py:41
  34.1 21.8 %collective-permute-start.14 = (bf16[128,2048]{1,0:T(8,128)(2,1)S(1)}, bf16[128,2048]{1,0:T(8,128)(2,1)S(1)}, u32[]{:S(2)}, u32[]{:S(2)}) collective-permute-start(bf16[128,2048]{1,0:T(8,128)(2,1)S(1)} %get-tuple-element.50), channel_id=1, source_target_pairs={{0,1},{1,2},{2,3},{3,0},{4,5},{5,6},{6,7},{7,4},{8,9},{9,10},{10,1... | collective-permute-start | bytes 1572872 | tf_op jit(solution)/shard_map/ppermute | solution.py:41
  35.2 4.7 %collective-permute-start.7 = (bf16[4,32,256]{2,1,0:T(8,128)(2,1)S(1)}, bf16[4,32,256]{2,1,0:T(8,128)(2,1)S(1)}, u32[]{:S(2)}, u32[]{:S(2)}) collective-permute-start(bf16[4,32,256]{2,1,0:T(8,128)(2,1)S(1)} %get-tuple-element.54), channel_id=1, source_target_pairs={{0,48},{8,56},{16,32},{24,40},{32,16},{40,24},{48,0},{56,8},{64,11... | collective-permute-start | bytes 196616 | tf_op jit(solution)/shard_map/ppermute | solution.py:33
  40.0 3.7 %collective-permute-start.8 = (bf16[5,32,256]{2,1,0:T(8,128)(2,1)S(1)}, bf16[5,32,256]{2,1,0:T(8,128)(2,1)S(1)}, u32[]{:S(2)}, u32[]{:S(2)}) collective-permute-start(bf16[5,32,256]{2,1,0:T(8,128)(2,1)S(1)} %get-tuple-element.56), channel_id=1, source_target_pairs={{0,64},{8,72},{16,80},{24,88},{32,96},{40,104},{48,112},{56,120},{... | collective-permute-start | bytes 245768 | tf_op jit(solution)/shard_map/ppermute | solution.py:33
  43.7 5.8 %collective-permute-start.9 = (bf16[6,32,256]{2,1,0:T(8,128)(2,1)S(1)}, bf16[6,32,256]{2,1,0:T(8,128)(2,1)S(1)}, u32[]{:S(2)}, u32[]{:S(2)}) collective-permute-start(bf16[6,32,256]{2,1,0:T(8,128)(2,1)S(1)} %get-tuple-element.58), channel_id=1, source_target_pairs={{0,128},{8,136},{16,144},{24,152},{32,160},{40,168},{48,176},{56,1... | collective-permute-start | bytes 294920 | tf_op jit(solution)/shard_map/ppermute | solution.py:33
  45.0 11.2 %collective-permute-start.19 = (bf16[64,2048]{1,0:T(8,128)(2,1)S(1)}, bf16[64,2048]{1,0:T(8,128)(2,1)S(1)}, u32[]{:S(2)}, u32[]{:S(2)}) collective-permute-start(bf16[64,2048]{1,0:T(8,128)(2,1)S(1)} %collective-permute-done.2.z_own), channel_id=1, source_target_pairs={{0,1},{1,2},{2,3},{3,0},{4,5},{5,6},{6,7},{7,4},{8,9},{9,10},{10,1... | collective-permute-start | bytes 786440 | tf_op jit(solution)/shard_map/ppermute | solution.py:41
  50.1 4.6 %collective-permute-start.10 = (bf16[4,32,256]{2,1,0:T(8,128)(2,1)S(1)}, bf16[4,32,256]{2,1,0:T(8,128)(2,1)S(1)}, u32[]{:S(2)}, u32[]{:S(2)}) collective-permute-start(bf16[4,32,256]{2,1,0:T(8,128)(2,1)S(1)} %get-tuple-element.62.first), channel_id=1, source_target_pairs={{0,48},{8,56},{16,32},{24,40},{32,16},{40,24},{48,0},{56,8},{64,11... | collective-permute-start | bytes 196616 | tf_op jit(solution)/shard_map/ppermute | solution.py:33
  52.6 13.8 %collective-permute-start.18 = (bf16[64,2048]{1,0:T(8,128)(2,1)S(1)}, bf16[64,2048]{1,0:T(8,128)(2,1)S(1)}, u32[]{:S(2)}, u32[]{:S(2)}) collective-permute-start(bf16[64,2048]{1,0:T(8,128)(2,1)S(1)} %collective-permute-done.2.z_own), channel_id=1, source_target_pairs={{0,2},{1,3},{2,0},{3,1},{4,6},{5,7},{6,4},{7,5},{8,10},{9,11},{10,... | collective-permute-start | bytes 786440 | tf_op jit(solution)/shard_map/ppermute | solution.py:41
  54.8 11.7 %collective-permute-start.17 = (bf16[64,2048]{1,0:T(8,128)(2,1)S(1)}, bf16[64,2048]{1,0:T(8,128)(2,1)S(1)}, u32[]{:S(2)}, u32[]{:S(2)}) collective-permute-start(bf16[64,2048]{1,0:T(8,128)(2,1)S(1)} %collective-permute-done.2.z_own), channel_id=1, source_target_pairs={{0,3},{1,0},{2,1},{3,2},{4,7},{5,4},{6,5},{7,6},{8,11},{9,8},{10,9... | collective-permute-start | bytes 786440 | tf_op jit(solution)/shard_map/ppermute | solution.py:41
  55.7 7.8 %collective-permute-start.11 = (bf16[2,4,32,256]{3,2,1,0:T(8,128)(2,1)S(1)}, bf16[2,4,32,256]{3,2,1,0:T(8,128)(2,1)S(1)}, u32[]{:S(2)}, u32[]{:S(2)}) collective-permute-start(bf16[2,4,32,256]{3,2,1,0:T(8,128)(2,1)S(1)} %join.1.own_near), channel_id=1, source_target_pairs={{0,16},{8,24},{16,0},{24,8},{32,48},{40,56},{48,32},{56,40},{64,80... | collective-permute-start | bytes 393224 | tf_op jit(solution)/shard_map/ppermute | solution.py:33
  56.0 17.5 %copy-start = (f32[1,32,8192]{2,1,0:T(8,128)S(1)}, f32[1,32,8192]{2,1,0:T(8,128)}, u32[]{:S(2)}) copy-start(f32[1,32,8192]{2,1,0:T(8,128)} %local_hbm.3) | copy-start | bytes 3145732
  56.1 17.5 %copy-start.1 = (f32[32,8192]{1,0:T(8,128)S(1)}, f32[32,8192]{1,0:T(8,128)}, u32[]{:S(2)}) copy-start(f32[32,8192]{1,0:T(8,128)} %global_hbm.3) | copy-start | bytes 3145732
  56.1 18.8 %collective-permute-start.16 = (bf16[64,2048]{1,0:T(8,128)(2,1)S(1)}, bf16[64,2048]{1,0:T(8,128)(2,1)S(1)}, u32[]{:S(2)}, u32[]{:S(2)}) collective-permute-start(bf16[64,2048]{1,0:T(8,128)(2,1)S(1)} %get-tuple-element.67), channel_id=1, source_target_pairs={{0,4},{1,5},{2,6},{3,7},{4,0},{5,1},{6,2},{7,3},{8,12},{9,13},{10,... | collective-permute-start | bytes 786440 | tf_op jit(solution)/shard_map/ppermute | solution.py:37
  56.2 17.3 %collective-permute-start.12 = (bf16[2,4,32,256]{3,2,1,0:T(8,128)(2,1)S(1)}, bf16[2,4,32,256]{3,2,1,0:T(8,128)(2,1)S(1)}, u32[]{:S(2)}, u32[]{:S(2)}) collective-permute-start(bf16[2,4,32,256]{3,2,1,0:T(8,128)(2,1)S(1)} %join.1.own_near), channel_id=1, source_target_pairs={{0,8},{8,0},{16,24},{24,16},{32,40},{40,32},{48,56},{56,48},{64,72... | collective-permute-start | bytes 393224 | tf_op jit(solution)/shard_map/ppermute | solution.py:33
  63.5 10.0 %collective-permute-start.13 = (bf16[2,4,32,256]{3,2,1,0:T(8,128)(2,1)S(1)}, bf16[2,4,32,256]{3,2,1,0:T(8,128)(2,1)S(1)}, u32[]{:S(2)}, u32[]{:S(2)}) collective-permute-start(bf16[2,4,32,256]{3,2,1,0:T(8,128)(2,1)S(1)} %collective-permute-done.11.own_far), channel_id=1, source_target_pairs={{0,8},{8,0},{16,24},{24,16},{32,40},{40,32},{48,56},{56,48},{64,72... | collective-permute-start | bytes 393224 | tf_op jit(solution)/shard_map/ppermute | solution.py:33

commit v3 on v2

--- a/solution.py
+++ b/solution.py
@@ -56,7 +56,7 @@
     )(*operands)
 
 
-BEGIN_MB, GRADIENTS_MB, MIX_MB = 51, 51, 51
+BEGIN_MB, NEAR_MB, GRADIENTS_MB, MIX_MB = 50, 6, 12, 6
 
 
 def column_of(rep, position, z_lo, core):
@@ -75,12 +75,12 @@
 
 def begin(
     rep_ref, fsdp_ref, local_hbm, global_hbm, tokens_hbm, weight_hbm,
-    keep, send, own_global, far, up, down, own,
-    local, globals_, ordered, weight, fragment_sems, token_sems, weight_sem,
+    keep, send, own_global, far, up, down, own, ordered,
+    local, globals_, weight, fragment_sems, token_sems, weight_sems,
 ):
     rep, fsdp = rep_ref[0], fsdp_ref[0]
     core = rep & 1
-    outs = ((2, far), (1, up), (3, down), (0, own))
+    outs = (own, up, far, down)
     fragment = []
     for part in range(2):
         at = pl.ds(part * 16, 16)
@@ -95,33 +95,42 @@
             )
         )
     token_copies = []
-    for i, (d, _) in enumerate(outs):
-        for z in range(2):
+    for z in range(2):
+        for d in range(4):
+            i = z * 4 + d
             token_copies.append(
                 pltpu.make_async_copy(
                     tokens_hbm.at[pl.ds(chunk_rows(fsdp, d, z), 64)],
-                    ordered.at[pl.ds(i * 128 + z * 64, 64)],
-                    token_sems.at[i * 2 + z],
+                    ordered.at[pl.ds(i * 64, 64)],
+                    token_sems.at[i],
                 )
             )
-    weight_copy = pltpu.make_async_copy(weight_hbm.at[0], weight, weight_sem)
-    for copy in token_copies:
+    weight_copies = [
+        pltpu.make_async_copy(
+            weight_hbm.at[0, :, pl.ds(half * 1024, 1024)],
+            weight.at[:, pl.ds(half * 1024, 1024)],
+            weight_sems.at[half],
+        )
+        for half in range(2)
+    ]
+    for copy in token_copies + weight_copies:
         copy.start()
-    weight_copy.start()
     for pair in fragment:
         for copy in pair:
             copy.start()
 
     for copy in token_copies:
         copy.wait()
-    weight_copy.wait()
     for tile in range(8):
+        if tile % 4 == 0:
+            weight_copies[tile // 4].wait()
         at = slice(tile * 256, tile * 256 + 256)
         partial = jnp.dot(ordered[...], weight[:, at], preferred_element_type=f32).astype(
             bf16
         )
-        for i, (_, out) in enumerate(outs):
-            out[:, at] = partial[i * 128 : i * 128 + 128]
+        for d, out in enumerate(outs):
+            out[:64, at] = partial[d * 64 : d * 64 + 64]
+            out[64:, at] = partial[256 + d * 64 : 256 + d * 64 + 64]
 
     def pseudo(rows, column):
         at = pl.ds(column, 128)
@@ -233,7 +242,7 @@
 
 
 def chunk_rows(fsdp, d, z):
-    return pl.multiple_of(z * 256 + ((fsdp + d) & 3) * 64, 64)
+    return pl.multiple_of(((fsdp >> 2) ^ z) * 256 + ((fsdp + d) & 3) * 64, 64)
 
 
 def pack(far, below, above, up, down):
@@ -250,65 +259,74 @@
     down_out[64:] = (down[64:].astype(f32) + from_above[:64].astype(f32)).astype(bf16)
 
 
-def fold(fsdp_ref, own, from_below, from_above, mine, theirs):
-    z_hi = fsdp_ref[0] >> 2
-
-    def total(z):
-        at = pl.ds(pl.multiple_of(z * 64, 64), 64)
-        return own[at].astype(f32) + from_below[at].astype(f32) + from_above[at].astype(f32)
-
-    mine[...] = total(z_hi)
-    theirs[...] = total(1 - z_hi).astype(bf16)
+def fold(own, from_below, from_above, mine, theirs):
+    total = own[...].astype(f32) + from_below[...].astype(f32) + from_above[...].astype(f32)
+    mine[...] = total[:64]
+    theirs[...] = total[64:].astype(bf16)
+
+
+def near_rows(rows, own, above, below, far_below, far_above):
+    for d, part in ((0, own), (1, above), (3, below)):
+        rows[d * 64 : d * 64 + 64] = part[...]
+    rows[128:160] = far_below[64:]
+    rows[160:192] = far_above[64:]
+
+
+def store_tokens(fsdp, source, grad_tokens_hbm, z, sems):
+    copies = []
+    for d in range(4):
+        copies.append(
+            pltpu.make_async_copy(
+                source.at[pl.ds(d * 64, 64)],
+                grad_tokens_hbm.at[pl.ds(chunk_rows(fsdp, d, z), 64)],
+                sems.at[d],
+            )
+        )
+        copies[-1].start()
+    return copies
+
+
+def near_gradients(
+    fsdp_ref, tokens, weight, own, above, below, far_below, far_above,
+    grad_tokens_hbm, turned, rows, tokens_near, sems,
+):
+    near_rows(rows, own, above, below, far_below, far_above)
+    for tile in range(4):
+        at = slice(tile * 256, tile * 256 + 256)
+        tokens_near[:, at] = lax.dot_general(
+            rows[...], weight[0, at], NT, preferred_element_type=f32
+        )
+    copies = store_tokens(fsdp_ref[0], tokens_near, grad_tokens_hbm, 0, sems)
+    turned[...] = tokens[...].T
+    for copy in copies:
+        copy.wait()
 
 
 def gradients(
-    fsdp_ref, tokens_hbm, weight_hbm, own, above, below, far_below, far_above,
+    fsdp_ref, turned, weight, _, own, above, below, far_below, far_above,
     z_own, z_above, z_far, z_below, grad_weight_hbm, grad_tokens_hbm,
-    rows, tokens, turned, weight, grad_weight, grad_tokens, in_sems, gx_sems, gw_sems,
+    rows, grad_weight, tokens_far, gw_sems, gx_sems,
 ):
-    fsdp = fsdp_ref[0]
-    z_hi = fsdp >> 2
-    token_copy = pltpu.make_async_copy(tokens_hbm, tokens, in_sems.at[0])
-    weight_copy = pltpu.make_async_copy(weight_hbm.at[0], weight, in_sems.at[1])
-    token_copy.start()
-    weight_copy.start()
-
-    for d, part in ((0, own), (1, above), (3, below)):
-        rows[pl.ds(chunk_rows(fsdp, d, z_hi), 64)] = part[...]
-    first = chunk_rows(fsdp, 2, z_hi)
-    rows[pl.ds(first, 32)] = far_below[64:]
-    rows[pl.ds(pl.multiple_of(first + 32, 32), 32)] = far_above[64:]
+    results = []
     for d, part in enumerate((z_own, z_above, z_far, z_below)):
-        rows[pl.ds(chunk_rows(fsdp, d, 1 - z_hi), 64)] = part[...]
-
-    token_copy.wait()
-    turned[...] = tokens[...].T
-    results = []
+        rows[256 + d * 64 : 256 + d * 64 + 64] = part[...]
+    near_rows(rows, own, above, below, far_below, far_above)
     for tile in range(4):
         at = slice(tile * 256, tile * 256 + 256)
         grad_weight[at] = jnp.dot(
             turned[at], rows[...], preferred_element_type=f32
         ).astype(bf16)
-        results.append(
-            pltpu.make_async_copy(
-                grad_weight.at[at], grad_weight_hbm.at[0, at], gw_sems.at[tile]
-            )
-        )
-        results[-1].start()
-    weight_copy.wait()
-    for tile in range(2):
+        copy = pltpu.make_async_copy(
+            grad_weight.at[at], grad_weight_hbm.at[0, at], gw_sems.at[tile]
+        )
+        copy.start()
+        results.append(copy)
+    for tile in range(4):
         at = slice(tile * 256, tile * 256 + 256)
-        for part in range(4):
-            to = slice(part * 256, part * 256 + 256)
-            grad_tokens[at, to] = lax.dot_general(
-                rows[at], weight[to], NT, preferred_element_type=f32
-            )
-        results.append(
-            pltpu.make_async_copy(
-                grad_tokens.at[at], grad_tokens_hbm.at[at], gx_sems.at[tile]
-            )
-        )
-        results[-1].start()
+        tokens_far[:, at] = lax.dot_general(
+            rows[256:], weight[0, at], NT, preferred_element_type=f32
+        )
+    results += store_tokens(fsdp_ref[0], tokens_far, grad_tokens_hbm, 1, gx_sems)
     for copy in results:
         copy.wait()
 
@@ -322,20 +340,20 @@
     z_own = swap_z(kv_cotangent)
     below = shift_y(kv_cotangent, 1)
     above = shift_y(kv_cotangent, -1)
-    keep, send, own_global, far, up, down, own = call(
+    keep, send, own_global, far, up, down, own, ordered = call(
         begin,
-        [((4, 4, *block), f32), ((4, 4, *block), bf16), (block, f32)] + [part] * 4,
+        [((4, 4, *block), f32), ((4, 4, *block), bf16), (block, f32)] + [part] * 4
+        + [((512, 1024), bf16)],
         (rep, fsdp, local_params, global_params, tokens, kv_weight),
         BEGIN_MB,
         in_specs=[SMEM] * 2 + [HBM] * 4,
         scratch_shapes=[
             pltpu.VMEM((ROWS, 8192), f32),
             pltpu.VMEM((ROWS, 8192), f32),
-            pltpu.VMEM((512, 1024), bf16),
             pltpu.VMEM((1024, 2048), bf16),
             pltpu.SemaphoreType.DMA((2, 2)),
             pltpu.SemaphoreType.DMA((8,)),
-            pltpu.SemaphoreType.DMA(()),
+            pltpu.SemaphoreType.DMA((2,)),
         ],
     )
     got_core = swap_rep(send, 1)
@@ -359,10 +377,23 @@
         (after(rest, up), got),
     )
     got = swap_rep(send, 6)
+    grad_near, turned = call(
+        near_gradients,
+        [((512, 1024), f32), ((1024, 512), bf16)],
+        (fsdp, ordered, kv_weight, after(kv_cotangent, send), above, below, from_below, from_above),
+        NEAR_MB,
+        in_specs=[SMEM] + [VMEM] * 7,
+        out_specs=(HBM, VMEM),
+        scratch_shapes=[
+            pltpu.VMEM((256, 2048), bf16),
+            pltpu.VMEM((256, 1024), f32),
+            pltpu.SemaphoreType.DMA((4,)),
+        ],
+    )
     rest, send = call(
         sum_x,
         [((4, *block), f32), ((5, *block), bf16)],
-        (after(rest, z_own), got, momentum),
+        (after(rest, turned), got, momentum),
     )
     near = swap_rep(send, 8)
     rest, send = call(
@@ -374,49 +405,48 @@
 
     z_own = after(z_own, near)
     z_pieces = (z_own, shift_y(z_own, -1), shift_y(z_own, 2), shift_y(z_own, 1))
+    mine, theirs = call(
+        fold,
+        [((64, 2048), f32), ((64, 2048), bf16)],
+        (after(own, z_far), sum_below, sum_above),
+    )
     new_global, new_momentum, update = call(
         update_step,
         [(block, f32), (block, f32), ((4, *block), bf16)],
-        (rep, rest, near, z_far, momentum, own_global),
+        (rep, after(rest, theirs), near, z_far, momentum, own_global),
         in_specs=[SMEM] + [VMEM] * 5,
     )
-    mine, theirs = call(
-        fold,
-        [((64, 2048), f32), ((64, 2048), bf16)],
-        (fsdp, after(own, update), sum_below, sum_above),
-        in_specs=[SMEM, VMEM, VMEM, VMEM],
-    )
     kv_out = mine + swap_z(theirs).astype(f32)
-    (first,) = call(join, [((2, 4, *block), bf16)], (update, swap_rep(update, 6)))
+    (first,) = call(join, [((2, 4, *block), bf16)], (after(update, *z_pieces), swap_rep(update, 6)))
     second = swap_rep(first, 2)
+    grad_weight, grad_tokens = call(
+        gradients,
+        [((1, 1024, 2048), bf16), ((512, 1024), f32)],
+        (fsdp, turned, kv_weight, grad_near, after(kv_cotangent, first),
+         above, below, from_below, from_above, *z_pieces),
+        GRADIENTS_MB,
+        in_specs=[SMEM, VMEM, VMEM, HBM] + [VMEM] * 9,
+        out_specs=(HBM, HBM),
+        input_output_aliases={3: 1},
+        scratch_shapes=[
+            pltpu.VMEM((512, 2048), bf16),
+            pltpu.VMEM((1024, 2048), bf16),
+            pltpu.VMEM((256, 1024), f32),
+            pltpu.SemaphoreType.DMA((4,)),
+            pltpu.SemaphoreType.DMA((4,)),
+        ],
+    )
+    other_first = swap_rep(after(first, grad_weight), 1)
+    other_second = swap_rep(after(second, grad_weight), 1)
     (mixed,) = call(
         mix,
         [(local_params.shape, f32)],
-        (rep, local_params, global_params, first, second, swap_rep(first, 1), swap_rep(second, 1)),
+        (rep, local_params, global_params, first, second, other_first, other_second),
         MIX_MB,
         in_specs=[SMEM, HBM, HBM] + [VMEM] * 4,
         out_specs=(HBM,),
         scratch_shapes=[pltpu.VMEM((ROWS, 8192), f32)] * 3
         + [pltpu.SemaphoreType.DMA((3, 4))],
-    )
-    grad_weight, grad_tokens = call(
-        gradients,
-        [((1, 1024, 2048), bf16), ((512, 1024), f32)],
-        (fsdp, tokens, kv_weight, after(kv_cotangent, first), above, below, from_below, from_above, *z_pieces),
-        GRADIENTS_MB,
-        in_specs=[SMEM, HBM, HBM] + [VMEM] * 9,
-        out_specs=(HBM, HBM),
-        scratch_shapes=[
-            pltpu.VMEM((512, 2048), bf16),
-            pltpu.VMEM((512, 1024), bf16),
-            pltpu.VMEM((1024, 512), bf16),
-            pltpu.VMEM((1024, 2048), bf16),
-            pltpu.VMEM((1024, 2048), bf16),
-            pltpu.VMEM((512, 1024), f32),
-            pltpu.SemaphoreType.DMA((2,)),
-            pltpu.SemaphoreType.DMA((2,)),
-            pltpu.SemaphoreType.DMA((4,)),
-        ],
     )
     return new_global, new_momentum, mixed, kv_out, grad_weight, grad_tokens
 

time: 75.8 us -> 70 us (0.923)
  the two profiles are of different devices: /device:TPU:1 before, /device:TPU:253 now
where the time goes in v3:
time: 70 us; the launch traced here: 69.9 us
  starting transfers between devices  32.9 us (47%)
  waiting for transfers between devices  20.1 us (29%)
  Pallas kernels  15.2 us (22%)
  between operations  0.9 us (1%)
  other arithmetic  0.85 us (1%)
    ppermute x9, starting transfers between devices, swap_rep(): return lax.ppermute(value, 'rep', [(r, r ^ mask) for r in range(N_REP)])  17.9 us
    pallas_call x13, Pallas kernels, call(): pl.pallas_call(kernel, out_shape=tuple((jax.ShapeDtypeStruct(*out) for ou...  15.2 us
    ppermute x9, waiting for transfers between devices, swap_rep(): return lax.ppermute(value, 'rep', [(r, r ^ mask) for r in range(N_REP)])  12 us
    ppermute x9, starting transfers between devices, shift_y(): lax.ppermute(value, 'fsdp', [(f, f & 4 | f + step & 3) for f in range(N_F...  9.23 us
    ppermute x2, starting transfers between devices, swap_z(): return lax.ppermute(value, 'fsdp', [(f, f ^ 4) for f in range(N_FSDP)])  5.74 us
    ppermute x2, waiting for transfers between devices, swap_z(): return lax.ppermute(value, 'fsdp', [(f, f ^ 4) for f in range(N_FSDP)])  4.27 us
    ppermute x9, waiting for transfers between devices, shift_y(): lax.ppermute(value, 'fsdp', [(f, f & 4 | f + step & 3) for f in range(N_F...  3.77 us
  transfers between devices with their start and end apart: 20, of which 10 were waited for; matrix products, arithmetic and copies ran while one was open for 1% of the time, Pallas kernels for 20%

profile of v3, /device:TPU:253, one launch (start us, length us, event | category | flops | bytes accessed | tf_op | source)
XLA Modules:
  0.0 69.9 jit_solution(3212255234949349039)
XLA Ops:
  0.7 1.5 %collective-permute-start.1 = (bf16[64,2048]{1,0:T(8,128)(2,1)}, bf16[64,2048]{1,0:T(8,128)(2,1)S(1)}, u32[]{:S(2)}, u32[]{:S(2)}) collective-permute-start(bf16[64,2048]{1,0:T(8,128)(2,1)} %own.1), channel_id=1, source_target_pairs={{0,3},{1,0},{2,1},{3,2},{4,7},{5,4},{6,5},{7,6},{8,11},{9,8},{10,9... | collective-permute-start | bytes 786440 | tf_op jit(solution)/shard_map/ppermute | solution.py:41
  2.2 1.2 %collective-permute-start.2 = (bf16[64,2048]{1,0:T(8,128)(2,1)}, bf16[64,2048]{1,0:T(8,128)(2,1)S(1)}, u32[]{:S(2)}, u32[]{:S(2)}) collective-permute-start(bf16[64,2048]{1,0:T(8,128)(2,1)} %own.1), channel_id=1, source_target_pairs={{0,4},{1,5},{2,6},{3,7},{4,0},{5,1},{6,2},{7,3},{8,12},{9,13},{10,... | collective-permute-start | bytes 786440 | tf_op jit(solution)/shard_map/ppermute | solution.py:37
  3.3 5.9 %begin.1 = (f32[4,4,32,256]{3,2,1,0:T(8,128)S(1)}, bf16[4,4,32,256]{3,2,1,0:T(8,128)(2,1)S(1)}, f32[32,256]{1,0:T(8,128)S(1)}, bf16[128,2048]{1,0:T(8,128)(2,1)S...) custom-call(s32[1]{0:T(128)} %bitcast.rep_ref, ...), custom_call_target="tpu_custom_call" | custom-call | tf_op jit(solution)/shard_map/begin/pallas_call | solution.py:47
  9.3 1.6 %collective-permute-start.3 = (bf16[4,4,32,256]{3,2,1,0:T(8,128)(2,1)S(1)}, bf16[4,4,32,256]{3,2,1,0:T(8,128)(2,1)S(1)}, u32[]{:S(2)}, u32[]{:S(2)}) collective-permute-start(bf16[4,4,32,256]{3,2,1,0:T(8,128)(2,1)S(1)} %get-tuple-element.51), channel_id=1, source_target_pairs={{0,8},{8,0},{16,24},{24,16},{32,40},{40,32},{48,56},{56,48},{64,72... | collective-permute-start | bytes 786440 | tf_op jit(solution)/shard_map/ppermute | solution.py:33
  10.9 1.2 %collective-permute-start.5 = (bf16[96,2048]{1,0:T(8,128)(2,1)S(1)}, bf16[96,2048]{1,0:T(8,128)(2,1)S(1)}, u32[]{:S(2)}, u32[]{:S(2)}) collective-permute-start(bf16[96,2048]{1,0:T(8,128)(2,1)S(1)} %get-tuple-element.49), channel_id=1, source_target_pairs={{0,1},{1,2},{2,3},{3,0},{4,5},{5,6},{6,7},{7,4},{8,9},{9,10},{10,1... | collective-permute-start | bytes 1179656 | tf_op jit(solution)/shard_map/ppermute | solution.py:41
  12.2 0.3 collective-permute-start.6
  12.5 4.3 %collective-permute-done.2.z_own = bf16[64,2048]{1,0:T(8,128)(2,1)S(1)} collective-permute-done((bf16[64,2048]{1,0:T(8,128)(2,1)}, bf16[64,2048]{1,0:T(8,128)(2,1)S(1)}, u32[]{:S(2)}, u32[]{:S(2)}) %collective-permute-start.2) | collective-permute-done | bytes 262176 | tf_op jit(solution)/shard_map/ppermute | solution.py:37
  16.8 1.0 %collective-permute-start.4 = (bf16[2,4,32,256]{3,2,1,0:T(8,128)(2,1)S(1)}, bf16[2,4,32,256]{3,2,1,0:T(8,128)(2,1)S(1)}, u32[]{:S(2)}, u32[]{:S(2)}) collective-permute-start(bf16[2,4,32,256]{3,2,1,0:T(8,128)(2,1)S(1)} %get-tuple-element.54), channel_id=1, source_target_pairs={{0,16},{8,24},{16,0},{24,8},{32,48},{40,56},{48,32},{56,40},{64,80... | collective-permute-start | bytes 393224 | tf_op jit(solution)/shard_map/ppermute | solution.py:33
  17.8 3.2 %collective-permute-done.4.got = bf16[2,4,32,256]{3,2,1,0:T(8,128)(2,1)S(1)} collective-permute-done((bf16[2,4,32,256]{3,2,1,0:T(8,128)(2,1)S(1)}, bf16[2,4,32,256]{3,2,1,0:T(8,128)(2,1)S(1)}, u32[]{:S(2)}, u32[]{:S(2)}) %collective-permute-start.4) | collective-permute-done | bytes 131104 | tf_op jit(solution)/shard_map/ppermute | solution.py:33
  21.0 0.7 collective-permute-done.5.from_below.far_below
  21.7 2.1 %collective-permute-done.6.from_above.far_above = bf16[96,2048]{1,0:T(8,128)(2,1)S(1)} collective-permute-done((bf16[96,2048]{1,0:T(8,128)(2,1)S(1)}, bf16[96,2048]{1,0:T(8,128)(2,1)S(1)}, u32[]{:S(2)}, u32[]{:S(2)}) %collective-permute-start.6) | collective-permute-done | bytes 393248 | tf_op jit(solution)/shard_map/ppermute | solution.py:41
  23.9 0.4 collective-permute-start.10
  24.3 1.1 %collective-permute-start.11 = (bf16[128,2048]{1,0:T(8,128)(2,1)S(1)}, bf16[128,2048]{1,0:T(8,128)(2,1)S(1)}, u32[]{:S(2)}, u32[]{:S(2)}) collective-permute-start(bf16[128,2048]{1,0:T(8,128)(2,1)S(1)} %get-tuple-element.72), channel_id=1, source_target_pairs={{0,3},{1,0},{2,1},{3,2},{4,7},{5,4},{6,5},{7,6},{8,11},{9,8},{10,9... | collective-permute-start | bytes 1572872 | tf_op jit(solution)/shard_map/ppermute | solution.py:41
  25.5 0.3 collective-permute-start.7
  25.8 2.3 %near_gradients.1 = (f32[512,1024]{1,0:T(8,128)}, bf16[1024,512]{1,0:T(8,128)(2,1)S(1)}) custom-call(s32[1]{0:T(128)} %bitcast.1.fsdp_ref, bf16[512,1024]{1,0:T(8,128)(2,1)S(1)} %get-tuple-element.61.tokens, bf16[1,1024,2048]{2,1,0:T(8,128)(2,1)S(1)} %copy-done, bf16[64,2048]{1,0:T(8,128)(2,1)S(1)} %copy-done.3, ...), custom_call_target="tpu_custom_call" | custom-call | tf_op jit(solution)/shard_map/near_gradients/pallas_call | solution.py:47
  28.1 0.8 %collective-permute-done.7.got = bf16[4,32,256]{2,1,0:T(8,128)(2,1)S(1)} collective-permute-done((bf16[4,32,256]{2,1,0:T(8,128)(2,1)S(1)}, bf16[4,32,256]{2,1,0:T(8,128)(2,1)S(1)}, u32[]{:S(2)}, u32[]{:S(2)}) %collective-permute-start.7) | collective-permute-done | bytes 65568 | tf_op jit(solution)/shard_map/ppermute | solution.py:33
  29.2 3.5 %collective-permute-done.8.got.near = bf16[5,32,256]{2,1,0:T(8,128)(2,1)S(1)} collective-permute-done((bf16[5,32,256]{2,1,0:T(8,128)(2,1)S(1)}, bf16[5,32,256]{2,1,0:T(8,128)(2,1)S(1)}, u32[]{:S(2)}, u32[]{:S(2)}) %collective-permute-start.8) | collective-permute-done | bytes 81952 | tf_op jit(solution)/shard_map/ppermute | solution.py:33
  32.8 0.3 collective-permute-start.12
  33.1 3.2 %collective-permute-start.13 = (bf16[64,2048]{1,0:T(8,128)(2,1)S(1)}, bf16[64,2048]{1,0:T(8,128)(2,1)S(1)}, u32[]{:S(2)}, u32[]{:S(2)}) collective-permute-start(bf16[64,2048]{1,0:T(8,128)(2,1)S(1)} %collective-permute-done.2.z_own), channel_id=1, source_target_pairs={{0,2},{1,3},{2,0},{3,1},{4,6},{5,7},{6,4},{7,5},{8,10},{9,11},{10,... | collective-permute-start | bytes 786440 | tf_op jit(solution)/shard_map/ppermute | solution.py:41
  36.3 2.0 %collective-permute-done.9.far = bf16[6,32,256]{2,1,0:T(8,128)(2,1)S(1)} collective-permute-done((bf16[6,32,256]{2,1,0:T(8,128)(2,1)S(1)}, bf16[6,32,256]{2,1,0:T(8,128)(2,1)S(1)}, u32[]{:S(2)}, u32[]{:S(2)}) %collective-permute-start.9) | collective-permute-done | bytes 98336 | tf_op jit(solution)/shard_map/ppermute | solution.py:33
  38.3 1.2 %collective-permute-start.14 = (bf16[64,2048]{1,0:T(8,128)(2,1)S(1)}, bf16[64,2048]{1,0:T(8,128)(2,1)S(1)}, u32[]{:S(2)}, u32[]{:S(2)}) collective-permute-start(bf16[64,2048]{1,0:T(8,128)(2,1)S(1)} %collective-permute-done.2.z_own), channel_id=1, source_target_pairs={{0,1},{1,2},{2,3},{3,0},{4,5},{5,6},{6,7},{7,4},{8,9},{9,10},{10,1... | collective-permute-start | bytes 786440 | tf_op jit(solution)/shard_map/ppermute | solution.py:41
  39.7 4.6 %collective-permute-start.19 = (bf16[64,2048]{1,0:T(8,128)(2,1)S(1)}, bf16[64,2048]{1,0:T(8,128)(2,1)S(1)}, u32[]{:S(2)}, u32[]{:S(2)}) collective-permute-start(bf16[64,2048]{1,0:T(8,128)(2,1)S(1)} %get-tuple-element.73), channel_id=1, source_target_pairs={{0,4},{1,5},{2,6},{3,7},{4,0},{5,1},{6,2},{7,3},{8,12},{9,13},{10,... | collective-permute-start | bytes 786440 | tf_op jit(solution)/shard_map/ppermute | solution.py:37
  44.2 0.7 update_step.1
  44.9 0.4 collective-permute-start.15
  45.3 1.0 %collective-permute-done.12.z_above = bf16[64,2048]{1,0:T(8,128)(2,1)S(1)} collective-permute-done((bf16[64,2048]{1,0:T(8,128)(2,1)S(1)}, bf16[64,2048]{1,0:T(8,128)(2,1)S(1)}, u32[]{:S(2)}, u32[]{:S(2)}) %collective-permute-start.12) | collective-permute-done | bytes 262176 | tf_op jit(solution)/shard_map/ppermute | solution.py:41
  46.3 2.0 %collective-permute-done.15.second = bf16[4,32,256]{2,1,0:T(8,128)(2,1)S(1)} collective-permute-done((bf16[4,32,256]{2,1,0:T(8,128)(2,1)S(1)}, bf16[4,32,256]{2,1,0:T(8,128)(2,1)S(1)}, u32[]{:S(2)}, u32[]{:S(2)}) %collective-permute-start.15) | collective-permute-done | bytes 65568 | tf_op jit(solution)/shard_map/ppermute | solution.py:33
  48.3 3.4 %collective-permute-start.16 = (bf16[2,4,32,256]{3,2,1,0:T(8,128)(2,1)S(1)}, bf16[2,4,32,256]{3,2,1,0:T(8,128)(2,1)S(1)}, u32[]{:S(2)}, u32[]{:S(2)}) collective-permute-start(bf16[2,4,32,256]{3,2,1,0:T(8,128)(2,1)S(1)} %join.1.own_near), channel_id=1, source_target_pairs={{0,16},{8,24},{16,0},{24,8},{32,48},{40,56},{48,32},{56,40},{64,80... | collective-permute-start | bytes 393224 | tf_op jit(solution)/shard_map/ppermute | solution.py:33
  51.8 4.5 %gradients.1 = (bf16[1,1024,2048]{2,1,0:T(8,128)(2,1)}, f32[512,1024]{1,0:T(8,128)}) custom-call(s32[1]{0:T(128)} %bitcast.1.fsdp_ref, bf16[1024,512]{1,0:T(8,128)(2,1)S(1)} %get-tuple-element.64.turned, bf16[1,1024,2048]{2,1,0:T(8,128)(2,1)S(1)} %copy-done, f32[512,1024]{1,0:T(8,128)} %get-tuple-element.81._, ...), custom_call_target="tpu_custom_call", output_to_operand_aliasing={{1}: (3, {})} | custom-call | tf_op jit(solution)/shard_map/gradients/pallas_call | solution.py:47
  56.3 10.8 %collective-permute-start.17 = (bf16[2,4,32,256]{3,2,1,0:T(8,128)(2,1)S(1)}, bf16[2,4,32,256]{3,2,1,0:T(8,128)(2,1)S(1)}, u32[]{:S(2)}, u32[]{:S(2)}) collective-permute-start(bf16[2,4,32,256]{3,2,1,0:T(8,128)(2,1)S(1)} %join.1.own_near), channel_id=1, source_target_pairs={{0,8},{8,0},{16,24},{24,16},{32,40},{40,32},{48,56},{56,48},{64,72... | collective-permute-start | bytes 393224 | tf_op jit(solution)/shard_map/ppermute | solution.py:33
  67.2 0.9 %convert_add_fusion = f32[64,2048]{1,0:T(8,128)} fusion(f32[64,2048]{1,0:T(8,128)S(1)} %get-tuple-element.86, bf16[64,2048]{1,0:T(8,128)(2,1)S(1)} %collective-permute-done.19), kind=kLoop, calls=%fused_computation | loop fusion | flops 262144 | bytes 1310720 | tf_op jit(solution)/shard_map/add | solution.py:419
  68.1 0.4 collective-permute-done.18.other_far
  68.5 1.3 %mix.1 = f32[1,32,8192]{2,1,0:T(8,128)} custom-call(s32[1]{0:T(128)} %bitcast.rep_ref, f32[1,32,8192]{2,1,0:T(8,128)S(1)} %copy-done.1, f32[32,8192]{1,0:T(8,128)S(1)} %copy-done.2, bf16[2,4,32,256]{3,2,1,0:T(8,128)(2,1)S(1)} %join.1.own_near, bf16[2,4,32,256]{3,2,1,0:T(8,128)(2,1)S(1)} %collective-permute-done.16.own_far, ...), custom_call_target="tpu_custom_call" | custom-call | tf_op jit(solution)/shard_map/mix/pallas_call | solution.py:47
  (32 shorter events, 1.0 us)
Async XLA Ops:
  0.6 10.2 %collective-permute-start = (bf16[64,2048]{1,0:T(8,128)(2,1)}, bf16[64,2048]{1,0:T(8,128)(2,1)S(1)}, u32[]{:S(2)}, u32[]{:S(2)}) collective-permute-start(bf16[64,2048]{1,0:T(8,128)(2,1)} %own.1), channel_id=1, source_target_pairs={{0,1},{1,2},{2,3},{3,0},{4,5},{5,6},{6,7},{7,4},{8,9},{9,10},{10,1... | collective-permute-start | bytes 786440 | tf_op jit(solution)/shard_map/ppermute | solution.py:41
  0.7 10.2 %collective-permute-start.1 = (bf16[64,2048]{1,0:T(8,128)(2,1)}, bf16[64,2048]{1,0:T(8,128)(2,1)S(1)}, u32[]{:S(2)}, u32[]{:S(2)}) collective-permute-start(bf16[64,2048]{1,0:T(8,128)(2,1)} %own.1), channel_id=1, source_target_pairs={{0,3},{1,0},{2,1},{3,2},{4,7},{5,4},{6,5},{7,6},{8,11},{9,8},{10,9... | collective-permute-start | bytes 786440 | tf_op jit(solution)/shard_map/ppermute | solution.py:41
  2.2 14.6 %collective-permute-start.2 = (bf16[64,2048]{1,0:T(8,128)(2,1)}, bf16[64,2048]{1,0:T(8,128)(2,1)S(1)}, u32[]{:S(2)}, u32[]{:S(2)}) collective-permute-start(bf16[64,2048]{1,0:T(8,128)(2,1)} %own.1), channel_id=1, source_target_pairs={{0,4},{1,5},{2,6},{3,7},{4,0},{5,1},{6,2},{7,3},{8,12},{9,13},{10,... | collective-permute-start | bytes 786440 | tf_op jit(solution)/shard_map/ppermute | solution.py:37
  3.3 22.5 %copy-start = (bf16[1,1024,2048]{2,1,0:T(8,128)(2,1)S(1)}, bf16[1,1024,2048]{2,1,0:T(8,128)(2,1)}, u32[]{:S(2)}) copy-start(bf16[1,1024,2048]{2,1,0:T(8,128)(2,1)} %weight.3) | copy-start | bytes 12582916
  3.3 22.5 %copy-start.3 = (bf16[64,2048]{1,0:T(8,128)(2,1)S(1)}, bf16[64,2048]{1,0:T(8,128)(2,1)}, u32[]{:S(2)}) copy-start(bf16[64,2048]{1,0:T(8,128)(2,1)} %own.1) | copy-start | bytes 786436
  9.3 7.5 %collective-permute-start.3 = (bf16[4,4,32,256]{3,2,1,0:T(8,128)(2,1)S(1)}, bf16[4,4,32,256]{3,2,1,0:T(8,128)(2,1)S(1)}, u32[]{:S(2)}, u32[]{:S(2)}) collective-permute-start(bf16[4,4,32,256]{3,2,1,0:T(8,128)(2,1)S(1)} %get-tuple-element.51), channel_id=1, source_target_pairs={{0,8},{8,0},{16,24},{24,16},{32,40},{40,32},{48,56},{56,48},{64,72... | collective-permute-start | bytes 786440 | tf_op jit(solution)/shard_map/ppermute | solution.py:33
  10.9 10.8 %collective-permute-start.5 = (bf16[96,2048]{1,0:T(8,128)(2,1)S(1)}, bf16[96,2048]{1,0:T(8,128)(2,1)S(1)}, u32[]{:S(2)}, u32[]{:S(2)}) collective-permute-start(bf16[96,2048]{1,0:T(8,128)(2,1)S(1)} %get-tuple-element.49), channel_id=1, source_target_pairs={{0,1},{1,2},{2,3},{3,0},{4,5},{5,6},{6,7},{7,4},{8,9},{9,10},{10,1... | collective-permute-start | bytes 1179656 | tf_op jit(solution)/shard_map/ppermute | solution.py:41
  12.2 11.6 %collective-permute-start.6 = (bf16[96,2048]{1,0:T(8,128)(2,1)S(1)}, bf16[96,2048]{1,0:T(8,128)(2,1)S(1)}, u32[]{:S(2)}, u32[]{:S(2)}) collective-permute-start(bf16[96,2048]{1,0:T(8,128)(2,1)S(1)} %get-tuple-element.57), channel_id=1, source_target_pairs={{0,3},{1,0},{2,1},{3,2},{4,7},{5,4},{6,5},{7,6},{8,11},{9,8},{10,9... | collective-permute-start | bytes 1179656 | tf_op jit(solution)/shard_map/ppermute | solution.py:41
  16.8 4.2 %collective-permute-start.4 = (bf16[2,4,32,256]{3,2,1,0:T(8,128)(2,1)S(1)}, bf16[2,4,32,256]{3,2,1,0:T(8,128)(2,1)S(1)}, u32[]{:S(2)}, u32[]{:S(2)}) collective-permute-start(bf16[2,4,32,256]{3,2,1,0:T(8,128)(2,1)S(1)} %get-tuple-element.54), channel_id=1, source_target_pairs={{0,16},{8,24},{16,0},{24,8},{32,48},{40,56},{48,32},{56,40},{64,80... | collective-permute-start | bytes 393224 | tf_op jit(solution)/shard_map/ppermute | solution.py:33
  23.8 5.2 %copy-start.4 = (f32[32,256]{1,0:T(8,128)S(1)}, f32[32,256]{1,0:T(8,128)}, u32[]{:S(2)}) copy-start(f32[32,256]{1,0:T(8,128)} %momentum.5) | copy-start | bytes 98308
  23.9 15.6 %collective-permute-start.10 = (bf16[128,2048]{1,0:T(8,128)(2,1)S(1)}, bf16[128,2048]{1,0:T(8,128)(2,1)S(1)}, u32[]{:S(2)}, u32[]{:S(2)}) collective-permute-start(bf16[128,2048]{1,0:T(8,128)(2,1)S(1)} %get-tuple-element.58), channel_id=1, source_target_pairs={{0,1},{1,2},{2,3},{3,0},{4,5},{5,6},{6,7},{7,4},{8,9},{9,10},{10,1... | collective-permute-start | bytes 1572872 | tf_op jit(solution)/shard_map/ppermute | solution.py:41
  24.3 15.2 %collective-permute-start.11 = (bf16[128,2048]{1,0:T(8,128)(2,1)S(1)}, bf16[128,2048]{1,0:T(8,128)(2,1)S(1)}, u32[]{:S(2)}, u32[]{:S(2)}) collective-permute-start(bf16[128,2048]{1,0:T(8,128)(2,1)S(1)} %get-tuple-element.72), channel_id=1, source_target_pairs={{0,3},{1,0},{2,1},{3,2},{4,7},{5,4},{6,5},{7,6},{8,11},{9,8},{10,9... | collective-permute-start | bytes 1572872 | tf_op jit(solution)/shard_map/ppermute | solution.py:41
  25.5 3.5 %collective-permute-start.7 = (bf16[4,32,256]{2,1,0:T(8,128)(2,1)S(1)}, bf16[4,32,256]{2,1,0:T(8,128)(2,1)S(1)}, u32[]{:S(2)}, u32[]{:S(2)}) collective-permute-start(bf16[4,32,256]{2,1,0:T(8,128)(2,1)S(1)} %get-tuple-element.62), channel_id=1, source_target_pairs={{0,48},{8,56},{16,32},{24,40},{32,16},{40,24},{48,0},{56,8},{64,11... | collective-permute-start | bytes 196616 | tf_op jit(solution)/shard_map/ppermute | solution.py:33
  29.0 3.7 %collective-permute-start.8 = (bf16[5,32,256]{2,1,0:T(8,128)(2,1)S(1)}, bf16[5,32,256]{2,1,0:T(8,128)(2,1)S(1)}, u32[]{:S(2)}, u32[]{:S(2)}) collective-permute-start(bf16[5,32,256]{2,1,0:T(8,128)(2,1)S(1)} %get-tuple-element.67), channel_id=1, source_target_pairs={{0,64},{8,72},{16,80},{24,88},{32,96},{40,104},{48,112},{56,120},{... | collective-permute-start | bytes 245768 | tf_op jit(solution)/shard_map/ppermute | solution.py:33
  32.7 5.6 %collective-permute-start.9 = (bf16[6,32,256]{2,1,0:T(8,128)(2,1)S(1)}, bf16[6,32,256]{2,1,0:T(8,128)(2,1)S(1)}, u32[]{:S(2)}, u32[]{:S(2)}) collective-permute-start(bf16[6,32,256]{2,1,0:T(8,128)(2,1)S(1)} %get-tuple-element.70), channel_id=1, source_target_pairs={{0,128},{8,136},{16,144},{24,152},{32,160},{40,168},{48,176},{56,1... | collective-permute-start | bytes 294920 | tf_op jit(solution)/shard_map/ppermute | solution.py:33
  32.8 13.5 %collective-permute-start.12 = (bf16[64,2048]{1,0:T(8,128)(2,1)S(1)}, bf16[64,2048]{1,0:T(8,128)(2,1)S(1)}, u32[]{:S(2)}, u32[]{:S(2)}) collective-permute-start(bf16[64,2048]{1,0:T(8,128)(2,1)S(1)} %collective-permute-done.2.z_own), channel_id=1, source_target_pairs={{0,3},{1,0},{2,1},{3,2},{4,7},{5,4},{6,5},{7,6},{8,11},{9,8},{10,9... | collective-permute-start | bytes 786440 | tf_op jit(solution)/shard_map/ppermute | solution.py:41
  33.1 13.2 %collective-permute-start.13 = (bf16[64,2048]{1,0:T(8,128)(2,1)S(1)}, bf16[64,2048]{1,0:T(8,128)(2,1)S(1)}, u32[]{:S(2)}, u32[]{:S(2)}) collective-permute-start(bf16[64,2048]{1,0:T(8,128)(2,1)S(1)} %collective-permute-done.2.z_own), channel_id=1, source_target_pairs={{0,2},{1,3},{2,0},{3,1},{4,6},{5,7},{6,4},{7,5},{8,10},{9,11},{10,... | collective-permute-start | bytes 786440 | tf_op jit(solution)/shard_map/ppermute | solution.py:41
  38.3 8.0 %collective-permute-start.14 = (bf16[64,2048]{1,0:T(8,128)(2,1)S(1)}, bf16[64,2048]{1,0:T(8,128)(2,1)S(1)}, u32[]{:S(2)}, u32[]{:S(2)}) collective-permute-start(bf16[64,2048]{1,0:T(8,128)(2,1)S(1)} %collective-permute-done.2.z_own), channel_id=1, source_target_pairs={{0,1},{1,2},{2,3},{3,0},{4,5},{5,6},{6,7},{7,4},{8,9},{9,10},{10,1... | collective-permute-start | bytes 786440 | tf_op jit(solution)/shard_map/ppermute | solution.py:41
  39.7 27.6 %collective-permute-start.19 = (bf16[64,2048]{1,0:T(8,128)(2,1)S(1)}, bf16[64,2048]{1,0:T(8,128)(2,1)S(1)}, u32[]{:S(2)}, u32[]{:S(2)}) collective-permute-start(bf16[64,2048]{1,0:T(8,128)(2,1)S(1)} %get-tuple-element.73), channel_id=1, source_target_pairs={{0,4},{1,5},{2,6},{3,7},{4,0},{5,1},{6,2},{7,3},{8,12},{9,13},{10,... | collective-permute-start | bytes 786440 | tf_op jit(solution)/shard_map/ppermute | solution.py:37
  44.9 3.4 %collective-permute-start.15 = (bf16[4,32,256]{2,1,0:T(8,128)(2,1)S(1)}, bf16[4,32,256]{2,1,0:T(8,128)(2,1)S(1)}, u32[]{:S(2)}, u32[]{:S(2)}) collective-permute-start(bf16[4,32,256]{2,1,0:T(8,128)(2,1)S(1)} %get-tuple-element.80.first), channel_id=1, source_target_pairs={{0,48},{8,56},{16,32},{24,40},{32,16},{40,24},{48,0},{56,8},{64,11... | collective-permute-start | bytes 196616 | tf_op jit(solution)/shard_map/ppermute | solution.py:33
  48.3 18.8 %collective-permute-start.16 = (bf16[2,4,32,256]{3,2,1,0:T(8,128)(2,1)S(1)}, bf16[2,4,32,256]{3,2,1,0:T(8,128)(2,1)S(1)}, u32[]{:S(2)}, u32[]{:S(2)}) collective-permute-start(bf16[2,4,32,256]{3,2,1,0:T(8,128)(2,1)S(1)} %join.1.own_near), channel_id=1, source_target_pairs={{0,16},{8,24},{16,0},{24,8},{32,48},{40,56},{48,32},{56,40},{64,80... | collective-permute-start | bytes 393224 | tf_op jit(solution)/shard_map/ppermute | solution.py:33
  51.7 16.7 %copy-start.1 = (f32[1,32,8192]{2,1,0:T(8,128)S(1)}, f32[1,32,8192]{2,1,0:T(8,128)}, u32[]{:S(2)}) copy-start(f32[1,32,8192]{2,1,0:T(8,128)} %local_hbm.3) | copy-start | bytes 3145732
  51.8 16.7 %copy-start.2 = (f32[32,8192]{1,0:T(8,128)S(1)}, f32[32,8192]{1,0:T(8,128)}, u32[]{:S(2)}) copy-start(f32[32,8192]{1,0:T(8,128)} %global_hbm.3) | copy-start | bytes 3145732
  56.3 11.8 %collective-permute-start.17 = (bf16[2,4,32,256]{3,2,1,0:T(8,128)(2,1)S(1)}, bf16[2,4,32,256]{3,2,1,0:T(8,128)(2,1)S(1)}, u32[]{:S(2)}, u32[]{:S(2)}) collective-permute-start(bf16[2,4,32,256]{3,2,1,0:T(8,128)(2,1)S(1)} %join.1.own_near), channel_id=1, source_target_pairs={{0,8},{8,0},{16,24},{24,16},{32,40},{40,32},{48,56},{56,48},{64,72... | collective-permute-start | bytes 393224 | tf_op jit(solution)/shard_map/ppermute | solution.py:33
  67.1 1.3 %collective-permute-start.18 = (bf16[2,4,32,256]{3,2,1,0:T(8,128)(2,1)S(1)}, bf16[2,4,32,256]{3,2,1,0:T(8,128)(2,1)S(1)}, u32[]{:S(2)}, u32[]{:S(2)}) collective-permute-start(bf16[2,4,32,256]{3,2,1,0:T(8,128)(2,1)S(1)} %collective-permute-done.16.own_far), channel_id=1, source_target_pairs={{0,8},{8,0},{16,24},{24,16},{32,40},{40,32},{48,56},{56,48},{64,72... | collective-permute-start | bytes 393224 | tf_op jit(solution)/shard_map/ppermute | solution.py:33

commit v4 on v3

--- a/solution.py
+++ b/solution.py
@@ -365,7 +365,7 @@
     rest, send = call(
         sum_core,
         [((2, 4, *block), f32), ((2, 4, *block), bf16)],
-        (after(keep, far_up, z_own), got_core),
+        (after(keep, far_up), got_core),
     )
     got = swap_rep(send, 2)
     up, down = call(add, [part] * 2, (after(up, got), down, from_below, from_above))
@@ -380,7 +380,7 @@
     grad_near, turned = call(
         near_gradients,
         [((512, 1024), f32), ((1024, 512), bf16)],
-        (fsdp, ordered, kv_weight, after(kv_cotangent, send), above, below, from_below, from_above),
+        (fsdp, ordered, kv_weight, after(kv_cotangent, send, z_own), above, below, from_below, from_above),
         NEAR_MB,
         in_specs=[SMEM] + [VMEM] * 7,
         out_specs=(HBM, VMEM),

time: 70 us -> 67.3 us (0.961)
  the two profiles are of different devices: /device:TPU:253 before, /device:TPU:1 now
where the time goes in v4:
time: 67.3 us; the launch traced here: 67 us
  starting transfers between devices  36.3 us (54%)
  Pallas kernels  15.2 us (23%)
  waiting for transfers between devices  13.7 us (20%)
  between operations  0.91 us (1%)
  other arithmetic  0.85 us (1%)
    ppermute x9, starting transfers between devices, swap_rep(): return lax.ppermute(value, 'rep', [(r, r ^ mask) for r in range(N_REP)])  16.1 us
    pallas_call x13, Pallas kernels, call(): pl.pallas_call(kernel, out_shape=tuple((jax.ShapeDtypeStruct(*out) for ou...  15.2 us
    ppermute x2, starting transfers between devices, swap_z(): return lax.ppermute(value, 'fsdp', [(f, f ^ 4) for f in range(N_FSDP)])  10.3 us
    ppermute x9, starting transfers between devices, shift_y(): lax.ppermute(value, 'fsdp', [(f, f & 4 | f + step & 3) for f in range(N_F...  9.99 us
    ppermute x9, waiting for transfers between devices, shift_y(): lax.ppermute(value, 'fsdp', [(f, f & 4 | f + step & 3) for f in range(N_F...  7.21 us
    ppermute x9, waiting for transfers between devices, swap_rep(): return lax.ppermute(value, 'rep', [(r, r ^ mask) for r in range(N_REP)])  6.49 us
  transfers between devices with their start and end apart: 20, of which 6 were waited for; matrix products, arithmetic and copies ran while one was open for 1% of the time, Pallas kernels for 21%

profile of v4, /device:TPU:1, one launch (start us, length us, event | category | flops | bytes accessed | tf_op | source)
XLA Modules:
  0.0 67.0 jit_solution(11322231541636659982)
XLA Ops:
  0.6 2.2 %collective-permute-start = (bf16[64,2048]{1,0:T(8,128)(2,1)}, bf16[64,2048]{1,0:T(8,128)(2,1)S(1)}, u32[]{:S(2)}, u32[]{:S(2)}) collective-permute-start(bf16[64,2048]{1,0:T(8,128)(2,1)} %own.1), channel_id=1, source_target_pairs={{0,1},{1,2},{2,3},{3,0},{4,5},{5,6},{6,7},{7,4},{8,9},{9,10},{10,1... | collective-permute-start | bytes 786440 | tf_op jit(solution)/shard_map/ppermute | solution.py:41
  2.8 1.5 %collective-permute-start.1 = (bf16[64,2048]{1,0:T(8,128)(2,1)}, bf16[64,2048]{1,0:T(8,128)(2,1)S(1)}, u32[]{:S(2)}, u32[]{:S(2)}) collective-permute-start(bf16[64,2048]{1,0:T(8,128)(2,1)} %own.1), channel_id=1, source_target_pairs={{0,3},{1,0},{2,1},{3,2},{4,7},{5,4},{6,5},{7,6},{8,11},{9,8},{10,9... | collective-permute-start | bytes 786440 | tf_op jit(solution)/shard_map/ppermute | solution.py:41
  4.4 5.9 %begin.1 = (f32[4,4,32,256]{3,2,1,0:T(8,128)S(1)}, bf16[4,4,32,256]{3,2,1,0:T(8,128)(2,1)S(1)}, f32[32,256]{1,0:T(8,128)S(1)}, bf16[128,2048]{1,0:T(8,128)(2,1)S...) custom-call(s32[1]{0:T(128)} %bitcast.rep_ref, ...), custom_call_target="tpu_custom_call" | custom-call | tf_op jit(solution)/shard_map/begin/pallas_call | solution.py:47
  10.3 2.9 %collective-permute-start.2 = (bf16[4,4,32,256]{3,2,1,0:T(8,128)(2,1)S(1)}, bf16[4,4,32,256]{3,2,1,0:T(8,128)(2,1)S(1)}, u32[]{:S(2)}, u32[]{:S(2)}) collective-permute-start(bf16[4,4,32,256]{3,2,1,0:T(8,128)(2,1)S(1)} %get-tuple-element.51), channel_id=1, source_target_pairs={{0,8},{8,0},{16,24},{24,16},{32,40},{40,32},{48,56},{56,48},{64,72... | collective-permute-start | bytes 786440 | tf_op jit(solution)/shard_map/ppermute | solution.py:33
  13.3 0.1 collective-permute-start.4
  13.4 2.7 %collective-permute-start.5 = (bf16[96,2048]{1,0:T(8,128)(2,1)S(1)}, bf16[96,2048]{1,0:T(8,128)(2,1)S(1)}, u32[]{:S(2)}, u32[]{:S(2)}) collective-permute-start(bf16[96,2048]{1,0:T(8,128)(2,1)S(1)} %get-tuple-element.57), channel_id=1, source_target_pairs={{0,3},{1,0},{2,1},{3,2},{4,7},{5,4},{6,5},{7,6},{8,11},{9,8},{10,9... | collective-permute-start | bytes 1179656 | tf_op jit(solution)/shard_map/ppermute | solution.py:41
  16.1 0.1 collective-permute-start.3
  16.2 6.4 %collective-permute-start.6 = (bf16[64,2048]{1,0:T(8,128)(2,1)S(1)}, bf16[64,2048]{1,0:T(8,128)(2,1)S(1)}, u32[]{:S(2)}, u32[]{:S(2)}) collective-permute-start(bf16[64,2048]{1,0:T(8,128)(2,1)S(1)} %copy-done.3), channel_id=1, source_target_pairs={{0,4},{1,5},{2,6},{3,7},{4,0},{5,1},{6,2},{7,3},{8,12},{9,13},{10,... | collective-permute-start | bytes 786440 | tf_op jit(solution)/shard_map/ppermute | solution.py:37
  22.6 2.7 %collective-permute-done.4.from_below.far_below = bf16[96,2048]{1,0:T(8,128)(2,1)S(1)} collective-permute-done((bf16[96,2048]{1,0:T(8,128)(2,1)S(1)}, bf16[96,2048]{1,0:T(8,128)(2,1)S(1)}, u32[]{:S(2)}, u32[]{:S(2)}) %collective-permute-start.4) | collective-permute-done | bytes 393248 | tf_op jit(solution)/shard_map/ppermute | solution.py:41
  25.3 0.1 add.6
  25.5 2.7 %collective-permute-start.11 = (bf16[128,2048]{1,0:T(8,128)(2,1)S(1)}, bf16[128,2048]{1,0:T(8,128)(2,1)S(1)}, u32[]{:S(2)}, u32[]{:S(2)}) collective-permute-start(bf16[128,2048]{1,0:T(8,128)(2,1)S(1)} %get-tuple-element.72), channel_id=1, source_target_pairs={{0,3},{1,0},{2,1},{3,2},{4,7},{5,4},{6,5},{7,6},{8,11},{9,8},{10,9... | collective-permute-start | bytes 1572872 | tf_op jit(solution)/shard_map/ppermute | solution.py:41
  28.2 0.5 collective-permute-start.7
  28.7 2.3 %near_gradients.1 = (f32[512,1024]{1,0:T(8,128)}, bf16[1024,512]{1,0:T(8,128)(2,1)S(1)}) custom-call(s32[1]{0:T(128)} %bitcast.1.fsdp_ref, bf16[512,1024]{1,0:T(8,128)(2,1)S(1)} %get-tuple-element.61.tokens, bf16[1,1024,2048]{2,1,0:T(8,128)(2,1)S(1)} %copy-done, bf16[64,2048]{1,0:T(8,128)(2,1)S(1)} %copy-done.3, ...), custom_call_target="tpu_custom_call" | custom-call | tf_op jit(solution)/shard_map/near_gradients/pallas_call | solution.py:47
  31.0 1.9 %collective-permute-done.7.got = bf16[4,32,256]{2,1,0:T(8,128)(2,1)S(1)} collective-permute-done((bf16[4,32,256]{2,1,0:T(8,128)(2,1)S(1)}, bf16[4,32,256]{2,1,0:T(8,128)(2,1)S(1)}, u32[]{:S(2)}, u32[]{:S(2)}) %collective-permute-start.7) | collective-permute-done | bytes 65568 | tf_op jit(solution)/shard_map/ppermute | solution.py:33
  32.9 3.9 %collective-permute-start.8 = (bf16[5,32,256]{2,1,0:T(8,128)(2,1)S(1)}, bf16[5,32,256]{2,1,0:T(8,128)(2,1)S(1)}, u32[]{:S(2)}, u32[]{:S(2)}) collective-permute-start(bf16[5,32,256]{2,1,0:T(8,128)(2,1)S(1)} %get-tuple-element.67), channel_id=1, source_target_pairs={{0,64},{8,72},{16,80},{24,88},{32,96},{40,104},{48,112},{56,120},{... | collective-permute-start | bytes 245768 | tf_op jit(solution)/shard_map/ppermute | solution.py:33
  36.8 2.1 %collective-permute-done.8.got.near = bf16[5,32,256]{2,1,0:T(8,128)(2,1)S(1)} collective-permute-done((bf16[5,32,256]{2,1,0:T(8,128)(2,1)S(1)}, bf16[5,32,256]{2,1,0:T(8,128)(2,1)S(1)}, u32[]{:S(2)}, u32[]{:S(2)}) %collective-permute-start.8) | collective-permute-done | bytes 81952 | tf_op jit(solution)/shard_map/ppermute | solution.py:33
  39.0 2.7 %collective-permute-start.9 = (bf16[6,32,256]{2,1,0:T(8,128)(2,1)S(1)}, bf16[6,32,256]{2,1,0:T(8,128)(2,1)S(1)}, u32[]{:S(2)}, u32[]{:S(2)}) collective-permute-start(bf16[6,32,256]{2,1,0:T(8,128)(2,1)S(1)} %get-tuple-element.70), channel_id=1, source_target_pairs={{0,128},{8,136},{16,144},{24,152},{32,160},{40,168},{48,176},{56,1... | collective-permute-start | bytes 294920 | tf_op jit(solution)/shard_map/ppermute | solution.py:33
  41.7 0.4 collective-permute-start.12
  42.1 0.4 collective-permute-start.13
  42.5 2.3 %collective-permute-done.9.far = bf16[6,32,256]{2,1,0:T(8,128)(2,1)S(1)} collective-permute-done((bf16[6,32,256]{2,1,0:T(8,128)(2,1)S(1)}, bf16[6,32,256]{2,1,0:T(8,128)(2,1)S(1)}, u32[]{:S(2)}, u32[]{:S(2)}) %collective-permute-start.9) | collective-permute-done | bytes 98336 | tf_op jit(solution)/shard_map/ppermute | solution.py:33
  44.8 0.2 fold.1
  45.0 3.9 %collective-permute-start.19 = (bf16[64,2048]{1,0:T(8,128)(2,1)S(1)}, bf16[64,2048]{1,0:T(8,128)(2,1)S(1)}, u32[]{:S(2)}, u32[]{:S(2)}) collective-permute-start(bf16[64,2048]{1,0:T(8,128)(2,1)S(1)} %get-tuple-element.73), channel_id=1, source_target_pairs={{0,4},{1,5},{2,6},{3,7},{4,0},{5,1},{6,2},{7,3},{8,12},{9,13},{10,... | collective-permute-start | bytes 786440 | tf_op jit(solution)/shard_map/ppermute | solution.py:37
  48.9 0.7 update_step.1
  49.6 1.8 %collective-permute-start.15 = (bf16[4,32,256]{2,1,0:T(8,128)(2,1)S(1)}, bf16[4,32,256]{2,1,0:T(8,128)(2,1)S(1)}, u32[]{:S(2)}, u32[]{:S(2)}) collective-permute-start(bf16[4,32,256]{2,1,0:T(8,128)(2,1)S(1)} %get-tuple-element.80.first), channel_id=1, source_target_pairs={{0,48},{8,56},{16,32},{24,40},{32,16},{40,24},{48,0},{56,8},{64,11... | collective-permute-start | bytes 196616 | tf_op jit(solution)/shard_map/ppermute | solution.py:33
  51.4 4.5 %collective-permute-done.14.z_below = bf16[64,2048]{1,0:T(8,128)(2,1)S(1)} collective-permute-done((bf16[64,2048]{1,0:T(8,128)(2,1)S(1)}, bf16[64,2048]{1,0:T(8,128)(2,1)S(1)}, u32[]{:S(2)}, u32[]{:S(2)}) %collective-permute-start.14) | collective-permute-done | bytes 262176 | tf_op jit(solution)/shard_map/ppermute | solution.py:41
  55.9 0.3 collective-permute-start.16
  56.2 4.5 %gradients.1 = (bf16[1,1024,2048]{2,1,0:T(8,128)(2,1)}, f32[512,1024]{1,0:T(8,128)}) custom-call(s32[1]{0:T(128)} %bitcast.1.fsdp_ref, bf16[1024,512]{1,0:T(8,128)(2,1)S(1)} %get-tuple-element.64.turned, bf16[1,1024,2048]{2,1,0:T(8,128)(2,1)S(1)} %copy-done, f32[512,1024]{1,0:T(8,128)} %get-tuple-element.81._, ...), custom_call_target="tpu_custom_call", output_to_operand_aliasing={{1}: (3, {})} | custom-call | tf_op jit(solution)/shard_map/gradients/pallas_call | solution.py:47
  60.8 3.4 %collective-permute-start.17 = (bf16[2,4,32,256]{3,2,1,0:T(8,128)(2,1)S(1)}, bf16[2,4,32,256]{3,2,1,0:T(8,128)(2,1)S(1)}, u32[]{:S(2)}, u32[]{:S(2)}) collective-permute-start(bf16[2,4,32,256]{3,2,1,0:T(8,128)(2,1)S(1)} %join.1.own_near), channel_id=1, source_target_pairs={{0,8},{8,0},{16,24},{24,16},{32,40},{40,32},{48,56},{56,48},{64,72... | collective-permute-start | bytes 393224 | tf_op jit(solution)/shard_map/ppermute | solution.py:33
  64.2 0.3 collective-permute-start.18
  64.5 0.9 %convert_add_fusion = f32[64,2048]{1,0:T(8,128)} fusion(f32[64,2048]{1,0:T(8,128)S(1)} %get-tuple-element.86, bf16[64,2048]{1,0:T(8,128)(2,1)S(1)} %collective-permute-done.19), kind=kLoop, calls=%fused_computation | loop fusion | flops 262144 | bytes 1310720 | tf_op jit(solution)/shard_map/add | solution.py:419
  65.4 0.2 collective-permute-done.18.other_far
  65.6 1.3 %mix.1 = f32[1,32,8192]{2,1,0:T(8,128)} custom-call(s32[1]{0:T(128)} %bitcast.rep_ref, f32[1,32,8192]{2,1,0:T(8,128)S(1)} %copy-done.1, f32[32,8192]{1,0:T(8,128)S(1)} %copy-done.2, bf16[2,4,32,256]{3,2,1,0:T(8,128)(2,1)S(1)} %join.1.own_near, bf16[2,4,32,256]{3,2,1,0:T(8,128)(2,1)S(1)} %collective-permute-done.16.own_far, ...), custom_call_target="tpu_custom_call" | custom-call | tf_op jit(solution)/shard_map/mix/pallas_call | solution.py:47
  (32 shorter events, 0.3 us)
Async XLA Ops:
  0.6 12.6 %collective-permute-start = (bf16[64,2048]{1,0:T(8,128)(2,1)}, bf16[64,2048]{1,0:T(8,128)(2,1)S(1)}, u32[]{:S(2)}, u32[]{:S(2)}) collective-permute-start(bf16[64,2048]{1,0:T(8,128)(2,1)} %own.1), channel_id=1, source_target_pairs={{0,1},{1,2},{2,3},{3,0},{4,5},{5,6},{6,7},{7,4},{8,9},{9,10},{10,1... | collective-permute-start | bytes 786440 | tf_op jit(solution)/shard_map/ppermute | solution.py:41
  2.8 10.4 %collective-permute-start.1 = (bf16[64,2048]{1,0:T(8,128)(2,1)}, bf16[64,2048]{1,0:T(8,128)(2,1)S(1)}, u32[]{:S(2)}, u32[]{:S(2)}) collective-permute-start(bf16[64,2048]{1,0:T(8,128)(2,1)} %own.1), channel_id=1, source_target_pairs={{0,3},{1,0},{2,1},{3,2},{4,7},{5,4},{6,5},{7,6},{8,11},{9,8},{10,9... | collective-permute-start | bytes 786440 | tf_op jit(solution)/shard_map/ppermute | solution.py:41
  4.4 11.8 %copy-start.3 = (bf16[64,2048]{1,0:T(8,128)(2,1)S(1)}, bf16[64,2048]{1,0:T(8,128)(2,1)}, u32[]{:S(2)}) copy-start(bf16[64,2048]{1,0:T(8,128)(2,1)} %own.1) | copy-start | bytes 786436
  4.4 24.4 %copy-start = (bf16[1,1024,2048]{2,1,0:T(8,128)(2,1)S(1)}, bf16[1,1024,2048]{2,1,0:T(8,128)(2,1)}, u32[]{:S(2)}) copy-start(bf16[1,1024,2048]{2,1,0:T(8,128)(2,1)} %weight.3) | copy-start | bytes 12582916
  10.3 5.7 %collective-permute-start.2 = (bf16[4,4,32,256]{3,2,1,0:T(8,128)(2,1)S(1)}, bf16[4,4,32,256]{3,2,1,0:T(8,128)(2,1)S(1)}, u32[]{:S(2)}, u32[]{:S(2)}) collective-permute-start(bf16[4,4,32,256]{3,2,1,0:T(8,128)(2,1)S(1)} %get-tuple-element.51), channel_id=1, source_target_pairs={{0,8},{8,0},{16,24},{24,16},{32,40},{40,32},{48,56},{56,48},{64,72... | collective-permute-start | bytes 786440 | tf_op jit(solution)/shard_map/ppermute | solution.py:33
  13.3 12.0 %collective-permute-start.4 = (bf16[96,2048]{1,0:T(8,128)(2,1)S(1)}, bf16[96,2048]{1,0:T(8,128)(2,1)S(1)}, u32[]{:S(2)}, u32[]{:S(2)}) collective-permute-start(bf16[96,2048]{1,0:T(8,128)(2,1)S(1)} %get-tuple-element.49), channel_id=1, source_target_pairs={{0,1},{1,2},{2,3},{3,0},{4,5},{5,6},{6,7},{7,4},{8,9},{9,10},{10,1... | collective-permute-start | bytes 1179656 | tf_op jit(solution)/shard_map/ppermute | solution.py:41
  13.4 11.9 %collective-permute-start.5 = (bf16[96,2048]{1,0:T(8,128)(2,1)S(1)}, bf16[96,2048]{1,0:T(8,128)(2,1)S(1)}, u32[]{:S(2)}, u32[]{:S(2)}) collective-permute-start(bf16[96,2048]{1,0:T(8,128)(2,1)S(1)} %get-tuple-element.57), channel_id=1, source_target_pairs={{0,3},{1,0},{2,1},{3,2},{4,7},{5,4},{6,5},{7,6},{8,11},{9,8},{10,9... | collective-permute-start | bytes 1179656 | tf_op jit(solution)/shard_map/ppermute | solution.py:41
  16.1 6.5 %collective-permute-start.3 = (bf16[2,4,32,256]{3,2,1,0:T(8,128)(2,1)S(1)}, bf16[2,4,32,256]{3,2,1,0:T(8,128)(2,1)S(1)}, u32[]{:S(2)}, u32[]{:S(2)}) collective-permute-start(bf16[2,4,32,256]{3,2,1,0:T(8,128)(2,1)S(1)} %get-tuple-element.54), channel_id=1, source_target_pairs={{0,16},{8,24},{16,0},{24,8},{32,48},{40,56},{48,32},{56,40},{64,80... | collective-permute-start | bytes 393224 | tf_op jit(solution)/shard_map/ppermute | solution.py:33
  16.2 12.6 %collective-permute-start.6 = (bf16[64,2048]{1,0:T(8,128)(2,1)S(1)}, bf16[64,2048]{1,0:T(8,128)(2,1)S(1)}, u32[]{:S(2)}, u32[]{:S(2)}) collective-permute-start(bf16[64,2048]{1,0:T(8,128)(2,1)S(1)} %copy-done.3), channel_id=1, source_target_pairs={{0,4},{1,5},{2,6},{3,7},{4,0},{5,1},{6,2},{7,3},{8,12},{9,13},{10,... | collective-permute-start | bytes 786440 | tf_op jit(solution)/shard_map/ppermute | solution.py:37
  25.3 7.6 %copy-start.4 = (f32[32,256]{1,0:T(8,128)S(1)}, f32[32,256]{1,0:T(8,128)}, u32[]{:S(2)}) copy-start(f32[32,256]{1,0:T(8,128)} %momentum.5) | copy-start | bytes 98308
  25.4 19.4 %collective-permute-start.10 = (bf16[128,2048]{1,0:T(8,128)(2,1)S(1)}, bf16[128,2048]{1,0:T(8,128)(2,1)S(1)}, u32[]{:S(2)}, u32[]{:S(2)}) collective-permute-start(bf16[128,2048]{1,0:T(8,128)(2,1)S(1)} %get-tuple-element.58), channel_id=1, source_target_pairs={{0,1},{1,2},{2,3},{3,0},{4,5},{5,6},{6,7},{7,4},{8,9},{9,10},{10,1... | collective-permute-start | bytes 1572872 | tf_op jit(solution)/shard_map/ppermute | solution.py:41
  25.5 19.3 %collective-permute-start.11 = (bf16[128,2048]{1,0:T(8,128)(2,1)S(1)}, bf16[128,2048]{1,0:T(8,128)(2,1)S(1)}, u32[]{:S(2)}, u32[]{:S(2)}) collective-permute-start(bf16[128,2048]{1,0:T(8,128)(2,1)S(1)} %get-tuple-element.72), channel_id=1, source_target_pairs={{0,3},{1,0},{2,1},{3,2},{4,7},{5,4},{6,5},{7,6},{8,11},{9,8},{10,9... | collective-permute-start | bytes 1572872 | tf_op jit(solution)/shard_map/ppermute | solution.py:41
  28.2 4.7 %collective-permute-start.7 = (bf16[4,32,256]{2,1,0:T(8,128)(2,1)S(1)}, bf16[4,32,256]{2,1,0:T(8,128)(2,1)S(1)}, u32[]{:S(2)}, u32[]{:S(2)}) collective-permute-start(bf16[4,32,256]{2,1,0:T(8,128)(2,1)S(1)} %get-tuple-element.62), channel_id=1, source_target_pairs={{0,48},{8,56},{16,32},{24,40},{32,16},{40,24},{48,0},{56,8},{64,11... | collective-permute-start | bytes 196616 | tf_op jit(solution)/shard_map/ppermute | solution.py:33
  32.9 6.0 %collective-permute-start.8 = (bf16[5,32,256]{2,1,0:T(8,128)(2,1)S(1)}, bf16[5,32,256]{2,1,0:T(8,128)(2,1)S(1)}, u32[]{:S(2)}, u32[]{:S(2)}) collective-permute-start(bf16[5,32,256]{2,1,0:T(8,128)(2,1)S(1)} %get-tuple-element.67), channel_id=1, source_target_pairs={{0,64},{8,72},{16,80},{24,88},{32,96},{40,104},{48,112},{56,120},{... | collective-permute-start | bytes 245768 | tf_op jit(solution)/shard_map/ppermute | solution.py:33
  39.0 5.8 %collective-permute-start.9 = (bf16[6,32,256]{2,1,0:T(8,128)(2,1)S(1)}, bf16[6,32,256]{2,1,0:T(8,128)(2,1)S(1)}, u32[]{:S(2)}, u32[]{:S(2)}) collective-permute-start(bf16[6,32,256]{2,1,0:T(8,128)(2,1)S(1)} %get-tuple-element.70), channel_id=1, source_target_pairs={{0,128},{8,136},{16,144},{24,152},{32,160},{40,168},{48,176},{56,1... | collective-permute-start | bytes 294920 | tf_op jit(solution)/shard_map/ppermute | solution.py:33
  41.7 9.7 %collective-permute-start.12 = (bf16[64,2048]{1,0:T(8,128)(2,1)S(1)}, bf16[64,2048]{1,0:T(8,128)(2,1)S(1)}, u32[]{:S(2)}, u32[]{:S(2)}) collective-permute-start(bf16[64,2048]{1,0:T(8,128)(2,1)S(1)} %collective-permute-done.6.z_own), channel_id=1, source_target_pairs={{0,3},{1,0},{2,1},{3,2},{4,7},{5,4},{6,5},{7,6},{8,11},{9,8},{10,9... | collective-permute-start | bytes 786440 | tf_op jit(solution)/shard_map/ppermute | solution.py:41
  42.1 9.2 %collective-permute-start.13 = (bf16[64,2048]{1,0:T(8,128)(2,1)S(1)}, bf16[64,2048]{1,0:T(8,128)(2,1)S(1)}, u32[]{:S(2)}, u32[]{:S(2)}) collective-permute-start(bf16[64,2048]{1,0:T(8,128)(2,1)S(1)} %collective-permute-done.6.z_own), channel_id=1, source_target_pairs={{0,2},{1,3},{2,0},{3,1},{4,6},{5,7},{6,4},{7,5},{8,10},{9,11},{10,... | collective-permute-start | bytes 786440 | tf_op jit(solution)/shard_map/ppermute | solution.py:41
  44.8 11.1 %collective-permute-start.14 = (bf16[64,2048]{1,0:T(8,128)(2,1)S(1)}, bf16[64,2048]{1,0:T(8,128)(2,1)S(1)}, u32[]{:S(2)}, u32[]{:S(2)}) collective-permute-start(bf16[64,2048]{1,0:T(8,128)(2,1)S(1)} %collective-permute-done.6.z_own), channel_id=1, source_target_pairs={{0,1},{1,2},{2,3},{3,0},{4,5},{5,6},{6,7},{7,4},{8,9},{9,10},{10,1... | collective-permute-start | bytes 786440 | tf_op jit(solution)/shard_map/ppermute | solution.py:41
  45.0 19.5 %collective-permute-start.19 = (bf16[64,2048]{1,0:T(8,128)(2,1)S(1)}, bf16[64,2048]{1,0:T(8,128)(2,1)S(1)}, u32[]{:S(2)}, u32[]{:S(2)}) collective-permute-start(bf16[64,2048]{1,0:T(8,128)(2,1)S(1)} %get-tuple-element.73), channel_id=1, source_target_pairs={{0,4},{1,5},{2,6},{3,7},{4,0},{5,1},{6,2},{7,3},{8,12},{9,13},{10,... | collective-permute-start | bytes 786440 | tf_op jit(solution)/shard_map/ppermute | solution.py:37
  49.6 6.3 %collective-permute-start.15 = (bf16[4,32,256]{2,1,0:T(8,128)(2,1)S(1)}, bf16[4,32,256]{2,1,0:T(8,128)(2,1)S(1)}, u32[]{:S(2)}, u32[]{:S(2)}) collective-permute-start(bf16[4,32,256]{2,1,0:T(8,128)(2,1)S(1)} %get-tuple-element.80.first), channel_id=1, source_target_pairs={{0,48},{8,56},{16,32},{24,40},{32,16},{40,24},{48,0},{56,8},{64,11... | collective-permute-start | bytes 196616 | tf_op jit(solution)/shard_map/ppermute | solution.py:33
  55.9 8.3 %collective-permute-start.16 = (bf16[2,4,32,256]{3,2,1,0:T(8,128)(2,1)S(1)}, bf16[2,4,32,256]{3,2,1,0:T(8,128)(2,1)S(1)}, u32[]{:S(2)}, u32[]{:S(2)}) collective-permute-start(bf16[2,4,32,256]{3,2,1,0:T(8,128)(2,1)S(1)} %join.1.own_near), channel_id=1, source_target_pairs={{0,16},{8,24},{16,0},{24,8},{32,48},{40,56},{48,32},{56,40},{64,80... | collective-permute-start | bytes 393224 | tf_op jit(solution)/shard_map/ppermute | solution.py:33
  56.2 9.3 %copy-start.1 = (f32[1,32,8192]{2,1,0:T(8,128)S(1)}, f32[1,32,8192]{2,1,0:T(8,128)}, u32[]{:S(2)}) copy-start(f32[1,32,8192]{2,1,0:T(8,128)} %local_hbm.3) | copy-start | bytes 3145732
  56.2 9.3 %copy-start.2 = (f32[32,8192]{1,0:T(8,128)S(1)}, f32[32,8192]{1,0:T(8,128)}, u32[]{:S(2)}) copy-start(f32[32,8192]{1,0:T(8,128)} %global_hbm.3) | copy-start | bytes 3145732
  60.8 4.6 %collective-permute-start.17 = (bf16[2,4,32,256]{3,2,1,0:T(8,128)(2,1)S(1)}, bf16[2,4,32,256]{3,2,1,0:T(8,128)(2,1)S(1)}, u32[]{:S(2)}, u32[]{:S(2)}) collective-permute-start(bf16[2,4,32,256]{3,2,1,0:T(8,128)(2,1)S(1)} %join.1.own_near), channel_id=1, source_target_pairs={{0,8},{8,0},{16,24},{24,16},{32,40},{40,32},{48,56},{56,48},{64,72... | collective-permute-start | bytes 393224 | tf_op jit(solution)/shard_map/ppermute | solution.py:33
  64.2 1.3 %collective-permute-start.18 = (bf16[2,4,32,256]{3,2,1,0:T(8,128)(2,1)S(1)}, bf16[2,4,32,256]{3,2,1,0:T(8,128)(2,1)S(1)}, u32[]{:S(2)}, u32[]{:S(2)}) collective-permute-start(bf16[2,4,32,256]{3,2,1,0:T(8,128)(2,1)S(1)} %collective-permute-done.16.own_far), channel_id=1, source_target_pairs={{0,8},{8,0},{16,24},{24,16},{32,40},{40,32},{48,56},{56,48},{64,72... | collective-permute-start | bytes 393224 | tf_op jit(solution)/shard_map/ppermute | solution.py:33

commit v5 on v4

--- a/solution.py
+++ b/solution.py
@@ -56,7 +56,7 @@
     )(*operands)
 
 
-BEGIN_MB, NEAR_MB, GRADIENTS_MB, MIX_MB = 50, 6, 12, 6
+BEGIN_MB, QUANTIZE_MB, NEAR_MB, GRADIENTS_MB, MIX_MB = 51, 50, 6, 12, 6
 
 
 def column_of(rep, position, z_lo, core):
@@ -73,27 +73,12 @@
     return (pseudo / scale).astype(bf16).astype(f32) * scale
 
 
-def begin(
-    rep_ref, fsdp_ref, local_hbm, global_hbm, tokens_hbm, weight_hbm,
-    keep, send, own_global, far, up, down, own, ordered,
-    local, globals_, weight, fragment_sems, token_sems, weight_sems,
-):
-    rep, fsdp = rep_ref[0], fsdp_ref[0]
-    core = rep & 1
+def project(
+    fsdp_ref, tokens_hbm, weight_hbm, far, up, down, own, ordered,
+    weight, token_sems, weight_sems,
+):
+    fsdp = fsdp_ref[0]
     outs = (own, up, far, down)
-    fragment = []
-    for part in range(2):
-        at = pl.ds(part * 16, 16)
-        fragment.append(
-            (
-                pltpu.make_async_copy(
-                    local_hbm.at[0, at], local.at[at], fragment_sems.at[0, part]
-                ),
-                pltpu.make_async_copy(
-                    global_hbm.at[at], globals_.at[at], fragment_sems.at[1, part]
-                ),
-            )
-        )
     token_copies = []
     for z in range(2):
         for d in range(4):
@@ -115,9 +100,6 @@
     ]
     for copy in token_copies + weight_copies:
         copy.start()
-    for pair in fragment:
-        for copy in pair:
-            copy.start()
 
     for copy in token_copies:
         copy.wait()
@@ -131,6 +113,29 @@
         for d, out in enumerate(outs):
             out[:64, at] = partial[d * 64 : d * 64 + 64]
             out[64:, at] = partial[256 + d * 64 : 256 + d * 64 + 64]
+
+
+def quantize(
+    rep_ref, local_hbm, global_hbm, keep, send, own_global, local, globals_, fragment_sems
+):
+    rep = rep_ref[0]
+    core = rep & 1
+    fragment = []
+    for part in range(2):
+        at = pl.ds(part * 16, 16)
+        fragment.append(
+            (
+                pltpu.make_async_copy(
+                    local_hbm.at[0, at], local.at[at], fragment_sems.at[0, part]
+                ),
+                pltpu.make_async_copy(
+                    global_hbm.at[at], globals_.at[at], fragment_sems.at[1, part]
+                ),
+            )
+        )
+    for pair in fragment:
+        for copy in pair:
+            copy.start()
 
     def pseudo(rows, column):
         at = pl.ds(column, 128)
@@ -313,6 +318,12 @@
     near_rows(rows, own, above, below, far_below, far_above)
     for tile in range(4):
         at = slice(tile * 256, tile * 256 + 256)
+        tokens_far[:, at] = lax.dot_general(
+            rows[256:], weight[0, at], NT, preferred_element_type=f32
+        )
+    results += store_tokens(fsdp_ref[0], tokens_far, grad_tokens_hbm, 1, gx_sems)
+    for tile in range(8):
+        at = slice(tile * 128, tile * 128 + 128)
         grad_weight[at] = jnp.dot(
             turned[at], rows[...], preferred_element_type=f32
         ).astype(bf16)
@@ -321,12 +332,6 @@
         )
         copy.start()
         results.append(copy)
-    for tile in range(4):
-        at = slice(tile * 256, tile * 256 + 256)
-        tokens_far[:, at] = lax.dot_general(
-            rows[256:], weight[0, at], NT, preferred_element_type=f32
-        )
-    results += store_tokens(fsdp_ref[0], tokens_far, grad_tokens_hbm, 1, gx_sems)
     for copy in results:
         copy.wait()
 
@@ -340,28 +345,36 @@
     z_own = swap_z(kv_cotangent)
     below = shift_y(kv_cotangent, 1)
     above = shift_y(kv_cotangent, -1)
-    keep, send, own_global, far, up, down, own, ordered = call(
-        begin,
-        [((4, 4, *block), f32), ((4, 4, *block), bf16), (block, f32)] + [part] * 4
-        + [((512, 1024), bf16)],
-        (rep, fsdp, local_params, global_params, tokens, kv_weight),
+    far, up, down, own, ordered = call(
+        project,
+        [part] * 4 + [((512, 1024), bf16)],
+        (fsdp, tokens, kv_weight),
         BEGIN_MB,
-        in_specs=[SMEM] * 2 + [HBM] * 4,
+        in_specs=[SMEM, HBM, HBM],
+        scratch_shapes=[
+            pltpu.VMEM((1024, 2048), bf16),
+            pltpu.SemaphoreType.DMA((8,)),
+            pltpu.SemaphoreType.DMA((2,)),
+        ],
+    )
+    far_up, far_down = call(pack, [((96, 2048), bf16)] * 2, (far, below, above))
+    from_below = shift_y(far_up, 1)
+    from_above = shift_y(far_down, -1)
+
+
+    keep, send, own_global = call(
+        quantize,
+        [((4, 4, *block), f32), ((4, 4, *block), bf16), (block, f32)],
+        (after(rep, far), local_params, global_params),
+        QUANTIZE_MB,
+        in_specs=[SMEM, HBM, HBM],
         scratch_shapes=[
             pltpu.VMEM((ROWS, 8192), f32),
             pltpu.VMEM((ROWS, 8192), f32),
-            pltpu.VMEM((1024, 2048), bf16),
             pltpu.SemaphoreType.DMA((2, 2)),
-            pltpu.SemaphoreType.DMA((8,)),
-            pltpu.SemaphoreType.DMA((2,)),
         ],
     )
     got_core = swap_rep(send, 1)
-    far_up, far_down = call(pack, [((96, 2048), bf16)] * 2, (far, below, above))
-    from_below = shift_y(far_up, 1)
-    from_above = shift_y(far_down, -1)
-
-
     rest, send = call(
         sum_core,
         [((2, 4, *block), f32), ((2, 4, *block), bf16)],
@@ -432,7 +445,7 @@
             pltpu.VMEM((512, 2048), bf16),
             pltpu.VMEM((1024, 2048), bf16),
             pltpu.VMEM((256, 1024), f32),
-            pltpu.SemaphoreType.DMA((4,)),
+            pltpu.SemaphoreType.DMA((8,)),
             pltpu.SemaphoreType.DMA((4,)),
         ],
     )

time: 67.3 us -> 67.9 us (level); the launches traced: 67 us -> 66.9 us
    ppermute x9, starting transfers between devices: 16.1 us -> 15 us  [swap_rep(): return lax.ppermute(value, 'rep', [(r, r ^ mask) for r in range(N_REP)])]
    ppermute x2, starting transfers between devices: 10.3 us -> 11.3 us  [swap_z(): return lax.ppermute(value, 'fsdp', [(f, f ^ 4) for f in range(N_FSDP)])]
    ppermute x9, waiting for transfers between devices: 7.21 us -> 6.29 us  [shift_y(): lax.ppermute(value, 'fsdp', [(f, f & 4 | f + step & 3) for f in range(N_F...]
    ppermute x9, waiting for transfers between devices: 6.49 us -> 7.3 us  [swap_rep(): return lax.ppermute(value, 'rep', [(r, r ^ mask) for r in range(N_REP)])]
    pallas_call x13 -> x14, Pallas kernels: 15.2 us -> 15 us  [call(): pl.pallas_call(kernel, out_shape=tuple((jax.ShapeDtypeStruct(*out) for ou...]
  transfers between devices with their start and end apart: 20 -> 20, of which waited for: 6 -> 6; matrix products, arithmetic and copies ran while one was open for 1% -> 1% of each run, Pallas kernels for 21% -> 20%
where the time goes in v5:
time: 67.9 us; the launch traced here: 66.9 us
  starting transfers between devices  36.5 us (54%)
  Pallas kernels  15 us (22%)
  waiting for transfers between devices  13.6 us (20%)
  between operations  0.97 us (1%)
  other arithmetic  0.84 us (1%)
    ppermute x9, starting transfers between devices, swap_rep(): return lax.ppermute(value, 'rep', [(r, r ^ mask) for r in range(N_REP)])  15 us
    pallas_call x14, Pallas kernels, call(): pl.pallas_call(kernel, out_shape=tuple((jax.ShapeDtypeStruct(*out) for ou...  15 us
    ppermute x2, starting transfers between devices, swap_z(): return lax.ppermute(value, 'fsdp', [(f, f ^ 4) for f in range(N_FSDP)])  11.3 us
    ppermute x9, starting transfers between devices, shift_y(): lax.ppermute(value, 'fsdp', [(f, f & 4 | f + step & 3) for f in range(N_F...  10.2 us
    ppermute x9, waiting for transfers between devices, swap_rep(): return lax.ppermute(value, 'rep', [(r, r ^ mask) for r in range(N_REP)])  7.3 us
    ppermute x9, waiting for transfers between devices, shift_y(): lax.ppermute(value, 'fsdp', [(f, f & 4 | f + step & 3) for f in range(N_F...  6.29 us
  transfers between devices with their start and end apart: 20, of which 6 were waited for; matrix products, arithmetic and copies ran while one was open for 1% of the time, Pallas kernels for 20%

profile of v5, /device:TPU:1, one launch (start us, length us, event | category | flops | bytes accessed | tf_op | source)
XLA Modules:
  0.0 66.9 jit_solution(14289956956910828540)
XLA Ops:
  0.7 2.2 %collective-permute-start = (bf16[64,2048]{1,0:T(8,128)(2,1)}, bf16[64,2048]{1,0:T(8,128)(2,1)S(1)}, u32[]{:S(2)}, u32[]{:S(2)}) collective-permute-start(bf16[64,2048]{1,0:T(8,128)(2,1)} %own.1), channel_id=1, source_target_pairs={{0,1},{1,2},{2,3},{3,0},{4,5},{5,6},{6,7},{7,4},{8,9},{9,10},{10,1... | collective-permute-start | bytes 786440 | tf_op jit(solution)/shard_map/ppermute | solution.py:41
  2.9 1.5 %collective-permute-start.1 = (bf16[64,2048]{1,0:T(8,128)(2,1)}, bf16[64,2048]{1,0:T(8,128)(2,1)S(1)}, u32[]{:S(2)}, u32[]{:S(2)}) collective-permute-start(bf16[64,2048]{1,0:T(8,128)(2,1)} %own.1), channel_id=1, source_target_pairs={{0,3},{1,0},{2,1},{3,2},{4,7},{5,4},{6,5},{7,6},{8,11},{9,8},{10,9... | collective-permute-start | bytes 786440 | tf_op jit(solution)/shard_map/ppermute | solution.py:41
  4.4 4.6 %project.1 = (bf16[128,2048]{1,0:T(8,128)(2,1)S(1)}, bf16[128,2048]{1,0:T(8,128)(2,1)S(1)}, bf16[128,2048]{1,0:T(8,128)(2,1)S(1)}, bf16[128,2048]{1,0:T(8,128)(2,1)S(1)}, bf16[512,1024]{1,0:T(8,128)(2,1)}) custom-call(s32[1]{0:T(128)} %bitcast.1.fsdp_ref, bf16[512,1024]{1,0:T(8,128)(2,1)} %tokens_hbm.1, bf16[1,1024,2048]{2,1,0:T(8,128)(2,1)} %weight.3), custom_call_target="tpu_custom_call" | custom-call | tf_op jit(solution)/shard_map/project/pallas_call | solution.py:47
  9.1 0.9 %quantize.1 = (f32[4,4,32,256]{3,2,1,0:T(8,128)S(1)}, bf16[4,4,32,256]{3,2,1,0:T(8,128)(2,1)S(1)}, f32[32,256]{1,0:T(8,128)S(1)}) custom-call(s32[1]{0:T(128)} %bitcast.rep_ref, f32[1,32,8192]{2,1,0:T(8,128)S(1)} %copy-done.1, f32[32,8192]{1,0:T(8,128)S(1)} %copy-done.2), custom_call_target="tpu_custom_call" | custom-call | tf_op jit(solution)/shard_map/quantize/pallas_call | solution.py:47
  10.0 2.9 %collective-permute-start.2 = (bf16[4,4,32,256]{3,2,1,0:T(8,128)(2,1)S(1)}, bf16[4,4,32,256]{3,2,1,0:T(8,128)(2,1)S(1)}, u32[]{:S(2)}, u32[]{:S(2)}) collective-permute-start(bf16[4,4,32,256]{3,2,1,0:T(8,128)(2,1)S(1)} %get-tuple-element.53), channel_id=1, source_target_pairs={{0,8},{8,0},{16,24},{24,16},{32,40},{40,32},{48,56},{56,48},{64,72... | collective-permute-start | bytes 786440 | tf_op jit(solution)/shard_map/ppermute | solution.py:33
  13.0 2.7 %collective-permute-start.5 = (bf16[96,2048]{1,0:T(8,128)(2,1)S(1)}, bf16[96,2048]{1,0:T(8,128)(2,1)S(1)}, u32[]{:S(2)}, u32[]{:S(2)}) collective-permute-start(bf16[96,2048]{1,0:T(8,128)(2,1)S(1)} %get-tuple-element.59), channel_id=1, source_target_pairs={{0,3},{1,0},{2,1},{3,2},{4,7},{5,4},{6,5},{7,6},{8,11},{9,8},{10,9... | collective-permute-start | bytes 1179656 | tf_op jit(solution)/shard_map/ppermute | solution.py:41
  15.8 0.1 collective-permute-start.3
  15.9 6.4 %collective-permute-start.6 = (bf16[64,2048]{1,0:T(8,128)(2,1)S(1)}, bf16[64,2048]{1,0:T(8,128)(2,1)S(1)}, u32[]{:S(2)}, u32[]{:S(2)}) collective-permute-start(bf16[64,2048]{1,0:T(8,128)(2,1)S(1)} %copy-done.3), channel_id=1, source_target_pairs={{0,4},{1,5},{2,6},{3,7},{4,0},{5,1},{6,2},{7,3},{8,12},{9,13},{10,... | collective-permute-start | bytes 786440 | tf_op jit(solution)/shard_map/ppermute | solution.py:37
  22.2 2.7 %collective-permute-done.4.from_below.far_below = bf16[96,2048]{1,0:T(8,128)(2,1)S(1)} collective-permute-done((bf16[96,2048]{1,0:T(8,128)(2,1)S(1)}, bf16[96,2048]{1,0:T(8,128)(2,1)S(1)}, u32[]{:S(2)}, u32[]{:S(2)}) %collective-permute-start.4) | collective-permute-done | bytes 393248 | tf_op jit(solution)/shard_map/ppermute | solution.py:41
  25.0 0.1 add.6
  25.2 2.7 %collective-permute-start.11 = (bf16[128,2048]{1,0:T(8,128)(2,1)S(1)}, bf16[128,2048]{1,0:T(8,128)(2,1)S(1)}, u32[]{:S(2)}, u32[]{:S(2)}) collective-permute-start(bf16[128,2048]{1,0:T(8,128)(2,1)S(1)} %get-tuple-element.74), channel_id=1, source_target_pairs={{0,3},{1,0},{2,1},{3,2},{4,7},{5,4},{6,5},{7,6},{8,11},{9,8},{10,9... | collective-permute-start | bytes 1572872 | tf_op jit(solution)/shard_map/ppermute | solution.py:41
  27.9 0.2 collective-permute-start.7
  28.1 2.3 %near_gradients.1 = (f32[512,1024]{1,0:T(8,128)}, bf16[1024,512]{1,0:T(8,128)(2,1)S(1)}) custom-call(s32[1]{0:T(128)} %bitcast.1.fsdp_ref, bf16[512,1024]{1,0:T(8,128)(2,1)S(1)} %copy-done.4, bf16[1,1024,2048]{2,1,0:T(8,128)(2,1)S(1)} %copy-done, bf16[64,2048]{1,0:T(8,128)(2,1)S(1)} %copy-done.3, bf16[64,2048]{1,0:T(8,128)(2,1)S(1)} %collective-permute-done.1.above, ...), custom_call_target="tpu_custom_call" | custom-call | tf_op jit(solution)/shard_map/near_gradients/pallas_call | solution.py:47
  30.4 2.2 %collective-permute-done.7.got = bf16[4,32,256]{2,1,0:T(8,128)(2,1)S(1)} collective-permute-done((bf16[4,32,256]{2,1,0:T(8,128)(2,1)S(1)}, bf16[4,32,256]{2,1,0:T(8,128)(2,1)S(1)}, u32[]{:S(2)}, u32[]{:S(2)}) %collective-permute-start.7) | collective-permute-done | bytes 65568 | tf_op jit(solution)/shard_map/ppermute | solution.py:33
  32.6 1.1 %collective-permute-start.8 = (bf16[5,32,256]{2,1,0:T(8,128)(2,1)S(1)}, bf16[5,32,256]{2,1,0:T(8,128)(2,1)S(1)}, u32[]{:S(2)}, u32[]{:S(2)}) collective-permute-start(bf16[5,32,256]{2,1,0:T(8,128)(2,1)S(1)} %get-tuple-element.69), channel_id=1, source_target_pairs={{0,64},{8,72},{16,80},{24,88},{32,96},{40,104},{48,112},{56,120},{... | collective-permute-start | bytes 245768 | tf_op jit(solution)/shard_map/ppermute | solution.py:33
  33.7 2.6 %collective-permute-done.8.got.near = bf16[5,32,256]{2,1,0:T(8,128)(2,1)S(1)} collective-permute-done((bf16[5,32,256]{2,1,0:T(8,128)(2,1)S(1)}, bf16[5,32,256]{2,1,0:T(8,128)(2,1)S(1)}, u32[]{:S(2)}, u32[]{:S(2)}) %collective-permute-start.8) | collective-permute-done | bytes 81952 | tf_op jit(solution)/shard_map/ppermute | solution.py:33
  36.4 4.9 %collective-permute-start.9 = (bf16[6,32,256]{2,1,0:T(8,128)(2,1)S(1)}, bf16[6,32,256]{2,1,0:T(8,128)(2,1)S(1)}, u32[]{:S(2)}, u32[]{:S(2)}) collective-permute-start(bf16[6,32,256]{2,1,0:T(8,128)(2,1)S(1)} %get-tuple-element.72), channel_id=1, source_target_pairs={{0,128},{8,136},{16,144},{24,152},{32,160},{40,168},{48,176},{56,1... | collective-permute-start | bytes 294920 | tf_op jit(solution)/shard_map/ppermute | solution.py:33
  41.2 0.7 %collective-permute-start.12 = (bf16[64,2048]{1,0:T(8,128)(2,1)S(1)}, bf16[64,2048]{1,0:T(8,128)(2,1)S(1)}, u32[]{:S(2)}, u32[]{:S(2)}) collective-permute-start(bf16[64,2048]{1,0:T(8,128)(2,1)S(1)} %collective-permute-done.6.z_own), channel_id=1, source_target_pairs={{0,3},{1,0},{2,1},{3,2},{4,7},{5,4},{6,5},{7,6},{8,11},{9,8},{10,9... | collective-permute-start | bytes 786440 | tf_op jit(solution)/shard_map/ppermute | solution.py:41
  42.0 0.2 collective-permute-start.13
  42.2 2.1 %collective-permute-done.9.far = bf16[6,32,256]{2,1,0:T(8,128)(2,1)S(1)} collective-permute-done((bf16[6,32,256]{2,1,0:T(8,128)(2,1)S(1)}, bf16[6,32,256]{2,1,0:T(8,128)(2,1)S(1)}, u32[]{:S(2)}, u32[]{:S(2)}) %collective-permute-start.9) | collective-permute-done | bytes 98336 | tf_op jit(solution)/shard_map/ppermute | solution.py:33
  44.3 0.2 fold.1
  44.5 4.9 %collective-permute-start.19 = (bf16[64,2048]{1,0:T(8,128)(2,1)S(1)}, bf16[64,2048]{1,0:T(8,128)(2,1)S(1)}, u32[]{:S(2)}, u32[]{:S(2)}) collective-permute-start(bf16[64,2048]{1,0:T(8,128)(2,1)S(1)} %get-tuple-element.75), channel_id=1, source_target_pairs={{0,4},{1,5},{2,6},{3,7},{4,0},{5,1},{6,2},{7,3},{8,12},{9,13},{10,... | collective-permute-start | bytes 786440 | tf_op jit(solution)/shard_map/ppermute | solution.py:37
  49.4 0.7 update_step.1
  50.1 1.9 %collective-permute-start.15 = (bf16[4,32,256]{2,1,0:T(8,128)(2,1)S(1)}, bf16[4,32,256]{2,1,0:T(8,128)(2,1)S(1)}, u32[]{:S(2)}, u32[]{:S(2)}) collective-permute-start(bf16[4,32,256]{2,1,0:T(8,128)(2,1)S(1)} %get-tuple-element.82.first), channel_id=1, source_target_pairs={{0,48},{8,56},{16,32},{24,40},{32,16},{40,24},{48,0},{56,8},{64,11... | collective-permute-start | bytes 196616 | tf_op jit(solution)/shard_map/ppermute | solution.py:33
  52.0 3.6 %collective-permute-done.14.z_below = bf16[64,2048]{1,0:T(8,128)(2,1)S(1)} collective-permute-done((bf16[64,2048]{1,0:T(8,128)(2,1)S(1)}, bf16[64,2048]{1,0:T(8,128)(2,1)S(1)}, u32[]{:S(2)}, u32[]{:S(2)}) %collective-permute-start.14) | collective-permute-done | bytes 262176 | tf_op jit(solution)/shard_map/ppermute | solution.py:41
  55.6 0.4 collective-permute-start.16
  56.0 4.7 %gradients.1 = (bf16[1,1024,2048]{2,1,0:T(8,128)(2,1)}, f32[512,1024]{1,0:T(8,128)}) custom-call(s32[1]{0:T(128)} %bitcast.1.fsdp_ref, bf16[1024,512]{1,0:T(8,128)(2,1)S(1)} %get-tuple-element.66.turned, bf16[1,1024,2048]{2,1,0:T(8,128)(2,1)S(1)} %copy-done, f32[512,1024]{1,0:T(8,128)} %get-tuple-element.83._, ...), custom_call_target="tpu_custom_call", output_to_operand_aliasing={{1}: (3, {})} | custom-call | tf_op jit(solution)/shard_map/gradients/pallas_call | solution.py:47
  60.6 3.4 %collective-permute-start.17 = (bf16[2,4,32,256]{3,2,1,0:T(8,128)(2,1)S(1)}, bf16[2,4,32,256]{3,2,1,0:T(8,128)(2,1)S(1)}, u32[]{:S(2)}, u32[]{:S(2)}) collective-permute-start(bf16[2,4,32,256]{3,2,1,0:T(8,128)(2,1)S(1)} %join.1.own_near), channel_id=1, source_target_pairs={{0,8},{8,0},{16,24},{24,16},{32,40},{40,32},{48,56},{56,48},{64,72... | collective-permute-start | bytes 393224 | tf_op jit(solution)/shard_map/ppermute | solution.py:33
  64.0 0.2 collective-permute-start.18
  64.2 0.8 %convert_add_fusion = f32[64,2048]{1,0:T(8,128)} fusion(f32[64,2048]{1,0:T(8,128)S(1)} %get-tuple-element.88, bf16[64,2048]{1,0:T(8,128)(2,1)S(1)} %collective-permute-done.19), kind=kLoop, calls=%fused_computation | loop fusion | flops 262144 | bytes 1310720 | tf_op jit(solution)/shard_map/add | solution.py:432
  65.1 0.3 collective-permute-done.18.other_far
  65.4 1.3 %mix.1 = f32[1,32,8192]{2,1,0:T(8,128)} custom-call(s32[1]{0:T(128)} %bitcast.rep_ref, f32[1,32,8192]{2,1,0:T(8,128)S(1)} %copy-done.1, f32[32,8192]{1,0:T(8,128)S(1)} %copy-done.2, bf16[2,4,32,256]{3,2,1,0:T(8,128)(2,1)S(1)} %join.1.own_near, bf16[2,4,32,256]{3,2,1,0:T(8,128)(2,1)S(1)} %collective-permute-done.16.own_far, ...), custom_call_target="tpu_custom_call" | custom-call | tf_op jit(solution)/shard_map/mix/pallas_call | solution.py:47
  (35 shorter events, 0.4 us)
Async XLA Ops:
  0.6 8.4 %copy-start.1 = (f32[1,32,8192]{2,1,0:T(8,128)S(1)}, f32[1,32,8192]{2,1,0:T(8,128)}, u32[]{:S(2)}) copy-start(f32[1,32,8192]{2,1,0:T(8,128)} %local_hbm.3) | copy-start | bytes 3145732
  0.6 8.4 %copy-start.2 = (f32[32,8192]{1,0:T(8,128)S(1)}, f32[32,8192]{1,0:T(8,128)}, u32[]{:S(2)}) copy-start(f32[32,8192]{1,0:T(8,128)} %global_hbm.3) | copy-start | bytes 3145732
  0.7 12.2 %collective-permute-start = (bf16[64,2048]{1,0:T(8,128)(2,1)}, bf16[64,2048]{1,0:T(8,128)(2,1)S(1)}, u32[]{:S(2)}, u32[]{:S(2)}) collective-permute-start(bf16[64,2048]{1,0:T(8,128)(2,1)} %own.1), channel_id=1, source_target_pairs={{0,1},{1,2},{2,3},{3,0},{4,5},{5,6},{6,7},{7,4},{8,9},{9,10},{10,1... | collective-permute-start | bytes 786440 | tf_op jit(solution)/shard_map/ppermute | solution.py:41
  2.9 10.0 %collective-permute-start.1 = (bf16[64,2048]{1,0:T(8,128)(2,1)}, bf16[64,2048]{1,0:T(8,128)(2,1)S(1)}, u32[]{:S(2)}, u32[]{:S(2)}) collective-permute-start(bf16[64,2048]{1,0:T(8,128)(2,1)} %own.1), channel_id=1, source_target_pairs={{0,3},{1,0},{2,1},{3,2},{4,7},{5,4},{6,5},{7,6},{8,11},{9,8},{10,9... | collective-permute-start | bytes 786440 | tf_op jit(solution)/shard_map/ppermute | solution.py:41
  4.4 11.5 %copy-start.3 = (bf16[64,2048]{1,0:T(8,128)(2,1)S(1)}, bf16[64,2048]{1,0:T(8,128)(2,1)}, u32[]{:S(2)}) copy-start(bf16[64,2048]{1,0:T(8,128)(2,1)} %own.1) | copy-start | bytes 786436
  9.0 19.0 %copy-start = (bf16[1,1024,2048]{2,1,0:T(8,128)(2,1)S(1)}, bf16[1,1024,2048]{2,1,0:T(8,128)(2,1)}, u32[]{:S(2)}) copy-start(bf16[1,1024,2048]{2,1,0:T(8,128)(2,1)} %weight.3) | copy-start | bytes 12582916
  9.0 19.0 %copy-start.4 = (bf16[512,1024]{1,0:T(8,128)(2,1)S(1)}, bf16[512,1024]{1,0:T(8,128)(2,1)}, u32[]{:S(2)}) copy-start(bf16[512,1024]{1,0:T(8,128)(2,1)} %get-tuple-element.63.tokens) | copy-start | bytes 3145732
  10.0 5.7 %collective-permute-start.2 = (bf16[4,4,32,256]{3,2,1,0:T(8,128)(2,1)S(1)}, bf16[4,4,32,256]{3,2,1,0:T(8,128)(2,1)S(1)}, u32[]{:S(2)}, u32[]{:S(2)}) collective-permute-start(bf16[4,4,32,256]{3,2,1,0:T(8,128)(2,1)S(1)} %get-tuple-element.53), channel_id=1, source_target_pairs={{0,8},{8,0},{16,24},{24,16},{32,40},{40,32},{48,56},{56,48},{64,72... | collective-permute-start | bytes 786440 | tf_op jit(solution)/shard_map/ppermute | solution.py:33
  13.0 12.0 %collective-permute-start.4 = (bf16[96,2048]{1,0:T(8,128)(2,1)S(1)}, bf16[96,2048]{1,0:T(8,128)(2,1)S(1)}, u32[]{:S(2)}, u32[]{:S(2)}) collective-permute-start(bf16[96,2048]{1,0:T(8,128)(2,1)S(1)} %get-tuple-element.51), channel_id=1, source_target_pairs={{0,1},{1,2},{2,3},{3,0},{4,5},{5,6},{6,7},{7,4},{8,9},{9,10},{10,1... | collective-permute-start | bytes 1179656 | tf_op jit(solution)/shard_map/ppermute | solution.py:41
  13.0 11.9 %collective-permute-start.5 = (bf16[96,2048]{1,0:T(8,128)(2,1)S(1)}, bf16[96,2048]{1,0:T(8,128)(2,1)S(1)}, u32[]{:S(2)}, u32[]{:S(2)}) collective-permute-start(bf16[96,2048]{1,0:T(8,128)(2,1)S(1)} %get-tuple-element.59), channel_id=1, source_target_pairs={{0,3},{1,0},{2,1},{3,2},{4,7},{5,4},{6,5},{7,6},{8,11},{9,8},{10,9... | collective-permute-start | bytes 1179656 | tf_op jit(solution)/shard_map/ppermute | solution.py:41
  15.8 6.5 %collective-permute-start.3 = (bf16[2,4,32,256]{3,2,1,0:T(8,128)(2,1)S(1)}, bf16[2,4,32,256]{3,2,1,0:T(8,128)(2,1)S(1)}, u32[]{:S(2)}, u32[]{:S(2)}) collective-permute-start(bf16[2,4,32,256]{3,2,1,0:T(8,128)(2,1)S(1)} %get-tuple-element.56), channel_id=1, source_target_pairs={{0,16},{8,24},{16,0},{24,8},{32,48},{40,56},{48,32},{56,40},{64,80... | collective-permute-start | bytes 393224 | tf_op jit(solution)/shard_map/ppermute | solution.py:33
  15.9 12.2 %collective-permute-start.6 = (bf16[64,2048]{1,0:T(8,128)(2,1)S(1)}, bf16[64,2048]{1,0:T(8,128)(2,1)S(1)}, u32[]{:S(2)}, u32[]{:S(2)}) collective-permute-start(bf16[64,2048]{1,0:T(8,128)(2,1)S(1)} %copy-done.3), channel_id=1, source_target_pairs={{0,4},{1,5},{2,6},{3,7},{4,0},{5,1},{6,2},{7,3},{8,12},{9,13},{10,... | collective-permute-start | bytes 786440 | tf_op jit(solution)/shard_map/ppermute | solution.py:37
  25.0 7.6 %copy-start.5 = (f32[32,256]{1,0:T(8,128)S(1)}, f32[32,256]{1,0:T(8,128)}, u32[]{:S(2)}) copy-start(f32[32,256]{1,0:T(8,128)} %momentum.5) | copy-start | bytes 98308
  25.1 19.2 %collective-permute-start.10 = (bf16[128,2048]{1,0:T(8,128)(2,1)S(1)}, bf16[128,2048]{1,0:T(8,128)(2,1)S(1)}, u32[]{:S(2)}, u32[]{:S(2)}) collective-permute-start(bf16[128,2048]{1,0:T(8,128)(2,1)S(1)} %get-tuple-element.60), channel_id=1, source_target_pairs={{0,1},{1,2},{2,3},{3,0},{4,5},{5,6},{6,7},{7,4},{8,9},{9,10},{10,1... | collective-permute-start | bytes 1572872 | tf_op jit(solution)/shard_map/ppermute | solution.py:41
  25.2 19.1 %collective-permute-start.11 = (bf16[128,2048]{1,0:T(8,128)(2,1)S(1)}, bf16[128,2048]{1,0:T(8,128)(2,1)S(1)}, u32[]{:S(2)}, u32[]{:S(2)}) collective-permute-start(bf16[128,2048]{1,0:T(8,128)(2,1)S(1)} %get-tuple-element.74), channel_id=1, source_target_pairs={{0,3},{1,0},{2,1},{3,2},{4,7},{5,4},{6,5},{7,6},{8,11},{9,8},{10,9... | collective-permute-start | bytes 1572872 | tf_op jit(solution)/shard_map/ppermute | solution.py:41
  27.9 4.7 %collective-permute-start.7 = (bf16[4,32,256]{2,1,0:T(8,128)(2,1)S(1)}, bf16[4,32,256]{2,1,0:T(8,128)(2,1)S(1)}, u32[]{:S(2)}, u32[]{:S(2)}) collective-permute-start(bf16[4,32,256]{2,1,0:T(8,128)(2,1)S(1)} %get-tuple-element.64), channel_id=1, source_target_pairs={{0,48},{8,56},{16,32},{24,40},{32,16},{40,24},{48,0},{56,8},{64,11... | collective-permute-start | bytes 196616 | tf_op jit(solution)/shard_map/ppermute | solution.py:33
  32.6 3.7 %collective-permute-start.8 = (bf16[5,32,256]{2,1,0:T(8,128)(2,1)S(1)}, bf16[5,32,256]{2,1,0:T(8,128)(2,1)S(1)}, u32[]{:S(2)}, u32[]{:S(2)}) collective-permute-start(bf16[5,32,256]{2,1,0:T(8,128)(2,1)S(1)} %get-tuple-element.69), channel_id=1, source_target_pairs={{0,64},{8,72},{16,80},{24,88},{32,96},{40,104},{48,112},{56,120},{... | collective-permute-start | bytes 245768 | tf_op jit(solution)/shard_map/ppermute | solution.py:33
  36.4 7.9 %collective-permute-start.9 = (bf16[6,32,256]{2,1,0:T(8,128)(2,1)S(1)}, bf16[6,32,256]{2,1,0:T(8,128)(2,1)S(1)}, u32[]{:S(2)}, u32[]{:S(2)}) collective-permute-start(bf16[6,32,256]{2,1,0:T(8,128)(2,1)S(1)} %get-tuple-element.72), channel_id=1, source_target_pairs={{0,128},{8,136},{16,144},{24,152},{32,160},{40,168},{48,176},{56,1... | collective-permute-start | bytes 294920 | tf_op jit(solution)/shard_map/ppermute | solution.py:33
  41.2 10.8 %collective-permute-start.12 = (bf16[64,2048]{1,0:T(8,128)(2,1)S(1)}, bf16[64,2048]{1,0:T(8,128)(2,1)S(1)}, u32[]{:S(2)}, u32[]{:S(2)}) collective-permute-start(bf16[64,2048]{1,0:T(8,128)(2,1)S(1)} %collective-permute-done.6.z_own), channel_id=1, source_target_pairs={{0,3},{1,0},{2,1},{3,2},{4,7},{5,4},{6,5},{7,6},{8,11},{9,8},{10,9... | collective-permute-start | bytes 786440 | tf_op jit(solution)/shard_map/ppermute | solution.py:41
  42.0 10.0 %collective-permute-start.13 = (bf16[64,2048]{1,0:T(8,128)(2,1)S(1)}, bf16[64,2048]{1,0:T(8,128)(2,1)S(1)}, u32[]{:S(2)}, u32[]{:S(2)}) collective-permute-start(bf16[64,2048]{1,0:T(8,128)(2,1)S(1)} %collective-permute-done.6.z_own), channel_id=1, source_target_pairs={{0,2},{1,3},{2,0},{3,1},{4,6},{5,7},{6,4},{7,5},{8,10},{9,11},{10,... | collective-permute-start | bytes 786440 | tf_op jit(solution)/shard_map/ppermute | solution.py:41
  44.3 11.3 %collective-permute-start.14 = (bf16[64,2048]{1,0:T(8,128)(2,1)S(1)}, bf16[64,2048]{1,0:T(8,128)(2,1)S(1)}, u32[]{:S(2)}, u32[]{:S(2)}) collective-permute-start(bf16[64,2048]{1,0:T(8,128)(2,1)S(1)} %collective-permute-done.6.z_own), channel_id=1, source_target_pairs={{0,1},{1,2},{2,3},{3,0},{4,5},{5,6},{6,7},{7,4},{8,9},{9,10},{10,1... | collective-permute-start | bytes 786440 | tf_op jit(solution)/shard_map/ppermute | solution.py:41
  44.5 19.8 %collective-permute-start.19 = (bf16[64,2048]{1,0:T(8,128)(2,1)S(1)}, bf16[64,2048]{1,0:T(8,128)(2,1)S(1)}, u32[]{:S(2)}, u32[]{:S(2)}) collective-permute-start(bf16[64,2048]{1,0:T(8,128)(2,1)S(1)} %get-tuple-element.75), channel_id=1, source_target_pairs={{0,4},{1,5},{2,6},{3,7},{4,0},{5,1},{6,2},{7,3},{8,12},{9,13},{10,... | collective-permute-start | bytes 786440 | tf_op jit(solution)/shard_map/ppermute | solution.py:37
  50.1 5.5 %collective-permute-start.15 = (bf16[4,32,256]{2,1,0:T(8,128)(2,1)S(1)}, bf16[4,32,256]{2,1,0:T(8,128)(2,1)S(1)}, u32[]{:S(2)}, u32[]{:S(2)}) collective-permute-start(bf16[4,32,256]{2,1,0:T(8,128)(2,1)S(1)} %get-tuple-element.82.first), channel_id=1, source_target_pairs={{0,48},{8,56},{16,32},{24,40},{32,16},{40,24},{48,0},{56,8},{64,11... | collective-permute-start | bytes 196616 | tf_op jit(solution)/shard_map/ppermute | solution.py:33
  55.6 8.5 %collective-permute-start.16 = (bf16[2,4,32,256]{3,2,1,0:T(8,128)(2,1)S(1)}, bf16[2,4,32,256]{3,2,1,0:T(8,128)(2,1)S(1)}, u32[]{:S(2)}, u32[]{:S(2)}) collective-permute-start(bf16[2,4,32,256]{3,2,1,0:T(8,128)(2,1)S(1)} %join.1.own_near), channel_id=1, source_target_pairs={{0,16},{8,24},{16,0},{24,8},{32,48},{40,56},{48,32},{56,40},{64,80... | collective-permute-start | bytes 393224 | tf_op jit(solution)/shard_map/ppermute | solution.py:33
  60.6 4.5 %collective-permute-start.17 = (bf16[2,4,32,256]{3,2,1,0:T(8,128)(2,1)S(1)}, bf16[2,4,32,256]{3,2,1,0:T(8,128)(2,1)S(1)}, u32[]{:S(2)}, u32[]{:S(2)}) collective-permute-start(bf16[2,4,32,256]{3,2,1,0:T(8,128)(2,1)S(1)} %join.1.own_near), channel_id=1, source_target_pairs={{0,8},{8,0},{16,24},{24,16},{32,40},{40,32},{48,56},{56,48},{64,72... | collective-permute-start | bytes 393224 | tf_op jit(solution)/shard_map/ppermute | solution.py:33
  64.0 1.3 %collective-permute-start.18 = (bf16[2,4,32,256]{3,2,1,0:T(8,128)(2,1)S(1)}, bf16[2,4,32,256]{3,2,1,0:T(8,128)(2,1)S(1)}, u32[]{:S(2)}, u32[]{:S(2)}) collective-permute-start(bf16[2,4,32,256]{3,2,1,0:T(8,128)(2,1)S(1)} %collective-permute-done.16.own_far), channel_id=1, source_target_pairs={{0,8},{8,0},{16,24},{24,16},{32,40},{40,32},{48,56},{56,48},{64,72... | collective-permute-start | bytes 393224 | tf_op jit(solution)/shard_map/ppermute | solution.py:33
